TPU v7x, 32 devices: a whole 2x2x4 slice. The times are simulated.
32 devices in a mesh: dp: 4 (over y, x), expert: 8 (over z, core).
Axes of the slice: x: 2, y: 2, z: 4, core: 2. Of those that a mesh axis runs over, the one named last changes fastest.
Arguments:
- tokens: bfloat16 [4096, 3584], P(('dp', 'expert')), may hold values from -6 to 6
- out_grad: bfloat16 [4096, 3584], P(('dp', 'expert')), may hold values from -1.5 to 1.5
- route: int32 [4096, 8], P(('dp', 'expert')), may hold values from 0 to 255, all different within a row; in each aligned block of 128 rows (0 to 127, 128 to 255, ...) at most 8 rows name the same one
- gate_fixed: int32 [4096, 8], P(('dp', 'expert')), may hold values from 16 to 256
- w_gate: bfloat16 [8, 3584, 256], P('expert'), may hold values from -0.09375 to 0.09375
- w_up: bfloat16 [8, 3584, 256], P('expert'), may hold values from -0.09375 to 0.09375
- w_down: bfloat16 [8, 256, 3584], P('expert'), may hold values from -0.125 to 0.125
- router_bias: float32 [256], replicated, may hold values from -1 to 1
- loads: int32 [32, 256], P(('dp', 'expert')), may hold values from 0 to 189
Outputs:
- token_grad: bfloat16 [4096, 3584], P(('dp', 'expert'))
- gate_grad: float32 [4096, 8], P(('dp', 'expert'))
- grad_gate: bfloat16 [8, 3584, 256], P('expert', 'dp')
- grad_up: bfloat16 [8, 3584, 256], P('expert', 'dp')
- grad_down: bfloat16 [8, 256, 3584], P('expert', None, 'dp')
- new_bias: float32 [256], replicated
Inputs may be any that keep to these rules, and one draw needn't show every extreme that they name: `route`: each row names 8 different experts. In the rows of one device no expert is named more than 8 times, a bound that some block reaches.
All inputs are finite; a program needn't handle non-finite values.
Results may differ from a plain program's by a relative error of at most 0.02.
Values may be sent and summed in bfloat16 or wider, within the bound.
No kernel may reach another device: no remote copies, remote signals or barrier semaphores. Data moves between devices by JAX's collectives and lax.ppermute only.
A program may use at most 128 MiB of HBM per device.

v0:
```python
import jax
import jax.numpy as jnp
from jax import lax
from jax.sharding import PartitionSpec as P

EXPERTS_ALL = 256
SPLIT = 8
CAP = 8


bias_step = 0.125


def contract(left, right, left_dim, right_dim):
    return lax.dot_general(
        left, right, (((left_dim,), (right_dim,)), ((), ())), preferred_element_type=jnp.float32
    )


def per_device(tokens, out_grad, route, gate_fixed, w_gate, w_up, w_down, router_bias, loads):
    row_count = tokens.shape[0]
    width = tokens.shape[1]
    top_count = route.shape[1]
    total = row_count * top_count
    devices_wide = lax.axis_size("expert")
    flights = devices_wide // SPLIT
    flat_route = route.reshape(-1)
    in_window = flat_route < flights
    expert_hot = (flat_route[:, None] == jnp.arange(flights, dtype=jnp.int32)[None, :]).astype(
        jnp.int32
    )
    earlier = jnp.cumsum(expert_hot, axis=0) - expert_hot
    slot_of = jnp.sum(earlier * expert_hot, axis=1)
    target = jnp.where(in_window, flat_route * CAP + slot_of, flights * CAP)
    slot_table = (
        jnp.full((flights * CAP,), total, jnp.int32)
        .at[target]
        .set(jnp.arange(total, dtype=jnp.int32), mode="drop")
    )
    is_valid = slot_table < total
    safe_index = jnp.minimum(slot_table, total - 1)
    token_of = safe_index // top_count
    send_in = jnp.where(is_valid[:, None], tokens[token_of], jnp.zeros((), tokens.dtype)).reshape(
        flights, CAP, width
    )
    send_grad = jnp.where(
        is_valid[:, None], out_grad[token_of], jnp.zeros((), out_grad.dtype)
    ).reshape(flights, CAP, width)
    gate_values = gate_fixed.reshape(-1)[safe_index].astype(jnp.float32) / 256.0
    send_gate = jnp.where(is_valid, gate_values, 0.0).astype(jnp.bfloat16).reshape(flights, CAP)

    def duplicate(values):
        spread = jnp.broadcast_to(values[:, None], (flights, SPLIT) + values.shape[1:])
        return spread.reshape((devices_wide,) + values.shape[1:])

    got_in, got_grad, got_gate = (
        lax.all_to_all(duplicate(send_in), "expert", split_axis=0, concat_axis=0, tiled=True),
        lax.all_to_all(duplicate(send_grad), "expert", split_axis=0, concat_axis=0, tiled=True),
        lax.all_to_all(duplicate(send_gate), "expert", split_axis=0, concat_axis=0, tiled=True),
    )
    rows_in = got_in.reshape(devices_wide * CAP, width)
    rows_grad = got_grad.reshape(devices_wide * CAP, width)
    row_gate = got_gate.reshape(devices_wide * CAP, 1).astype(jnp.float32)
    gate_slice = w_gate[0]
    up_slice = w_up[0]
    down_slice = w_down[0]
    pre_gate = jnp.dot(rows_in, gate_slice, preferred_element_type=jnp.float32)
    pre_up = jnp.dot(rows_in, up_slice, preferred_element_type=jnp.float32)
    sigmoid_gate = jax.nn.sigmoid(pre_gate)
    activated = pre_gate * sigmoid_gate
    hidden = activated * pre_up
    back_proj = contract(rows_grad, down_slice, 1, 1)
    part_gate = jnp.sum(back_proj * hidden, axis=1).astype(jnp.bfloat16)
    grad_hidden = row_gate * back_proj
    grad_pregate = (
        grad_hidden * pre_up * sigmoid_gate * (1.0 + pre_gate * (1.0 - sigmoid_gate))
    ).astype(jnp.bfloat16)
    grad_preup = (grad_hidden * activated).astype(jnp.bfloat16)
    scaled_hidden = (row_gate * hidden).astype(jnp.bfloat16)
    part_dx = (
        contract(grad_pregate, gate_slice, 1, 1) + contract(grad_preup, up_slice, 1, 1)
    ).astype(jnp.bfloat16)
    sum_gate = contract(rows_in, grad_pregate, 0, 0)
    sum_up = contract(rows_in, grad_preup, 0, 0)
    sum_down = contract(scaled_hidden, rows_grad, 0, 0)
    back_dx, back_gate = (
        lax.all_to_all(
            part_dx.reshape(devices_wide, CAP, width),
            "expert",
            split_axis=0,
            concat_axis=0,
            tiled=True,
        ),
        lax.all_to_all(
            part_gate.reshape(devices_wide, CAP), "expert", split_axis=0, concat_axis=0, tiled=True
        ),
    )
    summed_dx = jnp.sum(
        back_dx.reshape(flights, SPLIT, CAP, width).astype(jnp.float32), axis=1
    ).reshape(flights * CAP, width)
    summed_gate = jnp.sum(
        back_gate.reshape(flights, SPLIT, CAP).astype(jnp.float32), axis=1
    ).reshape(-1)
    token_index = jnp.where(is_valid, token_of, row_count)
    token_grad = jax.ops.segment_sum(summed_dx, token_index, num_segments=row_count).astype(
        jnp.bfloat16
    )
    gate_grad = jax.ops.segment_sum(summed_gate, slot_table, num_segments=total).reshape(
        row_count, top_count
    )
    share_gate, share_up, share_down = (
        lax.psum_scatter(
            sum_gate.astype(jnp.bfloat16), "dp", scatter_dimension=0, tiled=True
        ).astype(jnp.float32),
        lax.psum_scatter(sum_up.astype(jnp.bfloat16), "dp", scatter_dimension=0, tiled=True).astype(
            jnp.float32
        ),
        lax.psum_scatter(
            sum_down.astype(jnp.bfloat16), "dp", scatter_dimension=1, tiled=True
        ).astype(jnp.float32),
    )
    grad_gate = share_gate.astype(jnp.bfloat16)
    grad_up = share_up.astype(jnp.bfloat16)
    grad_down = share_down.astype(jnp.bfloat16)
    load = lax.psum(loads[0].astype(jnp.float32), ("dp", "expert"))
    overall = jnp.sum(load)
    new_bias = router_bias + bias_step * jnp.sign(overall - EXPERTS_ALL * load)
    return (token_grad, gate_grad, grad_gate[None], grad_up[None], grad_down[None], new_bias)


def solution(mesh):
    in_specs = (
        P(("dp", "expert"), None),
        P(("dp", "expert"), None),
        P(("dp", "expert"), None),
        P(("dp", "expert"), None),
        P("expert", None, None),
        P("expert", None, None),
        P("expert", None, None),
        P(),
        P(("dp", "expert"), None),
    )
    out_specs = (
        P(("dp", "expert"), None),
        P(("dp", "expert"), None),
        P("expert", "dp", None),
        P("expert", "dp", None),
        P("expert", None, "dp"),
        P(),
    )
    return jax.shard_map(
        per_device, mesh=mesh, in_specs=in_specs, out_specs=out_specs, check_vma=False
    )
```

profile of v0, /device:TPU:0, one launch (start us, length us, event | category | flops | bytes accessed | tf_op | source)
XLA Modules:
  0.0 181.4 jit_solution(9757721266918194529)
XLA Ops:
  7.2 0.8 broadcast_multiply_fusion
  8.0 0.7 fusion.27
  10.4 4.3 %scatter_custom_fusion = s32[8]{0:T(128)S(1)} fusion(s32[1024]{0:T(1024)S(1)} %bitcast.56, s32[1024]{0:T(1024)S(1)} %iota.3, s32[]{:T(128)} %constant.16.clone.1), kind=kCustom, calls=%fused_computation.62 | custom fusion | bytes 36 | tf_op jit(solution)/shard_map/scatter | solution.py:38
  14.7 0.8 copy.25
  15.6 0.6 gather_fusion
  16.8 6.3 %all-to-all-start = ((bf16[8,1,8]{2,1,0:T(2,128)(2,1)}), bf16[8,1,8]{2,1,0:T(2,128)(2,1)S(1)}, u32[]{:S(2)}, u32[]{:S(2)}) async-start(bf16[8,1,8]{2,1,0:T(2,128)(2,1)} %reshape.267), calls=%async_computation | async-start | bytes 8192 | tf_op jit(solution)/shard_map/all_to_all | solution.py:59
  23.2 1.9 %gather_fusion.2 = bf16[8,3584]{1,0:T(8,128)(2,1)S(1)} fusion(bf16[128,3584]{1,0:T(8,128)(2,1)} %param.9, s32[1024]{0:T(1024)S(1)} %pad_clamp_fusion), kind=kCustom, calls=%fused_computation.2 | custom fusion | bytes 114720 | tf_op jit(solution)/shard_map/gather | solution.py:43
  25.8 2.8 %all-to-all-done = bf16[8,1,8]{2,1,0:T(2,128)(2,1)S(1)} async-done(((bf16[8,1,8]{2,1,0:T(2,128)(2,1)}), bf16[8,1,8]{2,1,0:T(2,128)(2,1)S(1)}, u32[]{:S(2)}, u32[]{:S(2)}) %all-to-all-start) | async-done | bytes 160 | tf_op jit(solution)/shard_map/all_to_all | solution.py:59
  28.7 16.4 %all_to_all.27 = bf16[8,8,3584]{2,1,0:T(8,128)(2,1)S(1)} all-to-all(bf16[8,8,3584]{2,1,0:T(8,128)(2,1)S(1)} %reshape.270), channel_id=1, replica_groups=mesh['dp'=4,'expert'=8] {'expert'}, dimensions={0} | all-to-all | bytes 917504 | tf_op jit(solution)/shard_map/all_to_all | solution.py:57
  45.0 0.8 reshape.268
  45.8 3.5 %all-to-all-start.1 = ((bf16[8,8,3584]{2,1,0:T(8,128)(2,1)}), bf16[8,8,3584]{2,1,0:T(8,128)(2,1)S(1)}, u32[]{:S(2)}, u32[]{:S(2)}) async-start(bf16[8,8,3584]{2,1,0:T(8,128)(2,1)} %reshape.268), calls=%async_computation.1 | async-start | bytes 917504 | tf_op jit(solution)/shard_map/all_to_all | solution.py:58
  49.9 1.1 copy-done.1
  51.4 11.8 %all-to-all-done.1 = bf16[8,8,3584]{2,1,0:T(8,128)(2,1)S(1)} async-done(((bf16[8,8,3584]{2,1,0:T(8,128)(2,1)}), bf16[8,8,3584]{2,1,0:T(8,128)(2,1)S(1)}, u32[]{:S(2)}, u32[]{:S(2)}) %all-to-all-start.1) | async-done | bytes 458784 | tf_op jit(solution)/shard_map/all_to_all | solution.py:58
  63.2 2.0 %convolution_convert_fusion = bf16[256,3584]{1,0:T(8,128)(2,1)} fusion(bf16[8,8,3584]{2,1,0:T(8,128)(2,1)S(1)} %all-to-all-done.1, f32[64]{0:T(128)S(1)} %reshape.275, f32[64,256]{1,0:T(8,128)S(1)} %fusion.7, f32[64,256]{1,0:T(8,128)S(1)} %fusion.4), kind=kOutput, calls=%fused_computation.6 | convolution fusion | flops 118472704 | bytes 2425088 | tf_op jit(solution)/shard_map/dot_general | solution.py:15
  65.2 3.8 %copy.28 = bf16[256,3584]{0,1:T(8,128)(2,1)} copy(bf16[256,3584]{1,0:T(8,128)(2,1)} %convolution_convert_fusion) | data formatting | bytes 3670016
  69.1 2.3 %multiply_reduce_fusion = (bf16[64]{0:T(256)(128)(2,1)S(1)}, bf16[64,256]{1,0:T(8,128)(2,1)S(1)}, bf16[64,256]{1,0:T(8,128)(2,1)S(1)}) fusion(f32[64,256]{1,0:T(8,128)S(1)} %fusion.7, f32[64,256]{1,0:T(8,128)S(1)} %fusion.4, f32[64]{0:T(128)S(1)} %reshape.275, bf16[1,256,3584]{2,1,0:T(8,128)(2,1)} %param.15, bf16[8,8,3584]{2,1,0:T(8,128)(2,1)S(1)} %all-to-all-done.1), kind=kOutput, calls=%fused_computation.31 | convolution fusion | flops 117718976 | bytes 2490752 | tf_op jit(solution)/shard_map/dot_general | solution.py:15
  71.3 1.9 %convolution_convert_fusion.1 = bf16[3584,256]{1,0:T(8,128)(2,1)} fusion(bf16[64,256]{1,0:T(8,128)(2,1)S(1)} %get-tuple-element.24, bf16[8,8,3584]{2,1,0:T(8,128)(2,1)S(1)} %all_to_all.27), kind=kOutput, calls=%fused_computation.7 | convolution fusion | flops 118358016 | bytes 2326528 | tf_op jit(solution)/shard_map/dot_general | solution.py:15
  73.4 1.9 %convolution_convert_fusion.2 = bf16[3584,256]{1,0:T(8,128)(2,1)} fusion(bf16[64,256]{1,0:T(8,128)(2,1)S(1)} %get-tuple-element.23, bf16[8,8,3584]{2,1,0:T(8,128)(2,1)S(1)} %all_to_all.27), kind=kOutput, calls=%fused_computation.8 | convolution fusion | flops 118358016 | bytes 2326528 | tf_op jit(solution)/shard_map/dot_general | solution.py:15
  75.3 0.7 convert_element_type.132
  76.0 3.3 %all-to-all-start.4 = ((bf16[8,1,8]{2,1,0:T(2,128)(2,1)}), bf16[8,1,8]{2,1,0:T(2,128)(2,1)S(1)}, u32[]{:S(2)}, u32[]{:S(2)}) async-start(bf16[8,1,8]{2,1,0:T(2,128)(2,1)} %convert_element_type.132), calls=%async_computation.4 | async-start | bytes 8192 | tf_op jit(solution)/shard_map/all_to_all | solution.py:94
  79.3 0.7 fusion.2
  80.0 0.8 copy-done.2
  80.8 1.4 fusion.1
  82.3 2.4 %all-to-all-done.4 = bf16[8,1,8]{2,1,0:T(2,128)(2,1)S(1)} async-done(((bf16[8,1,8]{2,1,0:T(2,128)(2,1)}), bf16[8,1,8]{2,1,0:T(2,128)(2,1)S(1)}, u32[]{:S(2)}, u32[]{:S(2)}) %all-to-all-start.4) | async-done | bytes 160 | tf_op jit(solution)/shard_map/all_to_all | solution.py:94
  84.7 3.5 %all-to-all-start.3 = ((bf16[8,8,3584]{2,1,0:T(8,128)(2,1)}), bf16[8,8,3584]{2,1,0:T(8,128)(2,1)S(1)}, u32[]{:S(2)}, u32[]{:S(2)}) async-start(bf16[8,8,3584]{2,1,0:T(8,128)(2,1)} %fusion.1), calls=%async_computation.3 | async-start | bytes 917504 | tf_op jit(solution)/shard_map/all_to_all | solution.py:87
  88.2 40.8 %psum.7 = f32[256]{0:T(256)S(1)} all-reduce(f32[256]{0:T(256)S(1)} %bitcast.55), channel_id=1, replica_groups=mesh['dp'=4,'expert'=8] {'dp','expert'}, use_global_device_ids=true, to_apply=%region_11.12 | all-reduce | flops 256 | bytes 2048 | tf_op jit(solution)/shard_map/psum | solution.py:125
  129.6 1.2 multiply_add_fusion
  131.6 0.7 copy.27
  132.3 2.1 %scatter_custom_fusion.1 = f32[128,3584]{1,0:T(8,128)} fusion(s32[8]{0:T(128)S(1)} %get-tuple-element.27, f32[8,3584]{1,0:T(8,128)S(1)} %convert_reduce_fusion, f32[]{:T(128)} %constant.15.clone.1), kind=kCustom, calls=%fused_computation.22 | custom fusion | flops 28672 | bytes 1835012 | tf_op jit(solution)/shard_map/scatter-add | solution.py:105
  134.4 2.5 %convert_element_type.120 = bf16[128,3584]{1,0:T(8,128)(2,1)} convert(f32[128,3584]{1,0:T(8,128)} %scatter_custom_fusion.1) | non-fusion elementwise | flops 458752 | bytes 2752512 | tf_op jit(solution)/shard_map/convert_element_type | solution.py:105
  136.9 2.0 %copy.29 = bf16[256,896]{1,0:T(8,128)(2,1)} copy(bf16[256,896]{0,1:T(8,128)(2,1)} %bitcast.51) | data formatting | bytes 917504
  138.9 35.9 %reduce-scatter.6.cloned.1.call-done = bf16[896,256]{1,0:T(8,128)(2,1)} async-done(((bf16[3584,256]{1,0:T(8,128)(2,1)}), bf16[896,256]{1,0:T(8,128)(2,1)}) %reduce-scatter.6.cloned.1.call-update) | async-done | bytes 458768 | tf_op jit(solution)/shard_map/reduce_scatter | solution.py:112
  (55 shorter events, 5.6 us)
Async XLA Ops:
  7.2 42.3 %copy-start = (bf16[1,3584,256]{2,1,0:T(8,128)(2,1)S(1)}, bf16[1,3584,256]{2,1,0:T(8,128)(2,1)}, u32[]{:S(2)}) copy-start(bf16[1,3584,256]{2,1,0:T(8,128)(2,1)} %param.13) | copy-start | bytes 5505028
  7.2 18.0 %copy-start.3 = (bf16[128,3584]{1,0:T(8,128)(2,1)S(1)}, bf16[128,3584]{1,0:T(8,128)(2,1)}, u32[]{:S(2)}) copy-start(bf16[128,3584]{1,0:T(8,128)(2,1)} %param.10) | copy-start | bytes 2752516
  16.8 11.8 %all-to-all-start = ((bf16[8,1,8]{2,1,0:T(2,128)(2,1)}), bf16[8,1,8]{2,1,0:T(2,128)(2,1)S(1)}, u32[]{:S(2)}, u32[]{:S(2)}) async-start(bf16[8,1,8]{2,1,0:T(2,128)(2,1)} %reshape.267), calls=%async_computation | async-start | bytes 8192 | tf_op jit(solution)/shard_map/all_to_all | solution.py:59
  45.8 17.4 %all-to-all-start.1 = ((bf16[8,8,3584]{2,1,0:T(8,128)(2,1)}), bf16[8,8,3584]{2,1,0:T(8,128)(2,1)S(1)}, u32[]{:S(2)}, u32[]{:S(2)}) async-start(bf16[8,8,3584]{2,1,0:T(8,128)(2,1)} %reshape.268), calls=%async_computation.1 | async-start | bytes 917504 | tf_op jit(solution)/shard_map/all_to_all | solution.py:58
  49.3 87.6 %reduce-scatter.10.cloned.1.call-start = ((), (), s32[]{:S(2)}) async-start(), calls=%async_computation.10 | async-start | bytes 2293760
  49.5 1.5 copy-start.1
  69.0 69.9 %reduce-scatter.8.cloned.1.call-start = ((), (), s32[]{:S(2)}) async-start(), calls=%async_computation.9 | async-start | bytes 2293760 | tf_op jit(solution)/shard_map/reduce_scatter | solution.py:115
  73.3 101.6 %reduce-scatter.6.cloned.1.call-start = ((), (), s32[]{:S(2)}) async-start(), calls=%async_computation.8 | async-start | bytes 2293760 | tf_op jit(solution)/shard_map/reduce_scatter | solution.py:112
  76.0 8.7 %all-to-all-start.4 = ((bf16[8,1,8]{2,1,0:T(2,128)(2,1)}), bf16[8,1,8]{2,1,0:T(2,128)(2,1)S(1)}, u32[]{:S(2)}, u32[]{:S(2)}) async-start(bf16[8,1,8]{2,1,0:T(2,128)(2,1)} %convert_element_type.132), calls=%async_computation.4 | async-start | bytes 8192 | tf_op jit(solution)/shard_map/all_to_all | solution.py:94
  79.3 1.5 copy-start.2
  80.8 7.4 %copy-start.5 = (s32[1,256]{1,0:T(1,128)S(1)}, s32[1,256]{1,0:T(1,128)}, u32[]{:S(2)}) copy-start(s32[1,256]{1,0:T(1,128)} %param.17) | copy-start | bytes 3076
  80.8 48.8 %copy-start.4 = (f32[256]{0:T(256)S(1)}, f32[256]{0:T(256)}, u32[]{:S(2)}) copy-start(f32[256]{0:T(256)} %param.16) | copy-start | bytes 3076
  84.7 47.6 %all-to-all-start.3 = ((bf16[8,8,3584]{2,1,0:T(8,128)(2,1)}), bf16[8,8,3584]{2,1,0:T(8,128)(2,1)S(1)}, u32[]{:S(2)}, u32[]{:S(2)}) async-start(bf16[8,8,3584]{2,1,0:T(8,128)(2,1)} %fusion.1), calls=%async_computation.3 | async-start | bytes 917504 | tf_op jit(solution)/shard_map/all_to_all | solution.py:87
Sparse Core Ops, SparseCore 0:
  69.1 32.4 reduce-scatter.9
  105.2 32.9 reduce-scatter.7
  141.8 32.9 reduce-scatter.5
where the time goes:
time: 182 us; the launch traced here: 181 us
  blocking collectives  57.2 us (31%)
  waiting for transfers between devices  53 us (29%)
  local copies, waits for them, and re-layouts  20.1 us (11%)
  starting transfers between devices  16.7 us (9%)
  between operations  13.9 us (8%)
  matrix products  11.1 us (6%)
  other arithmetic  9.3 us (5%)
    psum x1, blocking collectives, per_device(): load = lax.psum(loads[0].astype(jnp.float32), ('dp', 'expert'))  40.8 us
    reduce_scatter x1, waiting for transfers between devices, per_device(): lax.psum_scatter(sum_gate.astype(jnp.bfloat16), 'dp', scatter_dimension=0...  35.9 us
    all_to_all x1, blocking collectives, per_device(): lax.all_to_all(duplicate(send_in), 'expert', split_axis=0, concat_axis=0,...  16.4 us
    all_to_all x1, waiting for transfers between devices, per_device(): lax.all_to_all(duplicate(send_grad), 'expert', split_axis=0, concat_axis=...  11.8 us
    dot_general x6, matrix products, contract(): lax.dot_general(left, right, (((left_dim,), (right_dim,)), ((), ())), pre...  10.2 us
    unnamed x16, local copies, waits for them, and re-layouts  9.2 us
    all_to_all x1, starting transfers between devices, per_device(): lax.all_to_all(duplicate(send_gate), 'expert', split_axis=0, concat_axis=...  6.33 us
    scatter x1, local copies, waits for them, and re-layouts, per_device(): slot_table = jnp.full((flights * CAP,), total, jnp.int32).at[target].set(...  4.3 us
  transfers between devices with their start and end apart: 7, of which 4 were waited for; matrix products, arithmetic and copies ran while one was open for 12% of the time, Pallas kernels for 0%

commit v1 on v0

v1 whole, which is shorter than its diff:
```python
import functools

import jax
import jax.numpy as jnp
from jax import lax
from jax.experimental import pallas as pl
from jax.experimental.pallas import tpu as pltpu
from jax.sharding import PartitionSpec as P

EXPERTS_ALL = 256
SPLIT = 8
CAP = 8
BLOCK = 2 * CAP
LANES = 128
bias_step = 0.125

F32 = jnp.float32
BF16 = jnp.bfloat16


def dot(left, right, left_dim, right_dim):
    return lax.dot_general(
        left, right, (((left_dim,), (right_dim,)), ((), ())), preferred_element_type=F32
    )


def call(kernel, outs, args, flops, scratch=()):
    size = sum(a.size * a.dtype.itemsize for a in (*args, *outs))
    return pl.pallas_call(
        kernel,
        out_shape=outs,
        in_specs=[pl.BlockSpec(memory_space=pltpu.VMEM)] * len(args),
        out_specs=[pl.BlockSpec(memory_space=pltpu.VMEM)] * len(outs),
        scratch_shapes=list(scratch),
        compiler_params=pltpu.CompilerParams(vmem_limit_bytes=48 * 1024 * 1024),
        cost_estimate=pl.CostEstimate(flops=flops, bytes_accessed=size, transcendentals=0),
    )(*args)


def select_kernel(flights, tok_ref, grad_ref, route_ref, fixed_ref, loads_ref, pay_ref, sel_ref):
    rows, width = tok_ref.shape
    route, fixed = route_ref[...], fixed_ref[...].astype(F32)
    before = lax.broadcasted_iota(jnp.int32, (rows, rows), 0) < lax.broadcasted_iota(
        jnp.int32, (rows, rows), 1
    )
    before = jnp.where(before, 1.0, 0.0).astype(BF16)
    place = lax.broadcasted_iota(jnp.int32, (CAP, rows), 0).astype(F32)
    picks, gates = [], []
    for flight in range(flights):
        hot = route == flight
        mask = jnp.sum(jnp.where(hot, 1.0, 0.0), axis=0, keepdims=True)
        weight = jnp.sum(jnp.where(hot, fixed, 0.0), axis=0, keepdims=True) * (1.0 / 256.0)
        mask = jnp.broadcast_to(mask, (CAP, rows))
        slot = dot(mask.astype(BF16), before, 1, 0)
        pick = jnp.where(slot == place, mask, 0.0)
        picks.append(pick)
        gates.append(jnp.sum(pick * weight, axis=1, keepdims=True))
    pick = jnp.concatenate(picks, axis=0)
    sel_ref[...] = pick
    rows_in = dot(pick.astype(BF16), tok_ref[...], 1, 0)
    rows_grad = dot(pick.astype(BF16), grad_ref[...], 1, 0)
    loads = loads_ref[...]
    high = loads // LANES
    low = (loads - high * LANES).astype(F32)
    high = high.astype(F32)
    line = lax.broadcasted_iota(jnp.int32, (CAP, LANES), 0)
    lane = lax.broadcasted_iota(jnp.int32, (CAP, LANES), 1)
    counts = jnp.zeros((CAP, LANES), F32)
    for at, part in enumerate((low[:, :LANES], low[:, LANES:], high[:, :LANES], high[:, LANES:])):
        counts = jnp.where(line == at, part, counts)
    for flight in range(flights):
        own = slice(flight * CAP, (flight + 1) * CAP)
        pay_ref[flight, :, :width] = jnp.concatenate([rows_in[own], rows_grad[own]], axis=0).astype(
            BF16
        )
        gate = jnp.where(lane == 0, gates[flight], 0.0)
        pay_ref[flight, :, width:] = jnp.concatenate([gate, counts], axis=0).astype(BF16)


def expert_kernel(blocks, groups, copies, shift, *refs):
    pay_refs, refs = refs[:-(len(groups) + copies + 4)], refs[-(len(groups) + copies + 4):]
    gate_ref, up_ref, down_ref = refs[:3]
    back_refs, share_refs, rows_ref = refs[3 : 3 + len(groups)], refs[3 + len(groups) : -1], refs[-1]
    width = gate_ref.shape[0]
    units = gate_ref.shape[1]
    quarter = width // copies
    half = width // 2
    pays = []
    for ref in pay_refs:
        pay = ref[...].reshape(-1, ref.shape[-1])
        pays.append(pay)
    at = 0
    for pay in pays:
        rows_ref[at : at + pay.shape[0], :] = pay[:, :width]
        at += pay.shape[0]
    extra = jnp.concatenate([pay[:, width:] for pay in pays], axis=0).astype(F32)
    extra = extra.reshape(blocks, BLOCK, LANES)
    row_gate = extra[:, :CAP, :1].reshape(blocks * CAP, 1)
    rows = rows_ref[...]

    def part(values, which):
        return values.reshape(blocks, BLOCK, values.shape[-1])[
            :, which * CAP : (which + 1) * CAP
        ].reshape(blocks * CAP, values.shape[-1])

    pre_gate = part(dot(rows, gate_ref[...], 1, 0), 0)
    pre_up = part(dot(rows, up_ref[...], 1, 0), 0)
    back_proj = part(dot(rows, down_ref[...], 1, 1), 1)
    sigmoid_gate = jax.nn.sigmoid(pre_gate)
    activated = pre_gate * sigmoid_gate
    hidden = activated * pre_up
    part_gate = jnp.sum(back_proj * hidden, axis=1, keepdims=True)
    grad_hidden = row_gate * back_proj
    grad_pregate = grad_hidden * pre_up * sigmoid_gate * (1.0 + pre_gate * (1.0 - sigmoid_gate))
    grad_preup = grad_hidden * activated
    scaled_hidden = row_gate * hidden

    def blocked(values):
        return values.reshape(blocks, CAP, values.shape[-1])

    sums = jnp.sum(extra[:, CAP : CAP + 4], axis=0)
    total = sums[0:2] + sums[2:4] * LANES
    top = jnp.floor(total * (1.0 / LANES**2))
    rest = total - top * LANES**2
    middle = jnp.floor(rest * (1.0 / LANES))
    low = rest - middle * LANES
    line = lax.broadcasted_iota(jnp.int32, (CAP, LANES), 0)
    digits = []
    for lanes in range(2):
        digit = jnp.zeros((CAP, LANES), F32)
        for place, value in enumerate((low, middle, top)):
            digit = jnp.where(line == place, value[lanes : lanes + 1], digit)
        digits.append(digit)
    digits = jnp.concatenate(digits, axis=1)[None]
    if blocks > 1:
        digits = jnp.concatenate([digits, jnp.zeros((blocks - 1, CAP, units), F32)], axis=0)
    left = jnp.concatenate([blocked(grad_pregate), blocked(scaled_hidden)], axis=1)
    right = jnp.concatenate([blocked(grad_preup), digits], axis=1)
    left = left.reshape(blocks * BLOCK, units).astype(BF16)
    right = right.reshape(blocks * BLOCK, units).astype(BF16)
    me = lax.axis_index("dp")
    for step in range(copies):
        to = shift(me, step)
        start = pl.multiple_of(to * quarter, LANES)
        share_refs[step][:, :quarter] = rows_ref[:, pl.ds(start, quarter)]
        share_refs[step][:, quarter : quarter + units] = left
        share_refs[step][:, quarter + units :] = right

    part_dx = dot(grad_pregate.astype(BF16), gate_ref[...], 1, 1) + dot(
        grad_preup.astype(BF16), up_ref[...], 1, 1
    )
    part_dx = blocked(part_dx)
    dx = jnp.concatenate([part_dx[:, :, :half], part_dx[:, :, half:]], axis=1).astype(BF16)
    lane = lax.broadcasted_iota(jnp.int32, (blocks, CAP, LANES), 2)
    tail = jnp.where(lane == 0, blocked(part_gate), 0.0)
    tail = jnp.concatenate([tail, jnp.zeros_like(tail)], axis=1).astype(BF16)
    for ref, members in zip(back_refs, groups):
        for at, block in enumerate(members):
            ref[at, :, :half] = dx[block]
            ref[at, :, half:] = tail[block]


def pair_kernel(mine_ref, other_ref, *out_refs):
    total = mine_ref[...].astype(F32) + other_ref[...].astype(F32)
    for at, ref in enumerate(out_refs):
        ref[...] = total[at].astype(ref.dtype)


def token_kernel(flights, sel_ref, route_ref, *refs):
    part_refs, (token_ref, gate_ref) = refs[:-2], refs[-2:]
    half = token_ref.shape[1] // 2
    total = 0.0
    for ref in part_refs:
        total = total + jnp.sum(ref[...].astype(F32), axis=1)
    total = total.reshape(flights, BLOCK, half + LANES)
    rows = jnp.concatenate([total[:, :CAP, :half], total[:, CAP:, :half]], axis=2)
    rows = rows.reshape(flights * CAP, 2 * half)
    pick = sel_ref[...]
    if flights == 1:
        token_ref[...] = dot(pick.astype(BF16), rows.astype(BF16), 0, 0).astype(BF16)
    else:
        token_ref[...] = lax.dot_general(
            pick,
            rows,
            (((0,), (0,)), ((), ())),
            precision=lax.Precision.HIGHEST,
            preferred_element_type=F32,
        ).astype(BF16)
    gates = jnp.zeros(gate_ref.shape, F32)
    for flight in range(flights):
        value = jnp.sum(
            pick[flight * CAP : (flight + 1) * CAP] * total[flight, :CAP, half : half + 1],
            axis=0,
            keepdims=True,
        )
        gates = jnp.where(route_ref[...] == flight, value, gates)
    gate_ref[...] = gates


def weight_kernel(units, bias_ref, *refs):
    share_refs, (gate_ref, up_ref, down_ref, new_ref) = refs[:-4], refs[-4:]
    quarter = share_refs[0].shape[1] - 2 * units
    rows = jnp.concatenate([ref[:, :quarter] for ref in share_refs], axis=0)
    grads = jnp.concatenate([ref[:, quarter:] for ref in share_refs], axis=0).astype(F32)
    line = lax.broadcasted_iota(jnp.int32, grads.shape, 0)
    is_token = line % BLOCK < CAP
    hidden = jnp.where(is_token, grads, 0.0).astype(BF16)
    scaled = jnp.where(is_token, 0.0, grads)[:, :units].astype(BF16)
    both = dot(rows, hidden, 0, 0)
    gate_ref[0] = both[:, :units].astype(BF16)
    up_ref[0] = both[:, units:].astype(BF16)
    down_ref[0] = dot(scaled, rows, 0, 0).astype(BF16)
    load = jnp.zeros((1, units), F32)
    for ref in share_refs:
        digit = ref[:BLOCK, quarter + units :].astype(F32)[CAP : CAP + 3]
        load = load + digit[0:1] + digit[1:2] * LANES + digit[2:3] * LANES**2
    diff = jnp.sum(load, axis=1, keepdims=True) - EXPERTS_ALL * load
    sign = jnp.where(diff > 0.0, 1.0, jnp.where(diff < 0.0, -1.0, 0.0))
    new_ref[...] = bias_ref[...] + bias_step * sign


def per_device(tokens, out_grad, route, gate_fixed, w_gate, w_up, w_down, router_bias, loads):
    row_count, width = tokens.shape
    top_count = route.shape[1]
    units = w_gate.shape[2]
    sources = lax.axis_size("expert")
    copies = lax.axis_size("dp")
    flights = sources // SPLIT
    half, quarter = width // 2, width // copies
    struct = jax.ShapeDtypeStruct

    payload, pick = call(
        functools.partial(select_kernel, flights),
        [struct((flights, BLOCK, width + LANES), BF16), struct((flights * CAP, row_count), F32)],
        [tokens, out_grad, route.T, gate_fixed.T, loads],
        4 * flights * CAP * row_count * width,
    )

    def swap(values, step):
        return lax.ppermute(values, "expert", [(i, i ^ step) for i in range(sources)])

    if flights == 1:
        near = {step: swap(payload, step) for step in range(2, SPLIT, 2)}
        near[0] = payload
        got = [near[k] if k % 2 == 0 else swap(near[k - 1], 1) for k in range(SPLIT)]
        groups = [list(range(0, SPLIT, 2)), list(range(1, SPLIT, 2))]
    else:
        spread = jnp.broadcast_to(payload[:, None], (flights, SPLIT) + payload.shape[1:])
        spread = spread.reshape((sources,) + payload.shape[1:])
        got = [lax.all_to_all(spread, "expert", split_axis=0, concat_axis=0, tiled=True)]
        groups = [list(range(sources))]

    if copies & (copies - 1) == 0:
        shift = lambda index, step: index ^ step
    else:
        shift = lambda index, step: lax.rem(index + step, copies)
    rows = sources * BLOCK
    outs = call(
        functools.partial(expert_kernel, sources, groups, copies, shift),
        [struct((len(group), BLOCK, half + LANES), BF16) for group in groups]
        + [struct((rows, quarter + 2 * units), BF16)] * copies,
        got + [w_gate[0], w_up[0], w_down[0]],
        8 * rows * width * units,
        [pltpu.VMEM((rows, width), BF16)],
    )
    back, shares = outs[: len(groups)], outs[len(groups) :]

    if flights == 1:
        other = swap(back[1], 1)
        block = (BLOCK, half + LANES)
        sums = call(
            pair_kernel,
            [struct(block, F32)] + [struct(block, BF16)] * 3,
            [back[0], other],
            0,
        )
        parts = [sums[0]] + [swap(sums[at], 2 * at) for at in range(1, 4)]
        parts = [part.reshape((1, 1) + block) for part in parts]
    else:
        parts = lax.all_to_all(back[0], "expert", split_axis=0, concat_axis=0, tiled=True)
        parts = [parts.reshape(flights, SPLIT, BLOCK, half + LANES)]
    sent = [shares[0]]
    for step in range(1, copies):
        pairs = [(i, int(shift(i, step)) if copies & (copies - 1) == 0 else (i + step) % copies) for i in range(copies)]
        sent.append(lax.ppermute(shares[step], "dp", pairs))

    grad_gate, grad_up, grad_down, new_bias = call(
        functools.partial(weight_kernel, units),
        [
            struct((1, quarter, units), BF16),
            struct((1, quarter, units), BF16),
            struct((1, units, quarter), BF16),
            struct((1, EXPERTS_ALL), F32),
        ],
        [router_bias[None]] + sent,
        6 * rows * copies * quarter * units,
    )
    token_grad, gate_grad = call(
        functools.partial(token_kernel, flights),
        [struct((row_count, width), BF16), struct((top_count, row_count), F32)],
        [pick, route.T] + parts,
        2 * flights * CAP * row_count * width,
    )
    return (token_grad, gate_grad.T, grad_gate, grad_up, grad_down, new_bias[0])


def solution(mesh):
    in_specs = (
        P(("dp", "expert"), None),
        P(("dp", "expert"), None),
        P(("dp", "expert"), None),
        P(("dp", "expert"), None),
        P("expert", None, None),
        P("expert", None, None),
        P("expert", None, None),
        P(),
        P(("dp", "expert"), None),
    )
    out_specs = (
        P(("dp", "expert"), None),
        P(("dp", "expert"), None),
        P("expert", "dp", None),
        P("expert", "dp", None),
        P("expert", None, "dp"),
        P(),
    )
    return jax.shard_map(
        per_device, mesh=mesh, in_specs=in_specs, out_specs=out_specs, check_vma=False
    )
```

time: 182 us -> 49.5 us (0.27)
  blocking collectives: 57.2 us -> 0 us
  waiting for transfers between devices: 53 us -> 19.3 us
  local copies, waits for them, and re-layouts: 20.1 us -> 4.54 us
  between operations: 13.9 us -> 0.69 us
  matrix products: 11.1 us -> 0 us
  other arithmetic: 9.3 us -> 0 us
  Pallas kernels: 0 us -> 8.99 us
    psum x1 -> x0, blocking collectives: 40.8 us -> none  [per_device(): load = lax.psum(loads[0].astype(jnp.float32), ('dp', 'expert'))]
    reduce_scatter x2 -> x0, waiting for transfers between devices: 35.9 us -> none  [the longest x1 35.9 us: per_device(): lax.psum_scatter(sum_gate.astype(jnp.bfloat16), 'dp', scatter_dimension=0...]
    ppermute x0 -> x14, waiting for transfers between devices: none -> 19.3 us  [the longest x11 15.2 us: swap(): lax.ppermute(values, 'expert', [(i, i ^ step) for i in range(sources)])]
    all_to_all x4 -> x0, waiting for transfers between devices: 17 us -> none  [the longest x1 11.8 us: per_device(): lax.all_to_all(duplicate(send_grad), 'expert', split_axis=0, concat_axis=...]
    all_to_all x4 -> x0, starting transfers between devices: 16.6 us -> none  [the longest x1 6.33 us: per_device(): lax.all_to_all(duplicate(send_gate), 'expert', split_axis=0, concat_axis=...]
    all_to_all x1 -> x0, blocking collectives: 16.4 us -> none  [per_device(): lax.all_to_all(duplicate(send_in), 'expert', split_axis=0, concat_axis=0,...]
    ppermute x0 -> x14, starting transfers between devices: none -> 15.7 us  [the longest x11 12.2 us: swap(): lax.ppermute(values, 'expert', [(i, i ^ step) for i in range(sources)])]
    dot_general x8 -> x0, matrix products: 11.1 us -> none  [the longest x6 10.2 us: contract(): lax.dot_general(left, right, (((left_dim,), (right_dim,)), ((), ())), pre...]
  transfers between devices with their start and end apart: 7 -> 14, of which waited for: 4 -> 7; matrix products, arithmetic and copies ran while one was open for 12% -> 0% of each run, Pallas kernels for 0% -> 3%
where the time goes in v1:
time: 49.5 us; the launch traced here: 49.3 us
  waiting for transfers between devices  19.3 us (39%)
  starting transfers between devices  15.7 us (32%)
  Pallas kernels  8.99 us (18%)
  local copies, waits for them, and re-layouts  4.54 us (9%)
  between operations  0.69 us (1%)
    ppermute x11, waiting for transfers between devices, swap(): lax.ppermute(values, 'expert', [(i, i ^ step) for i in range(sources)])  15.2 us
    ppermute x11, starting transfers between devices, swap(): lax.ppermute(values, 'expert', [(i, i ^ step) for i in range(sources)])  12.2 us
    pallas_call x5, Pallas kernels, call(): pl.pallas_call(kernel, out_shape=outs, in_specs=[pl.BlockSpec(memory_spac...  8.99 us
    unnamed x14, local copies, waits for them, and re-layouts  4.54 us
    ppermute x3, waiting for transfers between devices, per_device(): sent.append(lax.ppermute(shares[step], 'dp', pairs))  4.18 us
    ppermute x3, starting transfers between devices, per_device(): sent.append(lax.ppermute(shares[step], 'dp', pairs))  3.49 us
  transfers between devices with their start and end apart: 14, of which 7 were waited for; matrix products, arithmetic and copies ran while one was open for 0% of the time, Pallas kernels for 3%

profile of v1, /device:TPU:0, one launch (start us, length us, event | category | flops | bytes accessed | tf_op | source)
XLA Modules:
  0.0 49.3 jit_solution(8703536964971546259)
XLA Ops:
  0.7 1.3 %copy-done.1 = bf16[128,3584]{1,0:T(8,128)(2,1)S(1)} copy-done((bf16[128,3584]{1,0:T(8,128)(2,1)S(1)}, bf16[128,3584]{1,0:T(8,128)(2,1)}, u32[]{:S(2)}) %copy-start.1) | copy-done | bytes 917528
  2.0 1.2 %copy-done.2 = bf16[128,3584]{1,0:T(8,128)(2,1)S(1)} copy-done((bf16[128,3584]{1,0:T(8,128)(2,1)S(1)}, bf16[128,3584]{1,0:T(8,128)(2,1)}, u32[]{:S(2)}) %copy-start.2) | copy-done | bytes 917528
  3.1 0.7 %copy-done.3 = s32[128,8]{0,1:T(8,128)S(1)} copy-done((s32[128,8]{0,1:T(8,128)S(1)}, s32[128,8]{0,1:T(8,128)}, u32[]{:S(2)}) %copy-start.3) | copy-done | bytes 4120
  3.8 0.7 %copy-done.4 = s32[128,8]{0,1:T(8,128)S(1)} copy-done((s32[128,8]{0,1:T(8,128)S(1)}, s32[128,8]{0,1:T(8,128)}, u32[]{:S(2)}) %copy-start.4) | copy-done | bytes 4120
  4.5 0.7 %copy-done.5 = s32[1,256]{1,0:T(1,128)S(1)} copy-done((s32[1,256]{1,0:T(1,128)S(1)}, s32[1,256]{1,0:T(1,128)}, u32[]{:S(2)}) %copy-start.5) | copy-done | bytes 1048
  5.2 0.4 shard_map.136
  5.6 5.1 %collective-permute-start.5 = (bf16[1,16,3712]{2,1,0:T(8,128)(2,1)S(1)}, bf16[1,16,3712]{2,1,0:T(8,128)(2,1)S(1)}, u32[]{:S(2)}, u32[]{:S(2)}) collective-permute-start(bf16[1,16,3712]{2,1,0:T(8,128)(2,1)S(1)} %get-tuple-element.25.refs_0_), channel_id=1, source_target_pairs={{0,6},{1,7},{2,4},{3,5},{4,2},{5,3},{6,0},{7,1},{8,14},{9,15},{10,... | collective-permute-start | bytes 356360 | tf_op jit(solution)/shard_map/ppermute | solution.py:240
  10.7 0.0 collective-permute-start.3
  10.7 0.6 %collective-permute-start.1 = (bf16[1,16,3712]{2,1,0:T(8,128)(2,1)S(1)}, bf16[1,16,3712]{2,1,0:T(8,128)(2,1)S(1)}, u32[]{:S(2)}, u32[]{:S(2)}) collective-permute-start(bf16[1,16,3712]{2,1,0:T(8,128)(2,1)S(1)} %get-tuple-element.25.refs_0_), channel_id=1, source_target_pairs={{0,2},{1,3},{2,0},{3,1},{4,6},{5,7},{6,4},{7,5},{8,10},{9,11},{10,... | collective-permute-start | bytes 356360 | tf_op jit(solution)/shard_map/ppermute | solution.py:240
  11.4 0.0 collective-permute-start
  11.4 3.5 %collective-permute-done.5.refs_6_ = bf16[1,16,3712]{2,1,0:T(8,128)(2,1)S(1)} collective-permute-done((bf16[1,16,3712]{2,1,0:T(8,128)(2,1)S(1)}, bf16[1,16,3712]{2,1,0:T(8,128)(2,1)S(1)}, u32[]{:S(2)}, u32[]{:S(2)}) %collective-permute-start.5) | collective-permute-done | bytes 118816 | tf_op jit(solution)/shard_map/ppermute | solution.py:240
  14.9 5.9 %collective-permute-done.3.refs_4_ = bf16[1,16,3712]{2,1,0:T(8,128)(2,1)S(1)} collective-permute-done((bf16[1,16,3712]{2,1,0:T(8,128)(2,1)S(1)}, bf16[1,16,3712]{2,1,0:T(8,128)(2,1)S(1)}, u32[]{:S(2)}, u32[]{:S(2)}) %collective-permute-start.3) | collective-permute-done | bytes 118816 | tf_op jit(solution)/shard_map/ppermute | solution.py:240
  20.8 0.0 collective-permute-start.4
  20.8 0.5 %collective-permute-start.2 = (bf16[1,16,3712]{2,1,0:T(8,128)(2,1)S(1)}, bf16[1,16,3712]{2,1,0:T(8,128)(2,1)S(1)}, u32[]{:S(2)}, u32[]{:S(2)}) collective-permute-start(bf16[1,16,3712]{2,1,0:T(8,128)(2,1)S(1)} %collective-permute-done.1.refs_2_), channel_id=1, source_target_pairs={{0,1},{1,0},{2,3},{3,2},{4,5},{5,4},{6,7},{7,6},{8,9},{9,8},{10,11... | collective-permute-start | bytes 356360 | tf_op jit(solution)/shard_map/ppermute | solution.py:240
  21.3 0.8 %collective-permute-done.4.refs_5_ = bf16[1,16,3712]{2,1,0:T(8,128)(2,1)S(1)} collective-permute-done((bf16[1,16,3712]{2,1,0:T(8,128)(2,1)S(1)}, bf16[1,16,3712]{2,1,0:T(8,128)(2,1)S(1)}, u32[]{:S(2)}, u32[]{:S(2)}) %collective-permute-start.4) | collective-permute-done | bytes 118816 | tf_op jit(solution)/shard_map/ppermute | solution.py:240
  22.1 0.2 collective-permute-done.2.refs_3_
  22.3 5.3 %shard_map.137 = (bf16[4,16,1920]{2,1,0:T(8,128)(2,1)S(1)}, bf16[4,16,1920]{2,1,0:T(8,128)(2,1)S(1)}, bf16[128,1408]{1,0:T(8,128)(2,1)S(1)}, bf16[128,1408]{1,0:...) custom-call(bf16[1,16,3712]{2,1,0:T(8,128)(2,1)S(1)} %get-tuple-element.25.refs_0_, ...), custom_call_target="tpu_custom_call" | custom-call | flops 939524096 | bytes 8388608 | tf_op jit(solution)/shard_map/pallas_call | solution.py:29
  27.6 0.4 collective-permute-start.7
  28.0 1.5 %collective-permute-start.11 = (bf16[128,1408]{1,0:T(8,128)(2,1)S(1)}, bf16[128,1408]{1,0:T(8,128)(2,1)S(1)}, u32[]{:S(2)}, u32[]{:S(2)}) collective-permute-start(bf16[128,1408]{1,0:T(8,128)(2,1)S(1)} %get-tuple-element.35), channel_id=1, source_target_pairs={{0,8},{8,0},{16,24},{24,16},{1,9},{9,1},{17,25},{25,17},{2,10},{10... | collective-permute-start | bytes 1081352 | tf_op jit(solution)/shard_map/ppermute | solution.py:285
  29.5 1.5 %collective-permute-start.12 = (bf16[128,1408]{1,0:T(8,128)(2,1)S(1)}, bf16[128,1408]{1,0:T(8,128)(2,1)S(1)}, u32[]{:S(2)}, u32[]{:S(2)}) collective-permute-start(bf16[128,1408]{1,0:T(8,128)(2,1)S(1)} %get-tuple-element.36), channel_id=1, source_target_pairs={{0,16},{8,24},{16,0},{24,8},{1,17},{9,25},{17,1},{25,9},{2,18},{10... | collective-permute-start | bytes 1081352 | tf_op jit(solution)/shard_map/ppermute | solution.py:285
  31.0 0.5 collective-permute-start.13
  31.5 0.0 collective-permute-done.7.other_ref
  31.5 0.1 shard_map.138
  31.6 0.1 collective-permute-start.8
  31.7 3.0 %collective-permute-start.9 = (bf16[16,1920]{1,0:T(8,128)(2,1)S(1)}, bf16[16,1920]{1,0:T(8,128)(2,1)S(1)}, u32[]{:S(2)}, u32[]{:S(2)}) collective-permute-start(bf16[16,1920]{1,0:T(8,128)(2,1)S(1)} %get-tuple-element.30), channel_id=1, source_target_pairs={{0,4},{1,5},{2,6},{3,7},{4,0},{5,1},{6,2},{7,3},{8,12},{9,13},{10,... | collective-permute-start | bytes 184328 | tf_op jit(solution)/shard_map/ppermute | solution.py:240
  34.7 1.2 %collective-permute-done.8 = bf16[16,1920]{1,0:T(8,128)(2,1)S(1)} collective-permute-done((bf16[16,1920]{1,0:T(8,128)(2,1)S(1)}, bf16[16,1920]{1,0:T(8,128)(2,1)S(1)}, u32[]{:S(2)}, u32[]{:S(2)}) %collective-permute-start.8) | collective-permute-done | bytes 61472 | tf_op jit(solution)/shard_map/ppermute | solution.py:240
  35.9 2.4 %collective-permute-start.10 = (bf16[16,1920]{1,0:T(8,128)(2,1)S(1)}, bf16[16,1920]{1,0:T(8,128)(2,1)S(1)}, u32[]{:S(2)}, u32[]{:S(2)}) collective-permute-start(bf16[16,1920]{1,0:T(8,128)(2,1)S(1)} %get-tuple-element.31), channel_id=1, source_target_pairs={{0,6},{1,7},{2,4},{3,5},{4,2},{5,3},{6,0},{7,1},{8,14},{9,15},{10,... | collective-permute-start | bytes 184328 | tf_op jit(solution)/shard_map/ppermute | solution.py:240
  38.3 0.0 collective-permute-done.9
  38.3 3.6 %collective-permute-done.10 = bf16[16,1920]{1,0:T(8,128)(2,1)S(1)} collective-permute-done((bf16[16,1920]{1,0:T(8,128)(2,1)S(1)}, bf16[16,1920]{1,0:T(8,128)(2,1)S(1)}, u32[]{:S(2)}, u32[]{:S(2)}) %collective-permute-start.10) | collective-permute-done | bytes 61472 | tf_op jit(solution)/shard_map/ppermute | solution.py:240
  41.9 1.3 %shard_map.139 = (bf16[128,3584]{1,0:T(8,128)(2,1)}, f32[8,128]{1,0:T(8,128)}) custom-call(f32[8,128]{1,0:T(8,128)S(1)} %get-tuple-element.24.sel_ref, s32[8,128]{1,0:T(8,128)S(1)} %bitcast.18, f32[1,1,16,1920]{3,2,1,0:T(8,128)S(1)} %bitcast.13, bf16[1,1,16,1920]{3,2,1,0:T(8,128)(2,1)S(1)} %bitcast.14, bf16[1,1,16,1920]{3,2,1,0:T(8,128)(2,1)S(1)} %bitcast.15, ...), custom_call_target="tpu_custom_call" | custom-call | flops 7340032 | bytes 1236992 | tf_op jit(solution)/shard_map/pallas_call | solution.py:29
  43.3 4.2 %collective-permute-done.12.refs_2_ = bf16[128,1408]{1,0:T(8,128)(2,1)S(1)} collective-permute-done((bf16[128,1408]{1,0:T(8,128)(2,1)S(1)}, bf16[128,1408]{1,0:T(8,128)(2,1)S(1)}, u32[]{:S(2)}, u32[]{:S(2)}) %collective-permute-start.12) | collective-permute-done | bytes 360480 | tf_op jit(solution)/shard_map/ppermute | solution.py:285
  47.5 1.8 %shard_map.140 = (bf16[1,896,256]{2,1,0:T(8,128)(2,1)}, bf16[1,896,256]{2,1,0:T(8,128)(2,1)}, bf16[1,256,896]{2,1,0:T(8,128)(2,1)}, f32[1,256]{1,0:T(1,128)}) custom-call(f32[1,256]{1,0:T(1,128)S(1)} %bitcast.20, bf16[128,1408]{1,0:T(8,128)(2,1)S(1)} %get-tuple-element.34.refs_0_, bf16[128,1408]{1,0:T(8,128)(2,1)S(1)} %collective-permute-done.11.refs_1_, ...), custom_call_target="tpu_custom_call" | custom-call | flops 704643072 | bytes 2820096 | tf_op jit(solution)/shard_map/pallas_call | solution.py:29
  (15 shorter events, 0.0 us)
Async XLA Ops:
  0.6 21.6 %copy-start = (bf16[1,3584,256]{2,1,0:T(8,128)(2,1)S(1)}, bf16[1,3584,256]{2,1,0:T(8,128)(2,1)}, u32[]{:S(2)}) copy-start(bf16[1,3584,256]{2,1,0:T(8,128)(2,1)} %param.13) | copy-start | bytes 5505028
  0.6 1.3 %copy-start.1 = (bf16[128,3584]{1,0:T(8,128)(2,1)S(1)}, bf16[128,3584]{1,0:T(8,128)(2,1)}, u32[]{:S(2)}) copy-start(bf16[128,3584]{1,0:T(8,128)(2,1)} %tok_ref.1) | copy-start | bytes 2752516
  2.0 1.2 %copy-start.2 = (bf16[128,3584]{1,0:T(8,128)(2,1)S(1)}, bf16[128,3584]{1,0:T(8,128)(2,1)}, u32[]{:S(2)}) copy-start(bf16[128,3584]{1,0:T(8,128)(2,1)} %grad_ref.1) | copy-start | bytes 2752516
  3.1 0.7 %copy-start.3 = (s32[128,8]{0,1:T(8,128)S(1)}, s32[128,8]{0,1:T(8,128)}, u32[]{:S(2)}) copy-start(s32[128,8]{0,1:T(8,128)} %param.11) | copy-start | bytes 12292
  3.8 0.7 %copy-start.4 = (s32[128,8]{0,1:T(8,128)S(1)}, s32[128,8]{0,1:T(8,128)}, u32[]{:S(2)}) copy-start(s32[128,8]{0,1:T(8,128)} %param.12) | copy-start | bytes 12292
  4.5 0.7 %copy-start.5 = (s32[1,256]{1,0:T(1,128)S(1)}, s32[1,256]{1,0:T(1,128)}, u32[]{:S(2)}) copy-start(s32[1,256]{1,0:T(1,128)} %loads_ref.1) | copy-start | bytes 3076
  5.6 9.3 %collective-permute-start.5 = (bf16[1,16,3712]{2,1,0:T(8,128)(2,1)S(1)}, bf16[1,16,3712]{2,1,0:T(8,128)(2,1)S(1)}, u32[]{:S(2)}, u32[]{:S(2)}) collective-permute-start(bf16[1,16,3712]{2,1,0:T(8,128)(2,1)S(1)} %get-tuple-element.25.refs_0_), channel_id=1, source_target_pairs={{0,6},{1,7},{2,4},{3,5},{4,2},{5,3},{6,0},{7,1},{8,14},{9,15},{10,... | collective-permute-start | bytes 356360 | tf_op jit(solution)/shard_map/ppermute | solution.py:240
  10.7 10.0 %collective-permute-start.3 = (bf16[1,16,3712]{2,1,0:T(8,128)(2,1)S(1)}, bf16[1,16,3712]{2,1,0:T(8,128)(2,1)S(1)}, u32[]{:S(2)}, u32[]{:S(2)}) collective-permute-start(bf16[1,16,3712]{2,1,0:T(8,128)(2,1)S(1)} %get-tuple-element.25.refs_0_), channel_id=1, source_target_pairs={{0,4},{1,5},{2,6},{3,7},{4,0},{5,1},{6,2},{7,3},{8,12},{9,13},{10,... | collective-permute-start | bytes 356360 | tf_op jit(solution)/shard_map/ppermute | solution.py:240
  10.7 10.0 %collective-permute-start.1 = (bf16[1,16,3712]{2,1,0:T(8,128)(2,1)S(1)}, bf16[1,16,3712]{2,1,0:T(8,128)(2,1)S(1)}, u32[]{:S(2)}, u32[]{:S(2)}) collective-permute-start(bf16[1,16,3712]{2,1,0:T(8,128)(2,1)S(1)} %get-tuple-element.25.refs_0_), channel_id=1, source_target_pairs={{0,2},{1,3},{2,0},{3,1},{4,6},{5,7},{6,4},{7,5},{8,10},{9,11},{10,... | collective-permute-start | bytes 356360 | tf_op jit(solution)/shard_map/ppermute | solution.py:240
  11.4 9.9 %collective-permute-start = (bf16[1,16,3712]{2,1,0:T(8,128)(2,1)S(1)}, bf16[1,16,3712]{2,1,0:T(8,128)(2,1)S(1)}, u32[]{:S(2)}, u32[]{:S(2)}) collective-permute-start(bf16[1,16,3712]{2,1,0:T(8,128)(2,1)S(1)} %get-tuple-element.25.refs_0_), channel_id=1, source_target_pairs={{0,1},{1,0},{2,3},{3,2},{4,5},{5,4},{6,7},{7,6},{8,9},{9,8},{10,11... | collective-permute-start | bytes 356360 | tf_op jit(solution)/shard_map/ppermute | solution.py:240
  14.9 6.4 %collective-permute-start.6 = (bf16[1,16,3712]{2,1,0:T(8,128)(2,1)S(1)}, bf16[1,16,3712]{2,1,0:T(8,128)(2,1)S(1)}, u32[]{:S(2)}, u32[]{:S(2)}) collective-permute-start(bf16[1,16,3712]{2,1,0:T(8,128)(2,1)S(1)} %collective-permute-done.5.refs_6_), channel_id=1, source_target_pairs={{0,1},{1,0},{2,3},{3,2},{4,5},{5,4},{6,7},{7,6},{8,9},{9,8},{10,11... | collective-permute-start | bytes 356360 | tf_op jit(solution)/shard_map/ppermute | solution.py:240
  20.8 1.3 %collective-permute-start.4 = (bf16[1,16,3712]{2,1,0:T(8,128)(2,1)S(1)}, bf16[1,16,3712]{2,1,0:T(8,128)(2,1)S(1)}, u32[]{:S(2)}, u32[]{:S(2)}) collective-permute-start(bf16[1,16,3712]{2,1,0:T(8,128)(2,1)S(1)} %collective-permute-done.3.refs_4_), channel_id=1, source_target_pairs={{0,1},{1,0},{2,3},{3,2},{4,5},{5,4},{6,7},{7,6},{8,9},{9,8},{10,11... | collective-permute-start | bytes 356360 | tf_op jit(solution)/shard_map/ppermute | solution.py:240
  20.8 1.5 %collective-permute-start.2 = (bf16[1,16,3712]{2,1,0:T(8,128)(2,1)S(1)}, bf16[1,16,3712]{2,1,0:T(8,128)(2,1)S(1)}, u32[]{:S(2)}, u32[]{:S(2)}) collective-permute-start(bf16[1,16,3712]{2,1,0:T(8,128)(2,1)S(1)} %collective-permute-done.1.refs_2_), channel_id=1, source_target_pairs={{0,1},{1,0},{2,3},{3,2},{4,5},{5,4},{6,7},{7,6},{8,9},{9,8},{10,11... | collective-permute-start | bytes 356360 | tf_op jit(solution)/shard_map/ppermute | solution.py:240
  22.3 25.2 %copy-start.6 = (f32[256]{0:T(256)S(1)}, f32[256]{0:T(256)}, u32[]{:S(2)}) copy-start(f32[256]{0:T(256)} %param.16) | copy-start | bytes 3076
  27.6 3.9 %collective-permute-start.7 = (bf16[4,16,1920]{2,1,0:T(8,128)(2,1)S(1)}, bf16[4,16,1920]{2,1,0:T(8,128)(2,1)S(1)}, u32[]{:S(2)}, u32[]{:S(2)}) collective-permute-start(bf16[4,16,1920]{2,1,0:T(8,128)(2,1)S(1)} %get-tuple-element.27), channel_id=1, source_target_pairs={{0,1},{1,0},{2,3},{3,2},{4,5},{5,4},{6,7},{7,6},{8,9},{9,8},{10,11... | collective-permute-start | bytes 737288 | tf_op jit(solution)/shard_map/ppermute | solution.py:240
  28.0 15.2 %collective-permute-start.11 = (bf16[128,1408]{1,0:T(8,128)(2,1)S(1)}, bf16[128,1408]{1,0:T(8,128)(2,1)S(1)}, u32[]{:S(2)}, u32[]{:S(2)}) collective-permute-start(bf16[128,1408]{1,0:T(8,128)(2,1)S(1)} %get-tuple-element.35), channel_id=1, source_target_pairs={{0,8},{8,0},{16,24},{24,16},{1,9},{9,1},{17,25},{25,17},{2,10},{10... | collective-permute-start | bytes 1081352 | tf_op jit(solution)/shard_map/ppermute | solution.py:285
  29.5 17.9 %collective-permute-start.12 = (bf16[128,1408]{1,0:T(8,128)(2,1)S(1)}, bf16[128,1408]{1,0:T(8,128)(2,1)S(1)}, u32[]{:S(2)}, u32[]{:S(2)}) collective-permute-start(bf16[128,1408]{1,0:T(8,128)(2,1)S(1)} %get-tuple-element.36), channel_id=1, source_target_pairs={{0,16},{8,24},{16,0},{24,8},{1,17},{9,25},{17,1},{25,9},{2,18},{10... | collective-permute-start | bytes 1081352 | tf_op jit(solution)/shard_map/ppermute | solution.py:285
  31.0 16.4 %collective-permute-start.13 = (bf16[128,1408]{1,0:T(8,128)(2,1)S(1)}, bf16[128,1408]{1,0:T(8,128)(2,1)S(1)}, u32[]{:S(2)}, u32[]{:S(2)}) collective-permute-start(bf16[128,1408]{1,0:T(8,128)(2,1)S(1)} %get-tuple-element.37), channel_id=1, source_target_pairs={{0,24},{8,16},{16,8},{24,0},{1,25},{9,17},{17,9},{25,1},{2,26},{10... | collective-permute-start | bytes 1081352 | tf_op jit(solution)/shard_map/ppermute | solution.py:285
  31.6 4.3 %collective-permute-start.8 = (bf16[16,1920]{1,0:T(8,128)(2,1)S(1)}, bf16[16,1920]{1,0:T(8,128)(2,1)S(1)}, u32[]{:S(2)}, u32[]{:S(2)}) collective-permute-start(bf16[16,1920]{1,0:T(8,128)(2,1)S(1)} %get-tuple-element.29), channel_id=1, source_target_pairs={{0,2},{1,3},{2,0},{3,1},{4,6},{5,7},{6,4},{7,5},{8,10},{9,11},{10,... | collective-permute-start | bytes 184328 | tf_op jit(solution)/shard_map/ppermute | solution.py:240
  31.7 6.7 %collective-permute-start.9 = (bf16[16,1920]{1,0:T(8,128)(2,1)S(1)}, bf16[16,1920]{1,0:T(8,128)(2,1)S(1)}, u32[]{:S(2)}, u32[]{:S(2)}) collective-permute-start(bf16[16,1920]{1,0:T(8,128)(2,1)S(1)} %get-tuple-element.30), channel_id=1, source_target_pairs={{0,4},{1,5},{2,6},{3,7},{4,0},{5,1},{6,2},{7,3},{8,12},{9,13},{10,... | collective-permute-start | bytes 184328 | tf_op jit(solution)/shard_map/ppermute | solution.py:240
  35.9 6.0 %collective-permute-start.10 = (bf16[16,1920]{1,0:T(8,128)(2,1)S(1)}, bf16[16,1920]{1,0:T(8,128)(2,1)S(1)}, u32[]{:S(2)}, u32[]{:S(2)}) collective-permute-start(bf16[16,1920]{1,0:T(8,128)(2,1)S(1)} %get-tuple-element.31), channel_id=1, source_target_pairs={{0,6},{1,7},{2,4},{3,5},{4,2},{5,3},{6,0},{7,1},{8,14},{9,15},{10,... | collective-permute-start | bytes 184328 | tf_op jit(solution)/shard_map/ppermute | solution.py:240

commit v2 on v1

v2 whole, which is shorter than its diff:
```python
import functools

import jax
import jax.numpy as jnp
from jax import lax
from jax.experimental import pallas as pl
from jax.experimental.pallas import tpu as pltpu
from jax.sharding import PartitionSpec as P

EXPERTS_ALL = 256
SPLIT = 8
CAP = 8
BLOCK = 2 * CAP
LANES = 128
bias_step = 0.125

F32 = jnp.float32
BF16 = jnp.bfloat16


def dot(left, right, left_dim, right_dim):
    return lax.dot_general(
        left, right, (((left_dim,), (right_dim,)), ((), ())), preferred_element_type=F32
    )


def call(kernel, outs, args, cost, scratch=(), space=pltpu.VMEM, limit=6, after=()):
    if lax.axis_size("expert") > SPLIT:
        limit = 60
    if after:
        inner = kernel

        def kernel(*refs):
            inner(*refs[: len(args)], *refs[len(args) + len(after) :])

    return pl.pallas_call(
        kernel,
        out_shape=outs,
        in_specs=[pl.BlockSpec(memory_space=space)] * len(args)
        + [pl.BlockSpec(memory_space=pl.ANY)] * len(after),
        out_specs=[pl.BlockSpec(memory_space=pltpu.VMEM)] * len(outs),
        scratch_shapes=list(scratch),
        compiler_params=pltpu.CompilerParams(vmem_limit_bytes=limit * 1024 * 1024),
        cost_estimate=pl.CostEstimate(flops=0, bytes_accessed=cost, transcendentals=0),
    )(*args, *after)


def select_kernel(flights, *refs):
    given, (pay_ref, sel_ref), held, sems = refs[:5], refs[5:7], refs[7:12], refs[12]
    copies = [pltpu.make_async_copy(given[at], held[at], sems.at[at]) for at in range(5)]
    for copy in copies:
        copy.start()
    tok_ref, grad_ref, route_ref, fixed_ref, loads_ref = held
    rows, width = tok_ref.shape
    before = lax.broadcasted_iota(jnp.int32, (rows, rows), 0) < lax.broadcasted_iota(
        jnp.int32, (rows, rows), 1
    )
    before = jnp.where(before, 1.0, 0.0).astype(BF16)
    place = lax.broadcasted_iota(jnp.int32, (CAP, rows), 0).astype(F32)
    for copy in copies[2:]:
        copy.wait()
    route, fixed = route_ref[...], fixed_ref[...].astype(F32)
    picks, gates = [], []
    for flight in range(flights):
        hot = route == flight
        mask = jnp.sum(jnp.where(hot, 1.0, 0.0), axis=0, keepdims=True)
        weight = jnp.sum(jnp.where(hot, fixed, 0.0), axis=0, keepdims=True) * (1.0 / 256.0)
        mask = jnp.broadcast_to(mask, (CAP, rows))
        slot = dot(mask.astype(BF16), before, 1, 0)
        pick = jnp.where(slot == place, mask, 0.0)
        picks.append(pick)
        gates.append(jnp.sum(pick * weight, axis=1, keepdims=True))
    pick = jnp.concatenate(picks, axis=0)
    sel_ref[...] = pick
    loads = loads_ref[...]
    high = loads // LANES
    low = (loads - high * LANES).astype(F32)
    high = high.astype(F32)
    line = lax.broadcasted_iota(jnp.int32, (CAP, LANES), 0)
    lane = lax.broadcasted_iota(jnp.int32, (CAP, LANES), 1)
    counts = jnp.zeros((CAP, LANES), F32)
    for at, part in enumerate((low[:, :LANES], low[:, LANES:], high[:, :LANES], high[:, LANES:])):
        counts = jnp.where(line == at, part, counts)
    for flight in range(flights):
        gate = jnp.where(lane == 0, gates[flight], 0.0)
        pay_ref[flight, :, width:] = jnp.concatenate([gate, counts], axis=0).astype(BF16)
    for copy in copies[:2]:
        copy.wait()
    rows_in = dot(pick.astype(BF16), tok_ref[...], 1, 0)
    rows_grad = dot(pick.astype(BF16), grad_ref[...], 1, 0)
    for flight in range(flights):
        own = slice(flight * CAP, (flight + 1) * CAP)
        pay_ref[flight, :, :width] = jnp.concatenate([rows_in[own], rows_grad[own]], axis=0).astype(
            BF16
        )


def quarter_kernel(shift, count, *refs):
    copies = lax.axis_size("dp")
    pay_refs, out_refs, all_refs = refs[:count], refs[count : count + copies], refs[count + copies :]
    quarter = out_refs[0].shape[1] - LANES
    width = quarter * copies
    me = lax.axis_index("dp")
    sums = 0.0
    for ref in pay_refs:
        sums = sums + jnp.sum(ref[:, :, width:].astype(F32), axis=0)
    total = sums[CAP : CAP + 2] + sums[CAP + 2 : CAP + 4] * LANES
    top = jnp.floor(total * (1.0 / LANES**2))
    rest = total - top * LANES**2
    middle = jnp.floor(rest * (1.0 / LANES))
    low = rest - middle * LANES
    line = lax.broadcasted_iota(jnp.int32, (BLOCK, LANES), 0)
    digits = jnp.zeros((BLOCK, LANES), F32)
    for place, value in enumerate((low, middle, top)):
        for lanes in range(2):
            digits = jnp.where(line == 2 * place + lanes, value[lanes : lanes + 1], digits)
    digits = digits.astype(BF16)
    for step, out_ref in enumerate(out_refs):
        start = pl.multiple_of(shift(me, step) * quarter, LANES)
        at = 0
        for ref in pay_refs:
            for block in range(ref.shape[0]):
                out_ref[at : at + BLOCK, :quarter] = ref[block, :, pl.ds(start, quarter)]
                out_ref[at : at + BLOCK, quarter:] = digits if at == 0 else jnp.zeros_like(digits)
                at += BLOCK
    for all_ref in all_refs:
        at = 0
        for ref in pay_refs:
            all_ref[at : at + ref.shape[0]] = ref[...]
            at += ref.shape[0]


def stack_kernel(*refs):
    for at, ref in enumerate(refs[:-1]):
        refs[-1][at] = ref[...]


def fetch_kernel(*refs):
    count = len(refs) // 2
    copies = [
        pltpu.make_async_copy(refs[at], refs[count + at], refs[-1].at[at]) for at in range(count)
    ]
    for copy in copies:
        copy.start()
    for copy in copies:
        copy.wait()


def expert_kernel(blocks, groups, *refs):
    pay_refs, refs = refs[: -(len(groups) + 5)], refs[-(len(groups) + 5) :]
    (gate_ref, up_ref, down_ref), back_refs, (grads_ref, rows_ref) = refs[:3], refs[3:-2], refs[-2:]
    width, units = gate_ref.shape
    half = width // 2
    pays = [ref[...].reshape(-1, ref.shape[-1]) for ref in pay_refs]
    at = 0
    for pay in pays:
        rows_ref[at : at + pay.shape[0], :] = pay[:, :width]
        at += pay.shape[0]
    extra = jnp.concatenate([pay[:, width:] for pay in pays], axis=0).astype(F32)
    extra = extra.reshape(blocks, BLOCK, LANES)
    row_gate = extra[:, :CAP, :1].reshape(blocks * CAP, 1)
    rows = rows_ref[...]

    def part(values, which):
        return values.reshape(blocks, BLOCK, values.shape[-1])[
            :, which * CAP : (which + 1) * CAP
        ].reshape(blocks * CAP, values.shape[-1])

    pre_gate = part(dot(rows, gate_ref[...], 1, 0), 0)
    pre_up = part(dot(rows, up_ref[...], 1, 0), 0)
    back_proj = part(dot(rows, down_ref[...], 1, 1), 1)
    sigmoid_gate = jax.nn.sigmoid(pre_gate)
    activated = pre_gate * sigmoid_gate
    hidden = activated * pre_up
    part_gate = jnp.sum(back_proj * hidden, axis=1, keepdims=True)
    grad_hidden = row_gate * back_proj
    grad_pregate = grad_hidden * pre_up * sigmoid_gate * (1.0 + pre_gate * (1.0 - sigmoid_gate))
    grad_preup = grad_hidden * activated
    scaled_hidden = row_gate * hidden

    grads_ref[...] = jnp.concatenate([grad_pregate, grad_preup, scaled_hidden], axis=1).astype(BF16)
    part_dx = dot(grad_pregate.astype(BF16), gate_ref[...], 1, 1) + dot(
        grad_preup.astype(BF16), up_ref[...], 1, 1
    )
    part_dx = part_dx.reshape(blocks, CAP, width)
    dx = jnp.concatenate([part_dx[:, :, :half], part_dx[:, :, half:]], axis=1).astype(BF16)
    lane = lax.broadcasted_iota(jnp.int32, (blocks, CAP, LANES), 2)
    tail = jnp.where(lane == 0, part_gate.reshape(blocks, CAP, 1), 0.0)
    tail = jnp.concatenate([tail, jnp.zeros_like(tail)], axis=1).astype(BF16)
    at = 0
    for ref in back_refs:
        ref[:, :, :half] = dx[at : at + ref.shape[0]]
        ref[:, :, half:] = tail[at : at + ref.shape[0]]
        at += ref.shape[0]


def pair_kernel(mine_ref, *refs):
    out_refs = refs[-mine_ref.shape[0] :]
    other = jnp.concatenate([ref[...] for ref in refs[: -len(out_refs)]], axis=0)
    total = mine_ref[...].astype(F32) + other.astype(F32)
    for at, ref in enumerate(out_refs):
        ref[...] = total[at].astype(ref.dtype)


def token_kernel(flights, sel_ref, route_ref, *refs):
    part_refs, (token_ref, gate_ref) = refs[:-2], refs[-2:]
    half = token_ref.shape[1] // 2
    total = 0.0
    for ref in part_refs:
        total = total + jnp.sum(ref[...].astype(F32), axis=1)
    total = total.reshape(flights, BLOCK, half + LANES)
    rows = jnp.concatenate([total[:, :CAP, :half], total[:, CAP:, :half]], axis=2)
    rows = rows.reshape(flights * CAP, 2 * half)
    pick = sel_ref[...]
    if flights == 1:
        token_ref[...] = dot(pick.astype(BF16), rows.astype(BF16), 0, 0).astype(BF16)
    else:
        token_ref[...] = lax.dot_general(
            pick,
            rows,
            (((0,), (0,)), ((), ())),
            precision=lax.Precision.HIGHEST,
            preferred_element_type=F32,
        ).astype(BF16)
    gates = jnp.zeros(gate_ref.shape, F32)
    for flight in range(flights):
        value = jnp.sum(
            pick[flight * CAP : (flight + 1) * CAP] * total[flight, :CAP, half : half + 1],
            axis=0,
            keepdims=True,
        )
        gates = jnp.where(route_ref[...] == flight, value, gates)
    gate_ref[...] = gates


def weight_kernel(units, blocks, copies, bias_ref, *refs):
    given, (gate_ref, up_ref, down_ref, new_ref) = refs[:-4], refs[-4:]
    quarter = gate_ref.shape[1]
    grads = [ref[...] for ref in given[:copies]]
    rows = []
    load = jnp.zeros((2, LANES), F32)
    for step in range(copies):
        for ref in given[copies:]:
            ref = ref if len(ref.shape) == 2 else ref.at[step]
            rows.append(ref[:, :quarter])
            digit = ref[:BLOCK, quarter:].astype(F32)
            load = load + digit[0:2] + digit[2:4] * LANES + digit[4:6] * LANES**2
    rows = jnp.concatenate(rows, axis=0)
    hidden, scaled = [], []
    for value in grads:
        value = value.astype(F32)
        value = value.reshape(blocks, CAP, value.shape[1])
        left, right = value[:, :, : 2 * units], value[:, :, 2 * units : 3 * units]
        left = jnp.concatenate([left, jnp.zeros_like(left)], axis=1)
        right = jnp.concatenate([jnp.zeros_like(right), right], axis=1)
        hidden.append(left.reshape(blocks * BLOCK, 2 * units).astype(BF16))
        scaled.append(right.reshape(blocks * BLOCK, units).astype(BF16))
    both = dot(rows, jnp.concatenate(hidden, axis=0), 0, 0)
    gate_ref[0] = both[:, :units].astype(BF16)
    up_ref[0] = both[:, units:].astype(BF16)
    down_ref[0] = dot(jnp.concatenate(scaled, axis=0), rows, 0, 0).astype(BF16)
    load = jnp.concatenate([load[0:1], load[1:2]], axis=1)
    diff = jnp.sum(load, axis=1, keepdims=True) - EXPERTS_ALL * load
    sign = jnp.where(diff > 0.0, 1.0, jnp.where(diff < 0.0, -1.0, 0.0))
    new_ref[...] = bias_ref[...] + bias_step * sign


def per_device(tokens, out_grad, route, gate_fixed, w_gate, w_up, w_down, router_bias, loads):
    row_count, width = tokens.shape
    top_count = route.shape[1]
    units = w_gate.shape[2]
    sources = lax.axis_size("expert")
    copies = lax.axis_size("dp")
    flights = sources // SPLIT
    half, quarter = width // 2, width // copies
    struct = jax.ShapeDtypeStruct

    given = [tokens, out_grad, route.T, gate_fixed.T, loads]
    payload, pick = call(
        functools.partial(select_kernel, flights),
        [struct((flights, BLOCK, width + LANES), BF16), struct((flights * CAP, row_count), F32)],
        given,
        4 * row_count * width,
        [pltpu.VMEM(a.shape, a.dtype) for a in given] + [pltpu.SemaphoreType.DMA((len(given),))],
        pltpu.HBM,
        60,
    )

    weights = [w_gate[0], w_up[0], w_down[0]]
    weights = call(
        fetch_kernel,
        [struct(w.shape, w.dtype) for w in weights],
        weights,
        4 * 10**7,
        [pltpu.SemaphoreType.DMA((len(weights),))],
        pltpu.HBM,
        8,
        after=[pick],
    )

    def swap(values, step):
        return lax.ppermute(values, "expert", [(i, i ^ step) for i in range(sources)])

    if flights == 1:
        near = [payload] + [swap(payload, step) for step in range(2, SPLIT, 2)]
        groups = [SPLIT // 2, SPLIT // 4, SPLIT // 4]
    else:
        spread = jnp.broadcast_to(payload[:, None], (flights, SPLIT) + payload.shape[1:])
        spread = spread.reshape((sources,) + payload.shape[1:])
        near = [lax.all_to_all(spread, "expert", split_axis=0, concat_axis=0, tiled=True)]
        groups = [sources]

    paired = copies & (copies - 1) == 0

    def shift(index, step):
        return index ^ step if paired else (index + step) % copies

    def across(values, step):
        return lax.ppermute(values, "dp", [(i, shift(i, step)) for i in range(copies)])

    rows = sources * BLOCK
    kept = groups[0] * BLOCK
    got = [struct((groups[0],) + payload.shape[1:], BF16)] if flights == 1 else []
    sent = call(
        functools.partial(quarter_kernel, shift, len(near)),
        [struct((kept, quarter + LANES), BF16)] * copies + got,
        near,
        1000,
        after=[weights[2]],
    )
    got = [sent[-1], swap(sent[-1], 1)] if flights == 1 else near
    rows_in = [sent[0]] + [across(sent[step], step) for step in range(1, copies)]

    *back, grads = call(
        functools.partial(expert_kernel, sources, groups),
        [struct((group, BLOCK, half + LANES), BF16) for group in groups]
        + [struct((sources * CAP, 3 * units), BF16)],
        [*got, *weights],
        4 * 10**7,
        [pltpu.VMEM((rows, width), BF16)],
        limit=18,
    )
    grads = [grads] + [across(grads, step) for step in range(1, copies)]

    if flights == 1:
        other = [swap(value, 1) for value in back[1:]]
        block = (BLOCK, half + LANES)
        sums = call(
            pair_kernel,
            [struct(block, F32)] + [struct(block, BF16)] * 3,
            [back[0], *other],
            1000,
            after=rows_in[1:],
        )
        parts = [sums[0]] + [swap(sums[at], 2 * at) for at in range(1, 4)]
        parts = [part.reshape((1, 1) + block) for part in parts]
        rows_in = call(
            stack_kernel,
            [struct((copies,) + rows_in[0].shape, BF16)],
            rows_in,
            1000,
            after=[sums[0]],
        )
        rows_in = [rows_in[0], swap(rows_in[0], 1)]
    else:
        parts = lax.all_to_all(back[0], "expert", split_axis=0, concat_axis=0, tiled=True)
        parts = [parts.reshape(flights, SPLIT, BLOCK, half + LANES)]
        rows_in = [jnp.stack(rows_in)]

    grad_gate, grad_up, grad_down, new_bias = call(
        functools.partial(weight_kernel, units, sources, copies),
        [
            struct((1, quarter, units), BF16),
            struct((1, quarter, units), BF16),
            struct((1, units, quarter), BF16),
            struct((1, EXPERTS_ALL), F32),
        ],
        [router_bias[None], *grads, *rows_in],
        1000,
    )
    token_grad, gate_grad = call(
        functools.partial(token_kernel, flights),
        [struct((row_count, width), BF16), struct((top_count, row_count), F32)],
        [pick, route.T] + parts,
        1000,
    )
    return (token_grad, gate_grad.T, grad_gate, grad_up, grad_down, new_bias[0])


def solution(mesh):
    in_specs = (
        P(("dp", "expert"), None),
        P(("dp", "expert"), None),
        P(("dp", "expert"), None),
        P(("dp", "expert"), None),
        P("expert", None, None),
        P("expert", None, None),
        P("expert", None, None),
        P(),
        P(("dp", "expert"), None),
    )
    out_specs = (
        P(("dp", "expert"), None),
        P(("dp", "expert"), None),
        P("expert", "dp", None),
        P("expert", "dp", None),
        P("expert", None, "dp"),
        P(),
    )
    return jax.shard_map(
        per_device, mesh=mesh, in_specs=in_specs, out_specs=out_specs, check_vma=False
    )
```

time: 49.5 us -> 45.2 us (0.913)
  waiting for transfers between devices: 19.3 us -> 11.6 us
  starting transfers between devices: 15.7 us -> 19.4 us
  local copies, waits for them, and re-layouts: 4.54 us -> 3.71 us
  Pallas kernels: 8.99 us -> 9.54 us
    ppermute x11 -> x10, waiting for transfers between devices: 15.2 us -> 8.97 us  [swap(): lax.ppermute(values, 'expert', [(i, i ^ step) for i in range(sources)])]
    ppermute x3 -> x6, starting transfers between devices: 3.49 us -> 7.21 us  [across(): lax.ppermute(values, 'dp', [(i, shift(i, step)) for i in range(copies)])]
    ppermute x3 -> x6, waiting for transfers between devices: 4.18 us -> 2.6 us  [across(): lax.ppermute(values, 'dp', [(i, shift(i, step)) for i in range(copies)])]
    unnamed x14 -> x16, local copies, waits for them, and re-layouts: 4.54 us -> 3.71 us
    pallas_call x5 -> x8, Pallas kernels: 8.99 us -> 9.54 us  [call(): pl.pallas_call(kernel, out_shape=outs, in_specs=[pl.BlockSpec(memory_spac...]
    ppermute x11 -> x10, starting transfers between devices: 12.2 us -> 12.1 us  [swap(): lax.ppermute(values, 'expert', [(i, i ^ step) for i in range(sources)])]
  transfers between devices with their start and end apart: 14 -> 16, of which waited for: 7 -> 3; matrix products, arithmetic and copies ran while one was open for 0% -> 0% of each run, Pallas kernels for 3% -> 11%
where the time goes in v2:
time: 45.2 us; the launch traced here: 45 us
  starting transfers between devices  19.4 us (43%)
  waiting for transfers between devices  11.6 us (26%)
  Pallas kernels  9.54 us (21%)
  local copies, waits for them, and re-layouts  3.71 us (8%)
  between operations  0.78 us (2%)
    ppermute x10, starting transfers between devices, swap(): lax.ppermute(values, 'expert', [(i, i ^ step) for i in range(sources)])  12.1 us
    pallas_call x8, Pallas kernels, call(): pl.pallas_call(kernel, out_shape=outs, in_specs=[pl.BlockSpec(memory_spac...  9.54 us
    ppermute x10, waiting for transfers between devices, swap(): lax.ppermute(values, 'expert', [(i, i ^ step) for i in range(sources)])  8.97 us
    ppermute x6, starting transfers between devices, across(): lax.ppermute(values, 'dp', [(i, shift(i, step)) for i in range(copies)])  7.21 us
    unnamed x16, local copies, waits for them, and re-layouts  3.71 us
    ppermute x6, waiting for transfers between devices, across(): lax.ppermute(values, 'dp', [(i, shift(i, step)) for i in range(copies)])  2.6 us
  transfers between devices with their start and end apart: 16, of which 3 were waited for; matrix products, arithmetic and copies ran while one was open for 0% of the time, Pallas kernels for 11%

profile of v2, /device:TPU:0, one launch (start us, length us, event | category | flops | bytes accessed | tf_op | source)
XLA Modules:
  0.0 45.0 jit_solution(16811302019989078146)
XLA Ops:
  0.6 2.7 %shard_map.136 = (bf16[1,16,3712]{2,1,0:T(8,128)(2,1)}, f32[8,128]{1,0:T(8,128)}) custom-call(bf16[128,3584]{1,0:T(8,128)(2,1)} %refs_0_.1, bf16[128,3584]{1,0:T(8,128)(2,1)} %refs_1_.1, s32[8,128]{1,0:T(8,128)} %bitcast.19, s32[8,128]{1,0:T(8,128)} %bitcast.22, s32[1,256]{1,0:T(1,128)} %refs_4_.1), custom_call_target="tpu_custom_call" | custom-call | bytes 1835008 | tf_op jit(solution)/shard_map/pallas_call | solution.py:36
  3.3 5.1 %collective-permute-start.2 = (bf16[1,16,3712]{2,1,0:T(8,128)(2,1)}, bf16[1,16,3712]{2,1,0:T(8,128)(2,1)S(1)}, u32[]{:S(2)}, u32[]{:S(2)}) collective-permute-start(bf16[1,16,3712]{2,1,0:T(8,128)(2,1)} %get-tuple-element.31.refs_0_), channel_id=1, source_target_pairs={{0,6},{1,7},{2,4},{3,5},{4,2},{5,3},{6,0},{7,1},{8,14},{9,15},{10,... | collective-permute-start | bytes 356360 | tf_op jit(solution)/shard_map/ppermute | solution.py:302
  8.4 0.6 %collective-permute-start = (bf16[1,16,3712]{2,1,0:T(8,128)(2,1)}, bf16[1,16,3712]{2,1,0:T(8,128)(2,1)S(1)}, u32[]{:S(2)}, u32[]{:S(2)}) collective-permute-start(bf16[1,16,3712]{2,1,0:T(8,128)(2,1)} %get-tuple-element.31.refs_0_), channel_id=1, source_target_pairs={{0,2},{1,3},{2,0},{3,1},{4,6},{5,7},{6,4},{7,5},{8,10},{9,11},{10,... | collective-permute-start | bytes 356360 | tf_op jit(solution)/shard_map/ppermute | solution.py:302
  9.1 1.5 %copy-done.1 = bf16[1,3584,256]{2,1,0:T(8,128)(2,1)S(1)} copy-done((bf16[1,3584,256]{2,1,0:T(8,128)(2,1)S(1)}, bf16[1,3584,256]{2,1,0:T(8,128)(2,1)}, u32[]{:S(2)}) %copy-start.1) | copy-done | bytes 1835032
  10.6 1.5 %copy-done.2 = bf16[1,256,3584]{2,1,0:T(8,128)(2,1)S(1)} copy-done((bf16[1,256,3584]{2,1,0:T(8,128)(2,1)S(1)}, bf16[1,256,3584]{2,1,0:T(8,128)(2,1)}, u32[]{:S(2)}) %copy-start.2) | copy-done | bytes 1835032
  12.1 0.7 %copy-done.5 = f32[8,128]{1,0:T(8,128)S(1)} copy-done((f32[8,128]{1,0:T(8,128)S(1)}, f32[8,128]{1,0:T(8,128)}, u32[]{:S(2)}) %copy-start.5) | copy-done | bytes 4120
  12.8 0.4 shard_map.137
  13.2 5.5 %collective-permute-done.1.refs_2_ = bf16[1,16,3712]{2,1,0:T(8,128)(2,1)S(1)} collective-permute-done((bf16[1,16,3712]{2,1,0:T(8,128)(2,1)}, bf16[1,16,3712]{2,1,0:T(8,128)(2,1)S(1)}, u32[]{:S(2)}, u32[]{:S(2)}) %collective-permute-start.1) | collective-permute-done | bytes 118816 | tf_op jit(solution)/shard_map/ppermute | solution.py:302
  18.7 0.1 shard_map.138
  18.7 0.1 collective-permute-start.3
  18.8 1.6 %collective-permute-start.6 = (bf16[64,1024]{1,0:T(8,128)(2,1)S(1)}, bf16[64,1024]{1,0:T(8,128)(2,1)S(1)}, u32[]{:S(2)}, u32[]{:S(2)}) collective-permute-start(bf16[64,1024]{1,0:T(8,128)(2,1)S(1)} %get-tuple-element.39), channel_id=1, source_target_pairs={{0,8},{8,0},{16,24},{24,16},{1,9},{9,1},{17,25},{25,17},{2,10},{10... | collective-permute-start | bytes 393224 | tf_op jit(solution)/shard_map/ppermute | solution.py:319
  20.4 1.5 %collective-permute-start.7 = (bf16[64,1024]{1,0:T(8,128)(2,1)S(1)}, bf16[64,1024]{1,0:T(8,128)(2,1)S(1)}, u32[]{:S(2)}, u32[]{:S(2)}) collective-permute-start(bf16[64,1024]{1,0:T(8,128)(2,1)S(1)} %get-tuple-element.40), channel_id=1, source_target_pairs={{0,16},{8,24},{16,0},{24,8},{1,17},{9,25},{17,1},{25,9},{2,18},{10... | collective-permute-start | bytes 393224 | tf_op jit(solution)/shard_map/ppermute | solution.py:319
  21.9 0.5 %collective-permute-start.8 = (bf16[64,1024]{1,0:T(8,128)(2,1)S(1)}, bf16[64,1024]{1,0:T(8,128)(2,1)S(1)}, u32[]{:S(2)}, u32[]{:S(2)}) collective-permute-start(bf16[64,1024]{1,0:T(8,128)(2,1)S(1)} %get-tuple-element.41), channel_id=1, source_target_pairs={{0,24},{8,16},{16,8},{24,0},{1,25},{9,17},{17,9},{25,1},{2,26},{10... | collective-permute-start | bytes 393224 | tf_op jit(solution)/shard_map/ppermute | solution.py:319
  22.4 3.2 %shard_map.139 = (bf16[4,16,1920]{2,1,0:T(8,128)(2,1)S(1)}, bf16[2,16,1920]{2,1,0:T(8,128)(2,1)S(1)}, bf16[2,16,1920]{2,1,0:T(8,128)(2,1)S(1)}, bf16[64,768]{1,0:T(8,128)(2,1)S(1)}) custom-call(bf16[4,16,3712]{2,1,0:T(8,128)(2,1)S(1)} %get-tuple-element.33.refs_0_, bf16[4,16,3712]{2,1,0:T(8,128)(2,1)S(1)} %collective-permute-done.3.refs_1_, ...), custom_call_target="tpu_custom_call" | custom-call | bytes 40000000 | tf_op jit(solution)/shard_map/pallas_call | solution.py:36
  25.6 0.0 copy-start.4
  25.6 0.0 copy-start.6
  25.6 0.0 copy-start.7
  25.6 0.1 collective-permute-start.4
  25.7 0.5 %collective-permute-start.5 = (bf16[2,16,1920]{2,1,0:T(8,128)(2,1)S(1)}, bf16[2,16,1920]{2,1,0:T(8,128)(2,1)S(1)}, u32[]{:S(2)}, u32[]{:S(2)}) collective-permute-start(bf16[2,16,1920]{2,1,0:T(8,128)(2,1)S(1)} %get-tuple-element.38), channel_id=1, source_target_pairs={{0,1},{1,0},{2,3},{3,2},{4,5},{5,4},{6,7},{7,6},{8,9},{9,8},{10,11... | collective-permute-start | bytes 368648 | tf_op jit(solution)/shard_map/ppermute | solution.py:302
  26.2 2.6 %collective-permute-done.7.refs_4_.refs_2_ = bf16[64,1024]{1,0:T(8,128)(2,1)S(1)} collective-permute-done((bf16[64,1024]{1,0:T(8,128)(2,1)S(1)}, bf16[64,1024]{1,0:T(8,128)(2,1)S(1)}, u32[]{:S(2)}, u32[]{:S(2)}) %collective-permute-start.7) | collective-permute-done | bytes 131104 | tf_op jit(solution)/shard_map/ppermute | solution.py:319
  28.8 0.1 shard_map.140
  28.9 0.1 collective-permute-start.15
  29.0 0.2 collective-permute-start.9
  29.1 3.0 %collective-permute-start.10 = (bf16[16,1920]{1,0:T(8,128)(2,1)S(1)}, bf16[16,1920]{1,0:T(8,128)(2,1)S(1)}, u32[]{:S(2)}, u32[]{:S(2)}) collective-permute-start(bf16[16,1920]{1,0:T(8,128)(2,1)S(1)} %get-tuple-element.44), channel_id=1, source_target_pairs={{0,4},{1,5},{2,6},{3,7},{4,0},{5,1},{6,2},{7,3},{8,12},{9,13},{10,... | collective-permute-start | bytes 184328 | tf_op jit(solution)/shard_map/ppermute | solution.py:302
  32.1 1.5 %collective-permute-start.14 = (bf16[64,768]{1,0:T(8,128)(2,1)S(1)}, bf16[64,768]{1,0:T(8,128)(2,1)S(1)}, u32[]{:S(2)}, u32[]{:S(2)}) collective-permute-start(bf16[64,768]{1,0:T(8,128)(2,1)S(1)} %get-tuple-element.48.refs_0_), channel_id=1, source_target_pairs={{0,24},{8,16},{16,8},{24,0},{1,25},{9,17},{17,9},{25,1},{2,26},{10... | collective-permute-start | bytes 294920 | tf_op jit(solution)/shard_map/ppermute | solution.py:319
  33.6 1.2 %collective-permute-start.13 = (bf16[64,768]{1,0:T(8,128)(2,1)S(1)}, bf16[64,768]{1,0:T(8,128)(2,1)S(1)}, u32[]{:S(2)}, u32[]{:S(2)}) collective-permute-start(bf16[64,768]{1,0:T(8,128)(2,1)S(1)} %get-tuple-element.48.refs_0_), channel_id=1, source_target_pairs={{0,16},{8,24},{16,0},{24,8},{1,17},{9,25},{17,1},{25,9},{2,18},{10... | collective-permute-start | bytes 294920 | tf_op jit(solution)/shard_map/ppermute | solution.py:319
  34.8 1.0 %collective-permute-start.12 = (bf16[64,768]{1,0:T(8,128)(2,1)S(1)}, bf16[64,768]{1,0:T(8,128)(2,1)S(1)}, u32[]{:S(2)}, u32[]{:S(2)}) collective-permute-start(bf16[64,768]{1,0:T(8,128)(2,1)S(1)} %get-tuple-element.48.refs_0_), channel_id=1, source_target_pairs={{0,8},{8,0},{16,24},{24,16},{1,9},{9,1},{17,25},{25,17},{2,10},{10... | collective-permute-start | bytes 294920 | tf_op jit(solution)/shard_map/ppermute | solution.py:319
  35.7 0.0 collective-permute-done.10
  35.8 2.6 %collective-permute-start.11 = (bf16[16,1920]{1,0:T(8,128)(2,1)S(1)}, bf16[16,1920]{1,0:T(8,128)(2,1)S(1)}, u32[]{:S(2)}, u32[]{:S(2)}) collective-permute-start(bf16[16,1920]{1,0:T(8,128)(2,1)S(1)} %get-tuple-element.45), channel_id=1, source_target_pairs={{0,6},{1,7},{2,4},{3,5},{4,2},{5,3},{6,0},{7,1},{8,14},{9,15},{10,... | collective-permute-start | bytes 184328 | tf_op jit(solution)/shard_map/ppermute | solution.py:302
  38.3 3.4 %collective-permute-done.11 = bf16[16,1920]{1,0:T(8,128)(2,1)S(1)} collective-permute-done((bf16[16,1920]{1,0:T(8,128)(2,1)S(1)}, bf16[16,1920]{1,0:T(8,128)(2,1)S(1)}, u32[]{:S(2)}, u32[]{:S(2)}) %collective-permute-start.11) | collective-permute-done | bytes 61472 | tf_op jit(solution)/shard_map/ppermute | solution.py:302
  41.8 1.3 %shard_map.141 = (bf16[128,3584]{1,0:T(8,128)(2,1)}, f32[8,128]{1,0:T(8,128)}) custom-call(f32[8,128]{1,0:T(8,128)S(1)} %copy-done.6, s32[8,128]{1,0:T(8,128)S(1)} %bitcast.20, f32[1,1,16,1920]{3,2,1,0:T(8,128)S(1)} %bitcast.15, bf16[1,1,16,1920]{3,2,1,0:T(8,128)(2,1)S(1)} %bitcast.16, bf16[1,1,16,1920]{3,2,1,0:T(8,128)(2,1)S(1)} %bitcast.17, ...), custom_call_target="tpu_custom_call" | custom-call | bytes 1000 | tf_op jit(solution)/shard_map/pallas_call | solution.py:36
  43.2 1.8 %shard_map.143 = (bf16[1,896,256]{2,1,0:T(8,128)(2,1)}, bf16[1,896,256]{2,1,0:T(8,128)(2,1)}, bf16[1,256,896]{2,1,0:T(8,128)(2,1)}, f32[1,256]{1,0:T(1,128)}) custom-call(f32[1,256]{1,0:T(1,128)S(1)} %bitcast.21, bf16[64,768]{1,0:T(8,128)(2,1)S(1)} %get-tuple-element.48.refs_0_, bf16[64,768]{1,0:T(8,128)(2,1)S(1)} %collective-permute-done.12.refs_1_, ...), custom_call_target="tpu_custom_call" | custom-call | bytes 1000 | tf_op jit(solution)/shard_map/pallas_call | solution.py:36
  (24 shorter events, 0.1 us)
Async XLA Ops:
  0.6 8.4 %copy-start = (bf16[1,3584,256]{2,1,0:T(8,128)(2,1)S(1)}, bf16[1,3584,256]{2,1,0:T(8,128)(2,1)}, u32[]{:S(2)}) copy-start(bf16[1,3584,256]{2,1,0:T(8,128)(2,1)} %param.13) | copy-start | bytes 5505028
  3.3 9.9 %collective-permute-start.2 = (bf16[1,16,3712]{2,1,0:T(8,128)(2,1)}, bf16[1,16,3712]{2,1,0:T(8,128)(2,1)S(1)}, u32[]{:S(2)}, u32[]{:S(2)}) collective-permute-start(bf16[1,16,3712]{2,1,0:T(8,128)(2,1)} %get-tuple-element.31.refs_0_), channel_id=1, source_target_pairs={{0,6},{1,7},{2,4},{3,5},{4,2},{5,3},{6,0},{7,1},{8,14},{9,15},{10,... | collective-permute-start | bytes 356360 | tf_op jit(solution)/shard_map/ppermute | solution.py:302
  8.4 10.2 %collective-permute-start.1 = (bf16[1,16,3712]{2,1,0:T(8,128)(2,1)}, bf16[1,16,3712]{2,1,0:T(8,128)(2,1)S(1)}, u32[]{:S(2)}, u32[]{:S(2)}) collective-permute-start(bf16[1,16,3712]{2,1,0:T(8,128)(2,1)} %get-tuple-element.31.refs_0_), channel_id=1, source_target_pairs={{0,4},{1,5},{2,6},{3,7},{4,0},{5,1},{6,2},{7,3},{8,12},{9,13},{10,... | collective-permute-start | bytes 356360 | tf_op jit(solution)/shard_map/ppermute | solution.py:302
  8.4 10.2 %collective-permute-start = (bf16[1,16,3712]{2,1,0:T(8,128)(2,1)}, bf16[1,16,3712]{2,1,0:T(8,128)(2,1)S(1)}, u32[]{:S(2)}, u32[]{:S(2)}) collective-permute-start(bf16[1,16,3712]{2,1,0:T(8,128)(2,1)} %get-tuple-element.31.refs_0_), channel_id=1, source_target_pairs={{0,2},{1,3},{2,0},{3,1},{4,6},{5,7},{6,4},{7,5},{8,10},{9,11},{10,... | collective-permute-start | bytes 356360 | tf_op jit(solution)/shard_map/ppermute | solution.py:302
  9.1 1.5 %copy-start.1 = (bf16[1,3584,256]{2,1,0:T(8,128)(2,1)S(1)}, bf16[1,3584,256]{2,1,0:T(8,128)(2,1)}, u32[]{:S(2)}) copy-start(bf16[1,3584,256]{2,1,0:T(8,128)(2,1)} %param.14) | copy-start | bytes 5505028
  10.6 1.5 %copy-start.2 = (bf16[1,256,3584]{2,1,0:T(8,128)(2,1)S(1)}, bf16[1,256,3584]{2,1,0:T(8,128)(2,1)}, u32[]{:S(2)}) copy-start(bf16[1,256,3584]{2,1,0:T(8,128)(2,1)} %param.15) | copy-start | bytes 5505028
  12.1 0.7 %copy-start.5 = (f32[8,128]{1,0:T(8,128)S(1)}, f32[8,128]{1,0:T(8,128)}, u32[]{:S(2)}) copy-start(f32[8,128]{1,0:T(8,128)} %get-tuple-element.30.refs_3_.sel_ref) | copy-start | bytes 12292
  12.8 5.9 %copy-start.3 = (bf16[1,16,3712]{2,1,0:T(8,128)(2,1)S(1)}, bf16[1,16,3712]{2,1,0:T(8,128)(2,1)}, u32[]{:S(2)}) copy-start(bf16[1,16,3712]{2,1,0:T(8,128)(2,1)} %get-tuple-element.31.refs_0_) | copy-start | bytes 356356
  18.7 3.6 %collective-permute-start.3 = (bf16[4,16,3712]{2,1,0:T(8,128)(2,1)S(1)}, bf16[4,16,3712]{2,1,0:T(8,128)(2,1)S(1)}, u32[]{:S(2)}, u32[]{:S(2)}) collective-permute-start(bf16[4,16,3712]{2,1,0:T(8,128)(2,1)S(1)} %get-tuple-element.33.refs_0_), channel_id=1, source_target_pairs={{0,1},{1,0},{2,3},{3,2},{4,5},{5,4},{6,7},{7,6},{8,9},{9,8},{10,11... | collective-permute-start | bytes 1425416 | tf_op jit(solution)/shard_map/ppermute | solution.py:302
  18.8 7.3 %collective-permute-start.6 = (bf16[64,1024]{1,0:T(8,128)(2,1)S(1)}, bf16[64,1024]{1,0:T(8,128)(2,1)S(1)}, u32[]{:S(2)}, u32[]{:S(2)}) collective-permute-start(bf16[64,1024]{1,0:T(8,128)(2,1)S(1)} %get-tuple-element.39), channel_id=1, source_target_pairs={{0,8},{8,0},{16,24},{24,16},{1,9},{9,1},{17,25},{25,17},{2,10},{10... | collective-permute-start | bytes 393224 | tf_op jit(solution)/shard_map/ppermute | solution.py:319
  20.4 8.4 %collective-permute-start.7 = (bf16[64,1024]{1,0:T(8,128)(2,1)S(1)}, bf16[64,1024]{1,0:T(8,128)(2,1)S(1)}, u32[]{:S(2)}, u32[]{:S(2)}) collective-permute-start(bf16[64,1024]{1,0:T(8,128)(2,1)S(1)} %get-tuple-element.40), channel_id=1, source_target_pairs={{0,16},{8,24},{16,0},{24,8},{1,17},{9,25},{17,1},{25,9},{2,18},{10... | collective-permute-start | bytes 393224 | tf_op jit(solution)/shard_map/ppermute | solution.py:319
  21.9 6.9 %collective-permute-start.8 = (bf16[64,1024]{1,0:T(8,128)(2,1)S(1)}, bf16[64,1024]{1,0:T(8,128)(2,1)S(1)}, u32[]{:S(2)}, u32[]{:S(2)}) collective-permute-start(bf16[64,1024]{1,0:T(8,128)(2,1)S(1)} %get-tuple-element.41), channel_id=1, source_target_pairs={{0,24},{8,16},{16,8},{24,0},{1,25},{9,17},{17,9},{25,1},{2,26},{10... | collective-permute-start | bytes 393224 | tf_op jit(solution)/shard_map/ppermute | solution.py:319
  25.6 16.2 %copy-start.4 = (s32[128,8]{0,1:T(8,128)S(1)}, s32[128,8]{0,1:T(8,128)}, u32[]{:S(2)}) copy-start(s32[128,8]{0,1:T(8,128)} %param.11) | copy-start | bytes 12292
  25.6 16.2 %copy-start.6 = (f32[8,128]{1,0:T(8,128)S(1)}, f32[8,128]{1,0:T(8,128)}, u32[]{:S(2)}) copy-start(f32[8,128]{1,0:T(8,128)} %get-tuple-element.30.refs_3_.sel_ref) | copy-start | bytes 12292
  25.6 17.6 %copy-start.7 = (f32[256]{0:T(256)S(1)}, f32[256]{0:T(256)}, u32[]{:S(2)}) copy-start(f32[256]{0:T(256)} %param.16) | copy-start | bytes 3076
  25.6 3.2 %collective-permute-start.4 = (bf16[2,16,1920]{2,1,0:T(8,128)(2,1)S(1)}, bf16[2,16,1920]{2,1,0:T(8,128)(2,1)S(1)}, u32[]{:S(2)}, u32[]{:S(2)}) collective-permute-start(bf16[2,16,1920]{2,1,0:T(8,128)(2,1)S(1)} %get-tuple-element.37), channel_id=1, source_target_pairs={{0,1},{1,0},{2,3},{3,2},{4,5},{5,4},{6,7},{7,6},{8,9},{9,8},{10,11... | collective-permute-start | bytes 368648 | tf_op jit(solution)/shard_map/ppermute | solution.py:302
  25.7 3.1 %collective-permute-start.5 = (bf16[2,16,1920]{2,1,0:T(8,128)(2,1)S(1)}, bf16[2,16,1920]{2,1,0:T(8,128)(2,1)S(1)}, u32[]{:S(2)}, u32[]{:S(2)}) collective-permute-start(bf16[2,16,1920]{2,1,0:T(8,128)(2,1)S(1)} %get-tuple-element.38), channel_id=1, source_target_pairs={{0,1},{1,0},{2,3},{3,2},{4,5},{5,4},{6,7},{7,6},{8,9},{9,8},{10,11... | collective-permute-start | bytes 368648 | tf_op jit(solution)/shard_map/ppermute | solution.py:302
  28.9 14.3 %collective-permute-start.15 = (bf16[4,64,1024]{2,1,0:T(8,128)(2,1)S(1)}, bf16[4,64,1024]{2,1,0:T(8,128)(2,1)S(1)}, u32[]{:S(2)}, u32[]{:S(2)}) collective-permute-start(bf16[4,64,1024]{2,1,0:T(8,128)(2,1)S(1)} %shard_map.142.refs_4_), channel_id=1, source_target_pairs={{0,1},{1,0},{2,3},{3,2},{4,5},{5,4},{6,7},{7,6},{8,9},{9,8},{10,11... | collective-permute-start | bytes 1572872 | tf_op jit(solution)/shard_map/ppermute | solution.py:302
  29.0 5.8 %collective-permute-start.9 = (bf16[16,1920]{1,0:T(8,128)(2,1)S(1)}, bf16[16,1920]{1,0:T(8,128)(2,1)S(1)}, u32[]{:S(2)}, u32[]{:S(2)}) collective-permute-start(bf16[16,1920]{1,0:T(8,128)(2,1)S(1)} %get-tuple-element.43), channel_id=1, source_target_pairs={{0,2},{1,3},{2,0},{3,1},{4,6},{5,7},{6,4},{7,5},{8,10},{9,11},{10,... | collective-permute-start | bytes 184328 | tf_op jit(solution)/shard_map/ppermute | solution.py:302
  29.1 6.6 %collective-permute-start.10 = (bf16[16,1920]{1,0:T(8,128)(2,1)S(1)}, bf16[16,1920]{1,0:T(8,128)(2,1)S(1)}, u32[]{:S(2)}, u32[]{:S(2)}) collective-permute-start(bf16[16,1920]{1,0:T(8,128)(2,1)S(1)} %get-tuple-element.44), channel_id=1, source_target_pairs={{0,4},{1,5},{2,6},{3,7},{4,0},{5,1},{6,2},{7,3},{8,12},{9,13},{10,... | collective-permute-start | bytes 184328 | tf_op jit(solution)/shard_map/ppermute | solution.py:302
  32.1 11.1 %collective-permute-start.14 = (bf16[64,768]{1,0:T(8,128)(2,1)S(1)}, bf16[64,768]{1,0:T(8,128)(2,1)S(1)}, u32[]{:S(2)}, u32[]{:S(2)}) collective-permute-start(bf16[64,768]{1,0:T(8,128)(2,1)S(1)} %get-tuple-element.48.refs_0_), channel_id=1, source_target_pairs={{0,24},{8,16},{16,8},{24,0},{1,25},{9,17},{17,9},{25,1},{2,26},{10... | collective-permute-start | bytes 294920 | tf_op jit(solution)/shard_map/ppermute | solution.py:319
  33.6 9.6 %collective-permute-start.13 = (bf16[64,768]{1,0:T(8,128)(2,1)S(1)}, bf16[64,768]{1,0:T(8,128)(2,1)S(1)}, u32[]{:S(2)}, u32[]{:S(2)}) collective-permute-start(bf16[64,768]{1,0:T(8,128)(2,1)S(1)} %get-tuple-element.48.refs_0_), channel_id=1, source_target_pairs={{0,16},{8,24},{16,0},{24,8},{1,17},{9,25},{17,1},{25,9},{2,18},{10... | collective-permute-start | bytes 294920 | tf_op jit(solution)/shard_map/ppermute | solution.py:319
  34.8 8.4 %collective-permute-start.12 = (bf16[64,768]{1,0:T(8,128)(2,1)S(1)}, bf16[64,768]{1,0:T(8,128)(2,1)S(1)}, u32[]{:S(2)}, u32[]{:S(2)}) collective-permute-start(bf16[64,768]{1,0:T(8,128)(2,1)S(1)} %get-tuple-element.48.refs_0_), channel_id=1, source_target_pairs={{0,8},{8,0},{16,24},{24,16},{1,9},{9,1},{17,25},{25,17},{2,10},{10... | collective-permute-start | bytes 294920 | tf_op jit(solution)/shard_map/ppermute | solution.py:319
  35.8 6.0 %collective-permute-start.11 = (bf16[16,1920]{1,0:T(8,128)(2,1)S(1)}, bf16[16,1920]{1,0:T(8,128)(2,1)S(1)}, u32[]{:S(2)}, u32[]{:S(2)}) collective-permute-start(bf16[16,1920]{1,0:T(8,128)(2,1)S(1)} %get-tuple-element.45), channel_id=1, source_target_pairs={{0,6},{1,7},{2,4},{3,5},{4,2},{5,3},{6,0},{7,1},{8,14},{9,15},{10,... | collective-permute-start | bytes 184328 | tf_op jit(solution)/shard_map/ppermute | solution.py:302

commit v3 on v2

--- a/solution.py
+++ b/solution.py
@@ -98,30 +98,14 @@
 def quarter_kernel(shift, count, *refs):
     copies = lax.axis_size("dp")
     pay_refs, out_refs, all_refs = refs[:count], refs[count : count + copies], refs[count + copies :]
-    quarter = out_refs[0].shape[1] - LANES
-    width = quarter * copies
+    quarter = out_refs[0].shape[1]
     me = lax.axis_index("dp")
-    sums = 0.0
-    for ref in pay_refs:
-        sums = sums + jnp.sum(ref[:, :, width:].astype(F32), axis=0)
-    total = sums[CAP : CAP + 2] + sums[CAP + 2 : CAP + 4] * LANES
-    top = jnp.floor(total * (1.0 / LANES**2))
-    rest = total - top * LANES**2
-    middle = jnp.floor(rest * (1.0 / LANES))
-    low = rest - middle * LANES
-    line = lax.broadcasted_iota(jnp.int32, (BLOCK, LANES), 0)
-    digits = jnp.zeros((BLOCK, LANES), F32)
-    for place, value in enumerate((low, middle, top)):
-        for lanes in range(2):
-            digits = jnp.where(line == 2 * place + lanes, value[lanes : lanes + 1], digits)
-    digits = digits.astype(BF16)
     for step, out_ref in enumerate(out_refs):
         start = pl.multiple_of(shift(me, step) * quarter, LANES)
         at = 0
         for ref in pay_refs:
             for block in range(ref.shape[0]):
-                out_ref[at : at + BLOCK, :quarter] = ref[block, :, pl.ds(start, quarter)]
-                out_ref[at : at + BLOCK, quarter:] = digits if at == 0 else jnp.zeros_like(digits)
+                out_ref[at : at + BLOCK, :] = ref[block, :, pl.ds(start, quarter)]
                 at += BLOCK
     for all_ref in all_refs:
         at = 0
@@ -135,21 +119,18 @@
         refs[-1][at] = ref[...]
 
 
-def fetch_kernel(*refs):
-    count = len(refs) // 2
-    copies = [
-        pltpu.make_async_copy(refs[at], refs[count + at], refs[-1].at[at]) for at in range(count)
-    ]
-    for copy in copies:
-        copy.start()
-    for copy in copies:
-        copy.wait()
+def turn_kernel(gate_ref, up_ref, down_ref, in_ref, down_turned_ref, in_turned_ref):
+    units = gate_ref.shape[1]
+    for at, ref in enumerate((gate_ref, up_ref)):
+        in_ref[:, at * units : (at + 1) * units] = ref[...]
+        in_turned_ref[at * units : (at + 1) * units, :] = ref[...].T
+    down_turned_ref[...] = down_ref[...].T
 
 
 def expert_kernel(blocks, groups, *refs):
     pay_refs, refs = refs[: -(len(groups) + 5)], refs[-(len(groups) + 5) :]
-    (gate_ref, up_ref, down_ref), back_refs, (grads_ref, rows_ref) = refs[:3], refs[3:-2], refs[-2:]
-    width, units = gate_ref.shape
+    (in_ref, down_ref, turned_ref), back_refs, (grads_ref, rows_ref) = refs[:3], refs[3:-2], refs[-2:]
+    width, units = down_ref.shape
     half = width // 2
     pays = [ref[...].reshape(-1, ref.shape[-1]) for ref in pay_refs]
     at = 0
@@ -166,9 +147,9 @@
             :, which * CAP : (which + 1) * CAP
         ].reshape(blocks * CAP, values.shape[-1])
 
-    pre_gate = part(dot(rows, gate_ref[...], 1, 0), 0)
-    pre_up = part(dot(rows, up_ref[...], 1, 0), 0)
-    back_proj = part(dot(rows, down_ref[...], 1, 1), 1)
+    pre = part(dot(rows, in_ref[...], 1, 0), 0)
+    pre_gate, pre_up = pre[:, :units], pre[:, units:]
+    back_proj = part(dot(rows, down_ref[...], 1, 0), 1)
     sigmoid_gate = jax.nn.sigmoid(pre_gate)
     activated = pre_gate * sigmoid_gate
     hidden = activated * pre_up
@@ -178,10 +159,22 @@
     grad_preup = grad_hidden * activated
     scaled_hidden = row_gate * hidden
 
-    grads_ref[...] = jnp.concatenate([grad_pregate, grad_preup, scaled_hidden], axis=1).astype(BF16)
-    part_dx = dot(grad_pregate.astype(BF16), gate_ref[...], 1, 1) + dot(
-        grad_preup.astype(BF16), up_ref[...], 1, 1
-    )
+    grad_in = jnp.concatenate([grad_pregate, grad_preup], axis=1).astype(BF16)
+    grads_ref[:, : 2 * units] = grad_in
+    grads_ref[:, 2 * units : 3 * units] = scaled_hidden.astype(BF16)
+    sums = jnp.sum(extra[:, CAP : CAP + 4], axis=0)
+    total = sums[0:2] + sums[2:4] * LANES
+    top = jnp.floor(total * (1.0 / LANES**2))
+    rest = total - top * LANES**2
+    middle = jnp.floor(rest * (1.0 / LANES))
+    low = rest - middle * LANES
+    line = lax.broadcasted_iota(jnp.int32, (blocks * CAP, LANES), 0)
+    digits = jnp.zeros((blocks * CAP, LANES), F32)
+    for place, value in enumerate((low, middle, top)):
+        for lanes in range(2):
+            digits = jnp.where(line == 2 * place + lanes, value[lanes : lanes + 1], digits)
+    grads_ref[:, 3 * units :] = digits.astype(BF16)
+    part_dx = dot(grad_in, turned_ref[...], 1, 0)
     part_dx = part_dx.reshape(blocks, CAP, width)
     dx = jnp.concatenate([part_dx[:, :, :half], part_dx[:, :, half:]], axis=1).astype(BF16)
     lane = lax.broadcasted_iota(jnp.int32, (blocks, CAP, LANES), 2)
@@ -242,13 +235,13 @@
     for step in range(copies):
         for ref in given[copies:]:
             ref = ref if len(ref.shape) == 2 else ref.at[step]
-            rows.append(ref[:, :quarter])
-            digit = ref[:BLOCK, quarter:].astype(F32)
-            load = load + digit[0:2] + digit[2:4] * LANES + digit[4:6] * LANES**2
+            rows.append(ref[...])
     rows = jnp.concatenate(rows, axis=0)
     hidden, scaled = [], []
     for value in grads:
         value = value.astype(F32)
+        digit = value[:CAP, 3 * units :]
+        load = load + digit[0:2] + digit[2:4] * LANES + digit[4:6] * LANES**2
         value = value.reshape(blocks, CAP, value.shape[1])
         left, right = value[:, :, : 2 * units], value[:, :, 2 * units : 3 * units]
         left = jnp.concatenate([left, jnp.zeros_like(left)], axis=1)
@@ -288,13 +281,15 @@
 
     weights = [w_gate[0], w_up[0], w_down[0]]
     weights = call(
-        fetch_kernel,
-        [struct(w.shape, w.dtype) for w in weights],
+        turn_kernel,
+        [
+            struct((width, 2 * units), BF16),
+            struct((width, units), BF16),
+            struct((2 * units, width), BF16),
+        ],
         weights,
         4 * 10**7,
-        [pltpu.SemaphoreType.DMA((len(weights),))],
-        pltpu.HBM,
-        8,
+        limit=16,
         after=[pick],
     )
 
@@ -303,7 +298,7 @@
 
     if flights == 1:
         near = [payload] + [swap(payload, step) for step in range(2, SPLIT, 2)]
-        groups = [SPLIT // 2, SPLIT // 4, SPLIT // 4]
+        groups = [4, 1, 3]
     else:
         spread = jnp.broadcast_to(payload[:, None], (flights, SPLIT) + payload.shape[1:])
         spread = spread.reshape((sources,) + payload.shape[1:])
@@ -323,7 +318,7 @@
     got = [struct((groups[0],) + payload.shape[1:], BF16)] if flights == 1 else []
     sent = call(
         functools.partial(quarter_kernel, shift, len(near)),
-        [struct((kept, quarter + LANES), BF16)] * copies + got,
+        [struct((kept, quarter), BF16)] * copies + got,
         near,
         1000,
         after=[weights[2]],
@@ -334,7 +329,7 @@
     *back, grads = call(
         functools.partial(expert_kernel, sources, groups),
         [struct((group, BLOCK, half + LANES), BF16) for group in groups]
-        + [struct((sources * CAP, 3 * units), BF16)],
+        + [struct((sources * CAP, 3 * units + LANES), BF16)],
         [*got, *weights],
         4 * 10**7,
         [pltpu.VMEM((rows, width), BF16)],
@@ -344,24 +339,24 @@
 
     if flights == 1:
         other = [swap(value, 1) for value in back[1:]]
+        rows_in = call(
+            stack_kernel,
+            [struct((copies,) + rows_in[0].shape, BF16)],
+            rows_in,
+            1000,
+            after=[other[0]],
+        )
+        rows_in = [rows_in[0], swap(rows_in[0], 1)]
         block = (BLOCK, half + LANES)
         sums = call(
             pair_kernel,
             [struct(block, F32)] + [struct(block, BF16)] * 3,
             [back[0], *other],
             1000,
-            after=rows_in[1:],
+            after=[rows_in[1]],
         )
         parts = [sums[0]] + [swap(sums[at], 2 * at) for at in range(1, 4)]
         parts = [part.reshape((1, 1) + block) for part in parts]
-        rows_in = call(
-            stack_kernel,
-            [struct((copies,) + rows_in[0].shape, BF16)],
-            rows_in,
-            1000,
-            after=[sums[0]],
-        )
-        rows_in = [rows_in[0], swap(rows_in[0], 1)]
     else:
         parts = lax.all_to_all(back[0], "expert", split_axis=0, concat_axis=0, tiled=True)
         parts = [parts.reshape(flights, SPLIT, BLOCK, half + LANES)]

time: 45.2 us -> 43.1 us (0.954)
  waiting for transfers between devices: 11.6 us -> 9.71 us
    ppermute x10, waiting for transfers between devices: 8.97 us -> 5.9 us  [swap(): lax.ppermute(values, 'expert', [(i, i ^ step) for i in range(sources)])]
    ppermute x6, waiting for transfers between devices: 2.6 us -> 3.82 us  [across(): lax.ppermute(values, 'dp', [(i, shift(i, step)) for i in range(copies)])]
  transfers between devices with their start and end apart: 16 -> 16, of which waited for: 3 -> 4; matrix products, arithmetic and copies ran while one was open for 0% -> 0% of each run, Pallas kernels for 11% -> 13%
where the time goes in v3:
time: 43.1 us; the launch traced here: 42.9 us
  starting transfers between devices  19.1 us (44%)
  waiting for transfers between devices  9.71 us (23%)
  Pallas kernels  9.65 us (22%)
  local copies, waits for them, and re-layouts  3.71 us (9%)
  between operations  0.77 us (2%)
    ppermute x10, starting transfers between devices, swap(): lax.ppermute(values, 'expert', [(i, i ^ step) for i in range(sources)])  12 us
    pallas_call x8, Pallas kernels, call(): pl.pallas_call(kernel, out_shape=outs, in_specs=[pl.BlockSpec(memory_spac...  9.65 us
    ppermute x6, starting transfers between devices, across(): lax.ppermute(values, 'dp', [(i, shift(i, step)) for i in range(copies)])  7.04 us
    ppermute x10, waiting for transfers between devices, swap(): lax.ppermute(values, 'expert', [(i, i ^ step) for i in range(sources)])  5.9 us
    ppermute x6, waiting for transfers between devices, across(): lax.ppermute(values, 'dp', [(i, shift(i, step)) for i in range(copies)])  3.82 us
    unnamed x16, local copies, waits for them, and re-layouts  3.71 us
  transfers between devices with their start and end apart: 16, of which 4 were waited for; matrix products, arithmetic and copies ran while one was open for 0% of the time, Pallas kernels for 13%

profile of v3, /device:TPU:0, one launch (start us, length us, event | category | flops | bytes accessed | tf_op | source)
XLA Modules:
  0.0 42.9 jit_solution(5083548769790371546)
XLA Ops:
  0.6 2.7 %shard_map.136 = (bf16[1,16,3712]{2,1,0:T(8,128)(2,1)}, f32[8,128]{1,0:T(8,128)}) custom-call(bf16[128,3584]{1,0:T(8,128)(2,1)} %refs_0_.1, bf16[128,3584]{1,0:T(8,128)(2,1)} %refs_1_.1, s32[8,128]{1,0:T(8,128)} %bitcast.19, s32[8,128]{1,0:T(8,128)} %bitcast.22, s32[1,256]{1,0:T(1,128)} %refs_4_.1), custom_call_target="tpu_custom_call" | custom-call | bytes 1835008 | tf_op jit(solution)/shard_map/pallas_call | solution.py:36
  3.3 5.1 %collective-permute-start.2 = (bf16[1,16,3712]{2,1,0:T(8,128)(2,1)}, bf16[1,16,3712]{2,1,0:T(8,128)(2,1)S(1)}, u32[]{:S(2)}, u32[]{:S(2)}) collective-permute-start(bf16[1,16,3712]{2,1,0:T(8,128)(2,1)} %get-tuple-element.31.refs_0_), channel_id=1, source_target_pairs={{0,6},{1,7},{2,4},{3,5},{4,2},{5,3},{6,0},{7,1},{8,14},{9,15},{10,... | collective-permute-start | bytes 356360 | tf_op jit(solution)/shard_map/ppermute | solution.py:297
  8.4 0.6 %collective-permute-start = (bf16[1,16,3712]{2,1,0:T(8,128)(2,1)}, bf16[1,16,3712]{2,1,0:T(8,128)(2,1)S(1)}, u32[]{:S(2)}, u32[]{:S(2)}) collective-permute-start(bf16[1,16,3712]{2,1,0:T(8,128)(2,1)} %get-tuple-element.31.refs_0_), channel_id=1, source_target_pairs={{0,2},{1,3},{2,0},{3,1},{4,6},{5,7},{6,4},{7,5},{8,10},{9,11},{10,... | collective-permute-start | bytes 356360 | tf_op jit(solution)/shard_map/ppermute | solution.py:297
  9.1 1.5 %copy-done.1 = bf16[1,3584,256]{2,1,0:T(8,128)(2,1)S(1)} copy-done((bf16[1,3584,256]{2,1,0:T(8,128)(2,1)S(1)}, bf16[1,3584,256]{2,1,0:T(8,128)(2,1)}, u32[]{:S(2)}) %copy-start.1) | copy-done | bytes 1835032
  10.6 1.5 %copy-done.2 = bf16[1,256,3584]{2,1,0:T(8,128)(2,1)S(1)} copy-done((bf16[1,256,3584]{2,1,0:T(8,128)(2,1)S(1)}, bf16[1,256,3584]{2,1,0:T(8,128)(2,1)}, u32[]{:S(2)}) %copy-start.2) | copy-done | bytes 1835032
  12.1 0.7 %copy-done.5 = f32[8,128]{1,0:T(8,128)S(1)} copy-done((f32[8,128]{1,0:T(8,128)S(1)}, f32[8,128]{1,0:T(8,128)}, u32[]{:S(2)}) %copy-start.5) | copy-done | bytes 4120
  12.8 1.7 %shard_map.137 = (bf16[3584,512]{1,0:T(8,128)(2,1)S(1)}, bf16[3584,256]{1,0:T(8,128)(2,1)S(1)}, bf16[512,3584]{1,0:T(8,128)(2,1)S(1)}) custom-call(bf16[3584,256]{1,0:T(8,128)(2,1)S(1)} %bitcast.12, bf16[3584,256]{1,0:T(8,128)(2,1)S(1)} %bitcast.13, bf16[256,3584]{1,0:T(8,128)(2,1)S(1)} %bitcast.14, f32[8,128]{1,0:T(8,128)S(1)} %copy-done.5), custom_call_target="tpu_custom_call" | custom-call | bytes 40000000 | tf_op jit(solution)/shard_map/pallas_call | solution.py:36
  14.5 4.2 %collective-permute-done.1.refs_2_ = bf16[1,16,3712]{2,1,0:T(8,128)(2,1)S(1)} collective-permute-done((bf16[1,16,3712]{2,1,0:T(8,128)(2,1)}, bf16[1,16,3712]{2,1,0:T(8,128)(2,1)S(1)}, u32[]{:S(2)}, u32[]{:S(2)}) %collective-permute-start.1) | collective-permute-done | bytes 118816 | tf_op jit(solution)/shard_map/ppermute | solution.py:297
  18.7 0.1 shard_map.138
  18.7 0.1 collective-permute-start.3
  18.8 1.6 %collective-permute-start.6 = (bf16[64,896]{1,0:T(8,128)(2,1)S(1)}, bf16[64,896]{1,0:T(8,128)(2,1)S(1)}, u32[]{:S(2)}, u32[]{:S(2)}) collective-permute-start(bf16[64,896]{1,0:T(8,128)(2,1)S(1)} %get-tuple-element.40), channel_id=1, source_target_pairs={{0,8},{8,0},{16,24},{24,16},{1,9},{9,1},{17,25},{25,17},{2,10},{10... | collective-permute-start | bytes 344072 | tf_op jit(solution)/shard_map/ppermute | solution.py:314
  20.4 1.5 %collective-permute-start.7 = (bf16[64,896]{1,0:T(8,128)(2,1)S(1)}, bf16[64,896]{1,0:T(8,128)(2,1)S(1)}, u32[]{:S(2)}, u32[]{:S(2)}) collective-permute-start(bf16[64,896]{1,0:T(8,128)(2,1)S(1)} %get-tuple-element.41), channel_id=1, source_target_pairs={{0,16},{8,24},{16,0},{24,8},{1,17},{9,25},{17,1},{25,9},{2,18},{10... | collective-permute-start | bytes 344072 | tf_op jit(solution)/shard_map/ppermute | solution.py:314
  21.9 0.5 %collective-permute-start.8 = (bf16[64,896]{1,0:T(8,128)(2,1)S(1)}, bf16[64,896]{1,0:T(8,128)(2,1)S(1)}, u32[]{:S(2)}, u32[]{:S(2)}) collective-permute-start(bf16[64,896]{1,0:T(8,128)(2,1)S(1)} %get-tuple-element.42), channel_id=1, source_target_pairs={{0,24},{8,16},{16,8},{24,0},{1,25},{9,17},{17,9},{25,1},{2,26},{10... | collective-permute-start | bytes 344072 | tf_op jit(solution)/shard_map/ppermute | solution.py:314
  22.4 2.0 %shard_map.139 = (bf16[4,16,1920]{2,1,0:T(8,128)(2,1)S(1)}, bf16[1,16,1920]{2,1,0:T(8,128)(2,1)S(1)}, bf16[3,16,1920]{2,1,0:T(8,128)(2,1)S(1)}, bf16[64,896]{1,0:T(8,128)(2,1)S(1)}) custom-call(bf16[4,16,3712]{2,1,0:T(8,128)(2,1)S(1)} %get-tuple-element.33.refs_0_, bf16[4,16,3712]{2,1,0:T(8,128)(2,1)S(1)} %collective-permute-done.3.refs_1_, ...), custom_call_target="tpu_custom_call" | custom-call | bytes 40000000 | tf_op jit(solution)/shard_map/pallas_call | solution.py:36
  24.3 0.0 copy-start.7
  24.4 0.0 copy-start.4
  24.4 0.0 copy-start.6
  24.4 0.1 collective-permute-start.4
  24.5 3.6 %collective-permute-done.7.refs_2_ = bf16[64,896]{1,0:T(8,128)(2,1)S(1)} collective-permute-done((bf16[64,896]{1,0:T(8,128)(2,1)S(1)}, bf16[64,896]{1,0:T(8,128)(2,1)S(1)}, u32[]{:S(2)}, u32[]{:S(2)}) %collective-permute-start.7) | collective-permute-done | bytes 114720 | tf_op jit(solution)/shard_map/ppermute | solution.py:314
  28.1 0.1 collective-permute-start.9
  28.2 0.5 %collective-permute-start.5 = (bf16[3,16,1920]{2,1,0:T(8,128)(2,1)S(1)}, bf16[3,16,1920]{2,1,0:T(8,128)(2,1)S(1)}, u32[]{:S(2)}, u32[]{:S(2)}) collective-permute-start(bf16[3,16,1920]{2,1,0:T(8,128)(2,1)S(1)} %get-tuple-element.38), channel_id=1, source_target_pairs={{0,1},{1,0},{2,3},{3,2},{4,5},{5,4},{6,7},{7,6},{8,9},{9,8},{10,11... | collective-permute-start | bytes 552968 | tf_op jit(solution)/shard_map/ppermute | solution.py:297
  28.7 1.5 %collective-permute-start.15 = (bf16[64,896]{1,0:T(8,128)(2,1)S(1)}, bf16[64,896]{1,0:T(8,128)(2,1)S(1)}, u32[]{:S(2)}, u32[]{:S(2)}) collective-permute-start(bf16[64,896]{1,0:T(8,128)(2,1)S(1)} %get-tuple-element.49.refs_0_), channel_id=1, source_target_pairs={{0,24},{8,16},{16,8},{24,0},{1,25},{9,17},{17,9},{25,1},{2,26},{10... | collective-permute-start | bytes 344072 | tf_op jit(solution)/shard_map/ppermute | solution.py:314
  30.2 1.2 %collective-permute-start.14 = (bf16[64,896]{1,0:T(8,128)(2,1)S(1)}, bf16[64,896]{1,0:T(8,128)(2,1)S(1)}, u32[]{:S(2)}, u32[]{:S(2)}) collective-permute-start(bf16[64,896]{1,0:T(8,128)(2,1)S(1)} %get-tuple-element.49.refs_0_), channel_id=1, source_target_pairs={{0,16},{8,24},{16,0},{24,8},{1,17},{9,25},{17,1},{25,9},{2,18},{10... | collective-permute-start | bytes 344072 | tf_op jit(solution)/shard_map/ppermute | solution.py:314
  31.4 0.8 %collective-permute-start.13 = (bf16[64,896]{1,0:T(8,128)(2,1)S(1)}, bf16[64,896]{1,0:T(8,128)(2,1)S(1)}, u32[]{:S(2)}, u32[]{:S(2)}) collective-permute-start(bf16[64,896]{1,0:T(8,128)(2,1)S(1)} %get-tuple-element.49.refs_0_), channel_id=1, source_target_pairs={{0,8},{8,0},{16,24},{24,16},{1,9},{9,1},{17,25},{25,17},{2,10},{10... | collective-permute-start | bytes 344072 | tf_op jit(solution)/shard_map/ppermute | solution.py:314
  32.2 0.1 shard_map.141
  32.2 0.2 collective-permute-start.10
  32.4 3.0 %collective-permute-start.11 = (bf16[16,1920]{1,0:T(8,128)(2,1)S(1)}, bf16[16,1920]{1,0:T(8,128)(2,1)S(1)}, u32[]{:S(2)}, u32[]{:S(2)}) collective-permute-start(bf16[16,1920]{1,0:T(8,128)(2,1)S(1)} %get-tuple-element.45), channel_id=1, source_target_pairs={{0,4},{1,5},{2,6},{3,7},{4,0},{5,1},{6,2},{7,3},{8,12},{9,13},{10,... | collective-permute-start | bytes 184328 | tf_op jit(solution)/shard_map/ppermute | solution.py:297
  35.3 0.2 collective-permute-done.15.refs_3_
  35.6 2.5 %collective-permute-start.12 = (bf16[16,1920]{1,0:T(8,128)(2,1)S(1)}, bf16[16,1920]{1,0:T(8,128)(2,1)S(1)}, u32[]{:S(2)}, u32[]{:S(2)}) collective-permute-start(bf16[16,1920]{1,0:T(8,128)(2,1)S(1)} %get-tuple-element.46), channel_id=1, source_target_pairs={{0,6},{1,7},{2,4},{3,5},{4,2},{5,3},{6,0},{7,1},{8,14},{9,15},{10,... | collective-permute-start | bytes 184328 | tf_op jit(solution)/shard_map/ppermute | solution.py:297
  38.1 1.8 %shard_map.143 = (bf16[1,896,256]{2,1,0:T(8,128)(2,1)}, bf16[1,896,256]{2,1,0:T(8,128)(2,1)}, bf16[1,256,896]{2,1,0:T(8,128)(2,1)}, f32[1,256]{1,0:T(1,128)}) custom-call(f32[1,256]{1,0:T(1,128)S(1)} %bitcast.21, bf16[64,896]{1,0:T(8,128)(2,1)S(1)} %get-tuple-element.49.refs_0_, bf16[64,896]{1,0:T(8,128)(2,1)S(1)} %collective-permute-done.13.refs_1_, ...), custom_call_target="tpu_custom_call" | custom-call | bytes 1000 | tf_op jit(solution)/shard_map/pallas_call | solution.py:36
  39.9 1.7 %collective-permute-done.12 = bf16[16,1920]{1,0:T(8,128)(2,1)S(1)} collective-permute-done((bf16[16,1920]{1,0:T(8,128)(2,1)S(1)}, bf16[16,1920]{1,0:T(8,128)(2,1)S(1)}, u32[]{:S(2)}, u32[]{:S(2)}) %collective-permute-start.12) | collective-permute-done | bytes 61472 | tf_op jit(solution)/shard_map/ppermute | solution.py:297
  41.6 1.3 %shard_map.142 = (bf16[128,3584]{1,0:T(8,128)(2,1)}, f32[8,128]{1,0:T(8,128)}) custom-call(f32[8,128]{1,0:T(8,128)S(1)} %copy-done.6, s32[8,128]{1,0:T(8,128)S(1)} %bitcast.20, f32[1,1,16,1920]{3,2,1,0:T(8,128)S(1)} %bitcast.15, bf16[1,1,16,1920]{3,2,1,0:T(8,128)(2,1)S(1)} %bitcast.16, bf16[1,1,16,1920]{3,2,1,0:T(8,128)(2,1)S(1)} %bitcast.17, ...), custom_call_target="tpu_custom_call" | custom-call | bytes 1000 | tf_op jit(solution)/shard_map/pallas_call | solution.py:36
  (24 shorter events, 0.1 us)
Async XLA Ops:
  0.6 8.4 %copy-start = (bf16[1,3584,256]{2,1,0:T(8,128)(2,1)S(1)}, bf16[1,3584,256]{2,1,0:T(8,128)(2,1)}, u32[]{:S(2)}) copy-start(bf16[1,3584,256]{2,1,0:T(8,128)(2,1)} %param.13) | copy-start | bytes 5505028
  3.3 11.2 %collective-permute-start.2 = (bf16[1,16,3712]{2,1,0:T(8,128)(2,1)}, bf16[1,16,3712]{2,1,0:T(8,128)(2,1)S(1)}, u32[]{:S(2)}, u32[]{:S(2)}) collective-permute-start(bf16[1,16,3712]{2,1,0:T(8,128)(2,1)} %get-tuple-element.31.refs_0_), channel_id=1, source_target_pairs={{0,6},{1,7},{2,4},{3,5},{4,2},{5,3},{6,0},{7,1},{8,14},{9,15},{10,... | collective-permute-start | bytes 356360 | tf_op jit(solution)/shard_map/ppermute | solution.py:297
  8.4 10.2 %collective-permute-start.1 = (bf16[1,16,3712]{2,1,0:T(8,128)(2,1)}, bf16[1,16,3712]{2,1,0:T(8,128)(2,1)S(1)}, u32[]{:S(2)}, u32[]{:S(2)}) collective-permute-start(bf16[1,16,3712]{2,1,0:T(8,128)(2,1)} %get-tuple-element.31.refs_0_), channel_id=1, source_target_pairs={{0,4},{1,5},{2,6},{3,7},{4,0},{5,1},{6,2},{7,3},{8,12},{9,13},{10,... | collective-permute-start | bytes 356360 | tf_op jit(solution)/shard_map/ppermute | solution.py:297
  8.4 10.2 %collective-permute-start = (bf16[1,16,3712]{2,1,0:T(8,128)(2,1)}, bf16[1,16,3712]{2,1,0:T(8,128)(2,1)S(1)}, u32[]{:S(2)}, u32[]{:S(2)}) collective-permute-start(bf16[1,16,3712]{2,1,0:T(8,128)(2,1)} %get-tuple-element.31.refs_0_), channel_id=1, source_target_pairs={{0,2},{1,3},{2,0},{3,1},{4,6},{5,7},{6,4},{7,5},{8,10},{9,11},{10,... | collective-permute-start | bytes 356360 | tf_op jit(solution)/shard_map/ppermute | solution.py:297
  9.1 1.5 %copy-start.1 = (bf16[1,3584,256]{2,1,0:T(8,128)(2,1)S(1)}, bf16[1,3584,256]{2,1,0:T(8,128)(2,1)}, u32[]{:S(2)}) copy-start(bf16[1,3584,256]{2,1,0:T(8,128)(2,1)} %param.14) | copy-start | bytes 5505028
  10.6 1.5 %copy-start.2 = (bf16[1,256,3584]{2,1,0:T(8,128)(2,1)S(1)}, bf16[1,256,3584]{2,1,0:T(8,128)(2,1)}, u32[]{:S(2)}) copy-start(bf16[1,256,3584]{2,1,0:T(8,128)(2,1)} %param.15) | copy-start | bytes 5505028
  12.1 0.7 %copy-start.5 = (f32[8,128]{1,0:T(8,128)S(1)}, f32[8,128]{1,0:T(8,128)}, u32[]{:S(2)}) copy-start(f32[8,128]{1,0:T(8,128)} %get-tuple-element.30.refs_3_.sel_ref) | copy-start | bytes 12292
  12.8 5.9 %copy-start.3 = (bf16[1,16,3712]{2,1,0:T(8,128)(2,1)S(1)}, bf16[1,16,3712]{2,1,0:T(8,128)(2,1)}, u32[]{:S(2)}) copy-start(bf16[1,16,3712]{2,1,0:T(8,128)(2,1)} %get-tuple-element.31.refs_0_) | copy-start | bytes 356356
  18.7 3.6 %collective-permute-start.3 = (bf16[4,16,3712]{2,1,0:T(8,128)(2,1)S(1)}, bf16[4,16,3712]{2,1,0:T(8,128)(2,1)S(1)}, u32[]{:S(2)}, u32[]{:S(2)}) collective-permute-start(bf16[4,16,3712]{2,1,0:T(8,128)(2,1)S(1)} %get-tuple-element.33.refs_0_), channel_id=1, source_target_pairs={{0,1},{1,0},{2,3},{3,2},{4,5},{5,4},{6,7},{7,6},{8,9},{9,8},{10,11... | collective-permute-start | bytes 1425416 | tf_op jit(solution)/shard_map/ppermute | solution.py:297
  18.8 5.7 %collective-permute-start.6 = (bf16[64,896]{1,0:T(8,128)(2,1)S(1)}, bf16[64,896]{1,0:T(8,128)(2,1)S(1)}, u32[]{:S(2)}, u32[]{:S(2)}) collective-permute-start(bf16[64,896]{1,0:T(8,128)(2,1)S(1)} %get-tuple-element.40), channel_id=1, source_target_pairs={{0,8},{8,0},{16,24},{24,16},{1,9},{9,1},{17,25},{25,17},{2,10},{10... | collective-permute-start | bytes 344072 | tf_op jit(solution)/shard_map/ppermute | solution.py:314
  20.4 7.7 %collective-permute-start.7 = (bf16[64,896]{1,0:T(8,128)(2,1)S(1)}, bf16[64,896]{1,0:T(8,128)(2,1)S(1)}, u32[]{:S(2)}, u32[]{:S(2)}) collective-permute-start(bf16[64,896]{1,0:T(8,128)(2,1)S(1)} %get-tuple-element.41), channel_id=1, source_target_pairs={{0,16},{8,24},{16,0},{24,8},{1,17},{9,25},{17,1},{25,9},{2,18},{10... | collective-permute-start | bytes 344072 | tf_op jit(solution)/shard_map/ppermute | solution.py:314
  21.9 6.2 %collective-permute-start.8 = (bf16[64,896]{1,0:T(8,128)(2,1)S(1)}, bf16[64,896]{1,0:T(8,128)(2,1)S(1)}, u32[]{:S(2)}, u32[]{:S(2)}) collective-permute-start(bf16[64,896]{1,0:T(8,128)(2,1)S(1)} %get-tuple-element.42), channel_id=1, source_target_pairs={{0,24},{8,16},{16,8},{24,0},{1,25},{9,17},{17,9},{25,1},{2,26},{10... | collective-permute-start | bytes 344072 | tf_op jit(solution)/shard_map/ppermute | solution.py:314
  24.3 13.7 %copy-start.7 = (f32[256]{0:T(256)S(1)}, f32[256]{0:T(256)}, u32[]{:S(2)}) copy-start(f32[256]{0:T(256)} %param.16) | copy-start | bytes 3076
  24.4 17.2 %copy-start.4 = (s32[128,8]{0,1:T(8,128)S(1)}, s32[128,8]{0,1:T(8,128)}, u32[]{:S(2)}) copy-start(s32[128,8]{0,1:T(8,128)} %param.11) | copy-start | bytes 12292
  24.4 17.2 %copy-start.6 = (f32[8,128]{1,0:T(8,128)S(1)}, f32[8,128]{1,0:T(8,128)}, u32[]{:S(2)}) copy-start(f32[8,128]{1,0:T(8,128)} %get-tuple-element.30.refs_3_.sel_ref) | copy-start | bytes 12292
  24.4 3.7 %collective-permute-start.4 = (bf16[1,16,1920]{2,1,0:T(8,128)(2,1)S(1)}, bf16[1,16,1920]{2,1,0:T(8,128)(2,1)S(1)}, u32[]{:S(2)}, u32[]{:S(2)}) collective-permute-start(bf16[1,16,1920]{2,1,0:T(8,128)(2,1)S(1)} %get-tuple-element.37), channel_id=1, source_target_pairs={{0,1},{1,0},{2,3},{3,2},{4,5},{5,4},{6,7},{7,6},{8,9},{9,8},{10,11... | collective-permute-start | bytes 184328 | tf_op jit(solution)/shard_map/ppermute | solution.py:297
  28.1 4.1 %collective-permute-start.9 = (bf16[4,64,896]{2,1,0:T(8,128)(2,1)S(1)}, bf16[4,64,896]{2,1,0:T(8,128)(2,1)S(1)}, u32[]{:S(2)}, u32[]{:S(2)}) collective-permute-start(bf16[4,64,896]{2,1,0:T(8,128)(2,1)S(1)} %shard_map.140.refs_4_), channel_id=1, source_target_pairs={{0,1},{1,0},{2,3},{3,2},{4,5},{5,4},{6,7},{7,6},{8,9},{9,8},{10,11... | collective-permute-start | bytes 1376264 | tf_op jit(solution)/shard_map/ppermute | solution.py:297
  28.2 4.0 %collective-permute-start.5 = (bf16[3,16,1920]{2,1,0:T(8,128)(2,1)S(1)}, bf16[3,16,1920]{2,1,0:T(8,128)(2,1)S(1)}, u32[]{:S(2)}, u32[]{:S(2)}) collective-permute-start(bf16[3,16,1920]{2,1,0:T(8,128)(2,1)S(1)} %get-tuple-element.38), channel_id=1, source_target_pairs={{0,1},{1,0},{2,3},{3,2},{4,5},{5,4},{6,7},{7,6},{8,9},{9,8},{10,11... | collective-permute-start | bytes 552968 | tf_op jit(solution)/shard_map/ppermute | solution.py:297
  28.7 6.9 %collective-permute-start.15 = (bf16[64,896]{1,0:T(8,128)(2,1)S(1)}, bf16[64,896]{1,0:T(8,128)(2,1)S(1)}, u32[]{:S(2)}, u32[]{:S(2)}) collective-permute-start(bf16[64,896]{1,0:T(8,128)(2,1)S(1)} %get-tuple-element.49.refs_0_), channel_id=1, source_target_pairs={{0,24},{8,16},{16,8},{24,0},{1,25},{9,17},{17,9},{25,1},{2,26},{10... | collective-permute-start | bytes 344072 | tf_op jit(solution)/shard_map/ppermute | solution.py:314
  30.2 7.9 %collective-permute-start.14 = (bf16[64,896]{1,0:T(8,128)(2,1)S(1)}, bf16[64,896]{1,0:T(8,128)(2,1)S(1)}, u32[]{:S(2)}, u32[]{:S(2)}) collective-permute-start(bf16[64,896]{1,0:T(8,128)(2,1)S(1)} %get-tuple-element.49.refs_0_), channel_id=1, source_target_pairs={{0,16},{8,24},{16,0},{24,8},{1,17},{9,25},{17,1},{25,9},{2,18},{10... | collective-permute-start | bytes 344072 | tf_op jit(solution)/shard_map/ppermute | solution.py:314
  31.4 6.7 %collective-permute-start.13 = (bf16[64,896]{1,0:T(8,128)(2,1)S(1)}, bf16[64,896]{1,0:T(8,128)(2,1)S(1)}, u32[]{:S(2)}, u32[]{:S(2)}) collective-permute-start(bf16[64,896]{1,0:T(8,128)(2,1)S(1)} %get-tuple-element.49.refs_0_), channel_id=1, source_target_pairs={{0,8},{8,0},{16,24},{24,16},{1,9},{9,1},{17,25},{25,17},{2,10},{10... | collective-permute-start | bytes 344072 | tf_op jit(solution)/shard_map/ppermute | solution.py:314
  32.2 7.6 %collective-permute-start.10 = (bf16[16,1920]{1,0:T(8,128)(2,1)S(1)}, bf16[16,1920]{1,0:T(8,128)(2,1)S(1)}, u32[]{:S(2)}, u32[]{:S(2)}) collective-permute-start(bf16[16,1920]{1,0:T(8,128)(2,1)S(1)} %get-tuple-element.44), channel_id=1, source_target_pairs={{0,2},{1,3},{2,0},{3,1},{4,6},{5,7},{6,4},{7,5},{8,10},{9,11},{10,... | collective-permute-start | bytes 184328 | tf_op jit(solution)/shard_map/ppermute | solution.py:297
  32.4 7.5 %collective-permute-start.11 = (bf16[16,1920]{1,0:T(8,128)(2,1)S(1)}, bf16[16,1920]{1,0:T(8,128)(2,1)S(1)}, u32[]{:S(2)}, u32[]{:S(2)}) collective-permute-start(bf16[16,1920]{1,0:T(8,128)(2,1)S(1)} %get-tuple-element.45), channel_id=1, source_target_pairs={{0,4},{1,5},{2,6},{3,7},{4,0},{5,1},{6,2},{7,3},{8,12},{9,13},{10,... | collective-permute-start | bytes 184328 | tf_op jit(solution)/shard_map/ppermute | solution.py:297
  35.6 6.0 %collective-permute-start.12 = (bf16[16,1920]{1,0:T(8,128)(2,1)S(1)}, bf16[16,1920]{1,0:T(8,128)(2,1)S(1)}, u32[]{:S(2)}, u32[]{:S(2)}) collective-permute-start(bf16[16,1920]{1,0:T(8,128)(2,1)S(1)} %get-tuple-element.46), channel_id=1, source_target_pairs={{0,6},{1,7},{2,4},{3,5},{4,2},{5,3},{6,0},{7,1},{8,14},{9,15},{10,... | collective-permute-start | bytes 184328 | tf_op jit(solution)/shard_map/ppermute | solution.py:297

commit v4 on v3

--- a/solution.py
+++ b/solution.py
@@ -24,15 +24,17 @@
     )
 
 
-def call(kernel, outs, args, cost, scratch=(), space=pltpu.VMEM, limit=6, after=()):
+def call(kernel, outs, args, cost, scratch=(), space=pltpu.VMEM, limit=6, after=(), order=None):
     if lax.axis_size("expert") > SPLIT:
         limit = 60
-    if after:
-        inner = kernel
-
-        def kernel(*refs):
-            inner(*refs[: len(args)], *refs[len(args) + len(after) :])
-
+    order = order or range(len(args))
+    inner = kernel
+
+    def kernel(*refs):
+        given = [refs[order.index(at)] for at in range(len(args))]
+        inner(*given, *refs[len(args) + len(after) :])
+
+    args = [args[at] for at in order]
     return pl.pallas_call(
         kernel,
         out_shape=outs,
@@ -322,6 +324,7 @@
         near,
         1000,
         after=[weights[2]],
+        order=[0, 3, 1, 2] if flights == 1 else None,
     )
     got = [sent[-1], swap(sent[-1], 1)] if flights == 1 else near
     rows_in = [sent[0]] + [across(sent[step], step) for step in range(1, copies)]
@@ -345,6 +348,7 @@
             rows_in,
             1000,
             after=[other[0]],
+            order=[0, *range(copies - 1, 0, -1)],
         )
         rows_in = [rows_in[0], swap(rows_in[0], 1)]
         block = (BLOCK, half + LANES)
@@ -378,6 +382,7 @@
         [struct((row_count, width), BF16), struct((top_count, row_count), F32)],
         [pick, route.T] + parts,
         1000,
+        order=[0, 1, 2, 5, 4, 3] if flights == 1 else None,
     )
     return (token_grad, gate_grad.T, grad_gate, grad_up, grad_down, new_bias[0])
 

time: 43.1 us -> 41 us (0.951)
  waiting for transfers between devices: 9.71 us -> 7.77 us
    ppermute x10, waiting for transfers between devices: 5.9 us -> 4.38 us  [swap(): lax.ppermute(values, 'expert', [(i, i ^ step) for i in range(sources)])]
  transfers between devices with their start and end apart: 16 -> 16, of which waited for: 4 -> 7; matrix products, arithmetic and copies ran while one was open for 0% -> 0% of each run, Pallas kernels for 13% -> 14%
where the time goes in v4:
time: 41 us; the launch traced here: 40.8 us
  starting transfers between devices  18.9 us (46%)
  Pallas kernels  9.66 us (24%)
  waiting for transfers between devices  7.77 us (19%)
  local copies, waits for them, and re-layouts  3.71 us (9%)
  between operations  0.75 us (2%)
    ppermute x10, starting transfers between devices, swap(): lax.ppermute(values, 'expert', [(i, i ^ step) for i in range(sources)])  11.9 us
    pallas_call x8, Pallas kernels, call(): pl.pallas_call(kernel, out_shape=outs, in_specs=[pl.BlockSpec(memory_spac...  9.66 us
    ppermute x6, starting transfers between devices, across(): lax.ppermute(values, 'dp', [(i, shift(i, step)) for i in range(copies)])  7.04 us
    ppermute x10, waiting for transfers between devices, swap(): lax.ppermute(values, 'expert', [(i, i ^ step) for i in range(sources)])  4.38 us
    unnamed x16, local copies, waits for them, and re-layouts  3.71 us
    ppermute x6, waiting for transfers between devices, across(): lax.ppermute(values, 'dp', [(i, shift(i, step)) for i in range(copies)])  3.39 us
  transfers between devices with their start and end apart: 16, of which 7 were waited for; matrix products, arithmetic and copies ran while one was open for 0% of the time, Pallas kernels for 14%

profile of v4, /device:TPU:0, one launch (start us, length us, event | category | flops | bytes accessed | tf_op | source)
XLA Modules:
  0.0 40.8 jit_solution(13617791013486229005)
XLA Ops:
  0.6 2.7 %shard_map.136 = (bf16[1,16,3712]{2,1,0:T(8,128)(2,1)}, f32[8,128]{1,0:T(8,128)}) custom-call(bf16[128,3584]{1,0:T(8,128)(2,1)} %refs_0_.1, bf16[128,3584]{1,0:T(8,128)(2,1)} %refs_1_.1, s32[8,128]{1,0:T(8,128)} %bitcast.19, s32[8,128]{1,0:T(8,128)} %bitcast.22, s32[1,256]{1,0:T(1,128)} %refs_4_.1), custom_call_target="tpu_custom_call" | custom-call | bytes 1835008 | tf_op jit(solution)/shard_map/pallas_call | solution.py:38
  3.3 4.1 %collective-permute-start.2 = (bf16[1,16,3712]{2,1,0:T(8,128)(2,1)}, bf16[1,16,3712]{2,1,0:T(8,128)(2,1)S(1)}, u32[]{:S(2)}, u32[]{:S(2)}) collective-permute-start(bf16[1,16,3712]{2,1,0:T(8,128)(2,1)} %get-tuple-element.31.refs_0_), channel_id=1, source_target_pairs={{0,4},{1,5},{2,6},{3,7},{4,0},{5,1},{6,2},{7,3},{8,12},{9,13},{10,... | collective-permute-start | bytes 356360 | tf_op jit(solution)/shard_map/ppermute | solution.py:299
  7.4 1.6 %collective-permute-start.1 = (bf16[1,16,3712]{2,1,0:T(8,128)(2,1)}, bf16[1,16,3712]{2,1,0:T(8,128)(2,1)S(1)}, u32[]{:S(2)}, u32[]{:S(2)}) collective-permute-start(bf16[1,16,3712]{2,1,0:T(8,128)(2,1)} %get-tuple-element.31.refs_0_), channel_id=1, source_target_pairs={{0,2},{1,3},{2,0},{3,1},{4,6},{5,7},{6,4},{7,5},{8,10},{9,11},{10,... | collective-permute-start | bytes 356360 | tf_op jit(solution)/shard_map/ppermute | solution.py:299
  9.0 1.5 %copy-done.1 = bf16[1,3584,256]{2,1,0:T(8,128)(2,1)S(1)} copy-done((bf16[1,3584,256]{2,1,0:T(8,128)(2,1)S(1)}, bf16[1,3584,256]{2,1,0:T(8,128)(2,1)}, u32[]{:S(2)}) %copy-start.1) | copy-done | bytes 1835032
  10.5 1.5 %copy-done.2 = bf16[1,256,3584]{2,1,0:T(8,128)(2,1)S(1)} copy-done((bf16[1,256,3584]{2,1,0:T(8,128)(2,1)S(1)}, bf16[1,256,3584]{2,1,0:T(8,128)(2,1)}, u32[]{:S(2)}) %copy-start.2) | copy-done | bytes 1835032
  12.0 0.7 %copy-done.5 = f32[8,128]{1,0:T(8,128)S(1)} copy-done((f32[8,128]{1,0:T(8,128)S(1)}, f32[8,128]{1,0:T(8,128)}, u32[]{:S(2)}) %copy-start.5) | copy-done | bytes 4120
  12.7 1.7 %shard_map.137 = (bf16[3584,512]{1,0:T(8,128)(2,1)S(1)}, bf16[3584,256]{1,0:T(8,128)(2,1)S(1)}, bf16[512,3584]{1,0:T(8,128)(2,1)S(1)}) custom-call(bf16[3584,256]{1,0:T(8,128)(2,1)S(1)} %bitcast.12, bf16[3584,256]{1,0:T(8,128)(2,1)S(1)} %bitcast.13, bf16[256,3584]{1,0:T(8,128)(2,1)S(1)} %bitcast.14, f32[8,128]{1,0:T(8,128)S(1)} %copy-done.5), custom_call_target="tpu_custom_call" | custom-call | bytes 40000000 | tf_op jit(solution)/shard_map/pallas_call | solution.py:38
  14.4 0.6 %collective-permute-done.2.refs_3_ = bf16[1,16,3712]{2,1,0:T(8,128)(2,1)S(1)} collective-permute-done((bf16[1,16,3712]{2,1,0:T(8,128)(2,1)}, bf16[1,16,3712]{2,1,0:T(8,128)(2,1)S(1)}, u32[]{:S(2)}, u32[]{:S(2)}) %collective-permute-start.2) | collective-permute-done | bytes 118816 | tf_op jit(solution)/shard_map/ppermute | solution.py:299
  15.0 2.1 %collective-permute-done.refs_1_ = bf16[1,16,3712]{2,1,0:T(8,128)(2,1)S(1)} collective-permute-done((bf16[1,16,3712]{2,1,0:T(8,128)(2,1)}, bf16[1,16,3712]{2,1,0:T(8,128)(2,1)S(1)}, u32[]{:S(2)}, u32[]{:S(2)}) %collective-permute-start) | collective-permute-done | bytes 118816 | tf_op jit(solution)/shard_map/ppermute | solution.py:299
  17.1 0.1 shard_map.138
  17.2 0.1 collective-permute-start.3
  17.3 2.5 %collective-permute-start.6 = (bf16[64,896]{1,0:T(8,128)(2,1)S(1)}, bf16[64,896]{1,0:T(8,128)(2,1)S(1)}, u32[]{:S(2)}, u32[]{:S(2)}) collective-permute-start(bf16[64,896]{1,0:T(8,128)(2,1)S(1)} %get-tuple-element.40), channel_id=1, source_target_pairs={{0,24},{8,16},{16,8},{24,0},{1,25},{9,17},{17,9},{25,1},{2,26},{10... | collective-permute-start | bytes 344072 | tf_op jit(solution)/shard_map/ppermute | solution.py:316
  19.8 0.5 %collective-permute-start.7 = (bf16[64,896]{1,0:T(8,128)(2,1)S(1)}, bf16[64,896]{1,0:T(8,128)(2,1)S(1)}, u32[]{:S(2)}, u32[]{:S(2)}) collective-permute-start(bf16[64,896]{1,0:T(8,128)(2,1)S(1)} %get-tuple-element.41), channel_id=1, source_target_pairs={{0,16},{8,24},{16,0},{24,8},{1,17},{9,25},{17,1},{25,9},{2,18},{10... | collective-permute-start | bytes 344072 | tf_op jit(solution)/shard_map/ppermute | solution.py:316
  20.3 0.5 %collective-permute-start.8 = (bf16[64,896]{1,0:T(8,128)(2,1)S(1)}, bf16[64,896]{1,0:T(8,128)(2,1)S(1)}, u32[]{:S(2)}, u32[]{:S(2)}) collective-permute-start(bf16[64,896]{1,0:T(8,128)(2,1)S(1)} %get-tuple-element.42), channel_id=1, source_target_pairs={{0,8},{8,0},{16,24},{24,16},{1,9},{9,1},{17,25},{25,17},{2,10},{10... | collective-permute-start | bytes 344072 | tf_op jit(solution)/shard_map/ppermute | solution.py:316
  20.8 2.0 %shard_map.139 = (bf16[4,16,1920]{2,1,0:T(8,128)(2,1)S(1)}, bf16[1,16,1920]{2,1,0:T(8,128)(2,1)S(1)}, bf16[3,16,1920]{2,1,0:T(8,128)(2,1)S(1)}, bf16[64,896]{1,0:T(8,128)(2,1)S(1)}) custom-call(bf16[4,16,3712]{2,1,0:T(8,128)(2,1)S(1)} %get-tuple-element.33.refs_0_, bf16[4,16,3712]{2,1,0:T(8,128)(2,1)S(1)} %collective-permute-done.3.refs_1_, ...), custom_call_target="tpu_custom_call" | custom-call | bytes 40000000 | tf_op jit(solution)/shard_map/pallas_call | solution.py:38
  22.8 0.1 collective-permute-start.4
  22.9 0.9 %collective-permute-done.6.refs_1_ = bf16[64,896]{1,0:T(8,128)(2,1)S(1)} collective-permute-done((bf16[64,896]{1,0:T(8,128)(2,1)S(1)}, bf16[64,896]{1,0:T(8,128)(2,1)S(1)}, u32[]{:S(2)}, u32[]{:S(2)}) %collective-permute-start.6) | collective-permute-done | bytes 114720 | tf_op jit(solution)/shard_map/ppermute | solution.py:316
  23.8 2.4 %collective-permute-done.7.refs_2_ = bf16[64,896]{1,0:T(8,128)(2,1)S(1)} collective-permute-done((bf16[64,896]{1,0:T(8,128)(2,1)S(1)}, bf16[64,896]{1,0:T(8,128)(2,1)S(1)}, u32[]{:S(2)}, u32[]{:S(2)}) %collective-permute-start.7) | collective-permute-done | bytes 114720 | tf_op jit(solution)/shard_map/ppermute | solution.py:316
  26.2 0.1 collective-permute-done.8.refs_3_
  26.3 0.1 collective-permute-start.9
  26.4 0.5 %collective-permute-start.5 = (bf16[3,16,1920]{2,1,0:T(8,128)(2,1)S(1)}, bf16[3,16,1920]{2,1,0:T(8,128)(2,1)S(1)}, u32[]{:S(2)}, u32[]{:S(2)}) collective-permute-start(bf16[3,16,1920]{2,1,0:T(8,128)(2,1)S(1)} %get-tuple-element.38), channel_id=1, source_target_pairs={{0,1},{1,0},{2,3},{3,2},{4,5},{5,4},{6,7},{7,6},{8,9},{9,8},{10,11... | collective-permute-start | bytes 552968 | tf_op jit(solution)/shard_map/ppermute | solution.py:299
  26.9 1.6 %collective-permute-start.15 = (bf16[64,896]{1,0:T(8,128)(2,1)S(1)}, bf16[64,896]{1,0:T(8,128)(2,1)S(1)}, u32[]{:S(2)}, u32[]{:S(2)}) collective-permute-start(bf16[64,896]{1,0:T(8,128)(2,1)S(1)} %get-tuple-element.49.refs_1_), channel_id=1, source_target_pairs={{0,24},{8,16},{16,8},{24,0},{1,25},{9,17},{17,9},{25,1},{2,26},{10... | collective-permute-start | bytes 344072 | tf_op jit(solution)/shard_map/ppermute | solution.py:316
  28.5 1.3 %collective-permute-start.14 = (bf16[64,896]{1,0:T(8,128)(2,1)S(1)}, bf16[64,896]{1,0:T(8,128)(2,1)S(1)}, u32[]{:S(2)}, u32[]{:S(2)}) collective-permute-start(bf16[64,896]{1,0:T(8,128)(2,1)S(1)} %get-tuple-element.49.refs_1_), channel_id=1, source_target_pairs={{0,16},{8,24},{16,0},{24,8},{1,17},{9,25},{17,1},{25,9},{2,18},{10... | collective-permute-start | bytes 344072 | tf_op jit(solution)/shard_map/ppermute | solution.py:316
  29.9 0.5 %collective-permute-start.13 = (bf16[64,896]{1,0:T(8,128)(2,1)S(1)}, bf16[64,896]{1,0:T(8,128)(2,1)S(1)}, u32[]{:S(2)}, u32[]{:S(2)}) collective-permute-start(bf16[64,896]{1,0:T(8,128)(2,1)S(1)} %get-tuple-element.49.refs_1_), channel_id=1, source_target_pairs={{0,8},{8,0},{16,24},{24,16},{1,9},{9,1},{17,25},{25,17},{2,10},{10... | collective-permute-start | bytes 344072 | tf_op jit(solution)/shard_map/ppermute | solution.py:316
  30.4 0.1 shard_map.141
  30.5 2.5 %collective-permute-start.10 = (bf16[16,1920]{1,0:T(8,128)(2,1)S(1)}, bf16[16,1920]{1,0:T(8,128)(2,1)S(1)}, u32[]{:S(2)}, u32[]{:S(2)}) collective-permute-start(bf16[16,1920]{1,0:T(8,128)(2,1)S(1)} %get-tuple-element.44), channel_id=1, source_target_pairs={{0,6},{1,7},{2,4},{3,5},{4,2},{5,3},{6,0},{7,1},{8,14},{9,15},{10,... | collective-permute-start | bytes 184328 | tf_op jit(solution)/shard_map/ppermute | solution.py:299
  33.0 1.6 %collective-permute-start.11 = (bf16[16,1920]{1,0:T(8,128)(2,1)S(1)}, bf16[16,1920]{1,0:T(8,128)(2,1)S(1)}, u32[]{:S(2)}, u32[]{:S(2)}) collective-permute-start(bf16[16,1920]{1,0:T(8,128)(2,1)S(1)} %get-tuple-element.45), channel_id=1, source_target_pairs={{0,4},{1,5},{2,6},{3,7},{4,0},{5,1},{6,2},{7,3},{8,12},{9,13},{10,... | collective-permute-start | bytes 184328 | tf_op jit(solution)/shard_map/ppermute | solution.py:299
  34.6 1.3 %collective-permute-start.12 = (bf16[16,1920]{1,0:T(8,128)(2,1)S(1)}, bf16[16,1920]{1,0:T(8,128)(2,1)S(1)}, u32[]{:S(2)}, u32[]{:S(2)}) collective-permute-start(bf16[16,1920]{1,0:T(8,128)(2,1)S(1)} %get-tuple-element.46), channel_id=1, source_target_pairs={{0,2},{1,3},{2,0},{3,1},{4,6},{5,7},{6,4},{7,5},{8,10},{9,11},{10,... | collective-permute-start | bytes 184328 | tf_op jit(solution)/shard_map/ppermute | solution.py:299
  35.9 1.8 %shard_map.143 = (bf16[1,896,256]{2,1,0:T(8,128)(2,1)}, bf16[1,896,256]{2,1,0:T(8,128)(2,1)}, bf16[1,256,896]{2,1,0:T(8,128)(2,1)}, f32[1,256]{1,0:T(1,128)}) custom-call(f32[1,256]{1,0:T(1,128)S(1)} %bitcast.21, bf16[64,896]{1,0:T(8,128)(2,1)S(1)} %get-tuple-element.49.refs_1_, bf16[64,896]{1,0:T(8,128)(2,1)S(1)} %collective-permute-done.13.refs_2_, ...), custom_call_target="tpu_custom_call" | custom-call | bytes 1000 | tf_op jit(solution)/shard_map/pallas_call | solution.py:38
  37.8 1.1 %collective-permute-done.11 = bf16[16,1920]{1,0:T(8,128)(2,1)S(1)} collective-permute-done((bf16[16,1920]{1,0:T(8,128)(2,1)S(1)}, bf16[16,1920]{1,0:T(8,128)(2,1)S(1)}, u32[]{:S(2)}, u32[]{:S(2)}) %collective-permute-start.11) | collective-permute-done | bytes 61472 | tf_op jit(solution)/shard_map/ppermute | solution.py:299
  38.8 0.6 %collective-permute-done.12 = bf16[16,1920]{1,0:T(8,128)(2,1)S(1)} collective-permute-done((bf16[16,1920]{1,0:T(8,128)(2,1)S(1)}, bf16[16,1920]{1,0:T(8,128)(2,1)S(1)}, u32[]{:S(2)}, u32[]{:S(2)}) %collective-permute-start.12) | collective-permute-done | bytes 61472 | tf_op jit(solution)/shard_map/ppermute | solution.py:299
  39.4 1.3 %shard_map.142 = (bf16[128,3584]{1,0:T(8,128)(2,1)}, f32[8,128]{1,0:T(8,128)}) custom-call(f32[8,128]{1,0:T(8,128)S(1)} %copy-done.6, s32[8,128]{1,0:T(8,128)S(1)} %bitcast.20, f32[1,1,16,1920]{3,2,1,0:T(8,128)S(1)} %bitcast.15, bf16[1,1,16,1920]{3,2,1,0:T(8,128)(2,1)S(1)} %bitcast.16, bf16[1,1,16,1920]{3,2,1,0:T(8,128)(2,1)S(1)} %bitcast.17, ...), custom_call_target="tpu_custom_call" | custom-call | bytes 1000 | tf_op jit(solution)/shard_map/pallas_call | solution.py:38
  (24 shorter events, 0.1 us)
Async XLA Ops:
  0.6 8.4 %copy-start = (bf16[1,3584,256]{2,1,0:T(8,128)(2,1)S(1)}, bf16[1,3584,256]{2,1,0:T(8,128)(2,1)}, u32[]{:S(2)}) copy-start(bf16[1,3584,256]{2,1,0:T(8,128)(2,1)} %param.13) | copy-start | bytes 5505028
  3.3 11.7 %collective-permute-start.2 = (bf16[1,16,3712]{2,1,0:T(8,128)(2,1)}, bf16[1,16,3712]{2,1,0:T(8,128)(2,1)S(1)}, u32[]{:S(2)}, u32[]{:S(2)}) collective-permute-start(bf16[1,16,3712]{2,1,0:T(8,128)(2,1)} %get-tuple-element.31.refs_0_), channel_id=1, source_target_pairs={{0,4},{1,5},{2,6},{3,7},{4,0},{5,1},{6,2},{7,3},{8,12},{9,13},{10,... | collective-permute-start | bytes 356360 | tf_op jit(solution)/shard_map/ppermute | solution.py:299
  7.4 7.6 %collective-permute-start.1 = (bf16[1,16,3712]{2,1,0:T(8,128)(2,1)}, bf16[1,16,3712]{2,1,0:T(8,128)(2,1)S(1)}, u32[]{:S(2)}, u32[]{:S(2)}) collective-permute-start(bf16[1,16,3712]{2,1,0:T(8,128)(2,1)} %get-tuple-element.31.refs_0_), channel_id=1, source_target_pairs={{0,2},{1,3},{2,0},{3,1},{4,6},{5,7},{6,4},{7,5},{8,10},{9,11},{10,... | collective-permute-start | bytes 356360 | tf_op jit(solution)/shard_map/ppermute | solution.py:299
  9.0 8.1 %collective-permute-start = (bf16[1,16,3712]{2,1,0:T(8,128)(2,1)}, bf16[1,16,3712]{2,1,0:T(8,128)(2,1)S(1)}, u32[]{:S(2)}, u32[]{:S(2)}) collective-permute-start(bf16[1,16,3712]{2,1,0:T(8,128)(2,1)} %get-tuple-element.31.refs_0_), channel_id=1, source_target_pairs={{0,6},{1,7},{2,4},{3,5},{4,2},{5,3},{6,0},{7,1},{8,14},{9,15},{10,... | collective-permute-start | bytes 356360 | tf_op jit(solution)/shard_map/ppermute | solution.py:299
  9.0 1.5 %copy-start.1 = (bf16[1,3584,256]{2,1,0:T(8,128)(2,1)S(1)}, bf16[1,3584,256]{2,1,0:T(8,128)(2,1)}, u32[]{:S(2)}) copy-start(bf16[1,3584,256]{2,1,0:T(8,128)(2,1)} %param.14) | copy-start | bytes 5505028
  10.5 1.5 %copy-start.2 = (bf16[1,256,3584]{2,1,0:T(8,128)(2,1)S(1)}, bf16[1,256,3584]{2,1,0:T(8,128)(2,1)}, u32[]{:S(2)}) copy-start(bf16[1,256,3584]{2,1,0:T(8,128)(2,1)} %param.15) | copy-start | bytes 5505028
  12.0 0.7 %copy-start.5 = (f32[8,128]{1,0:T(8,128)S(1)}, f32[8,128]{1,0:T(8,128)}, u32[]{:S(2)}) copy-start(f32[8,128]{1,0:T(8,128)} %get-tuple-element.30.refs_3_.refs_0_) | copy-start | bytes 12292
  12.7 4.4 %copy-start.3 = (bf16[1,16,3712]{2,1,0:T(8,128)(2,1)S(1)}, bf16[1,16,3712]{2,1,0:T(8,128)(2,1)}, u32[]{:S(2)}) copy-start(bf16[1,16,3712]{2,1,0:T(8,128)(2,1)} %get-tuple-element.31.refs_0_) | copy-start | bytes 356356
  17.2 3.6 %collective-permute-start.3 = (bf16[4,16,3712]{2,1,0:T(8,128)(2,1)S(1)}, bf16[4,16,3712]{2,1,0:T(8,128)(2,1)S(1)}, u32[]{:S(2)}, u32[]{:S(2)}) collective-permute-start(bf16[4,16,3712]{2,1,0:T(8,128)(2,1)S(1)} %get-tuple-element.33.refs_0_), channel_id=1, source_target_pairs={{0,1},{1,0},{2,3},{3,2},{4,5},{5,4},{6,7},{7,6},{8,9},{9,8},{10,11... | collective-permute-start | bytes 1425416 | tf_op jit(solution)/shard_map/ppermute | solution.py:299
  17.3 6.6 %collective-permute-start.6 = (bf16[64,896]{1,0:T(8,128)(2,1)S(1)}, bf16[64,896]{1,0:T(8,128)(2,1)S(1)}, u32[]{:S(2)}, u32[]{:S(2)}) collective-permute-start(bf16[64,896]{1,0:T(8,128)(2,1)S(1)} %get-tuple-element.40), channel_id=1, source_target_pairs={{0,24},{8,16},{16,8},{24,0},{1,25},{9,17},{17,9},{25,1},{2,26},{10... | collective-permute-start | bytes 344072 | tf_op jit(solution)/shard_map/ppermute | solution.py:316
  19.8 6.4 %collective-permute-start.7 = (bf16[64,896]{1,0:T(8,128)(2,1)S(1)}, bf16[64,896]{1,0:T(8,128)(2,1)S(1)}, u32[]{:S(2)}, u32[]{:S(2)}) collective-permute-start(bf16[64,896]{1,0:T(8,128)(2,1)S(1)} %get-tuple-element.41), channel_id=1, source_target_pairs={{0,16},{8,24},{16,0},{24,8},{1,17},{9,25},{17,1},{25,9},{2,18},{10... | collective-permute-start | bytes 344072 | tf_op jit(solution)/shard_map/ppermute | solution.py:316
  20.3 6.0 %collective-permute-start.8 = (bf16[64,896]{1,0:T(8,128)(2,1)S(1)}, bf16[64,896]{1,0:T(8,128)(2,1)S(1)}, u32[]{:S(2)}, u32[]{:S(2)}) collective-permute-start(bf16[64,896]{1,0:T(8,128)(2,1)S(1)} %get-tuple-element.42), channel_id=1, source_target_pairs={{0,8},{8,0},{16,24},{24,16},{1,9},{9,1},{17,25},{25,17},{2,10},{10... | collective-permute-start | bytes 344072 | tf_op jit(solution)/shard_map/ppermute | solution.py:316
  22.8 13.2 %copy-start.7 = (f32[256]{0:T(256)S(1)}, f32[256]{0:T(256)}, u32[]{:S(2)}) copy-start(f32[256]{0:T(256)} %param.16) | copy-start | bytes 3076
  22.8 16.6 %copy-start.4 = (s32[128,8]{0,1:T(8,128)S(1)}, s32[128,8]{0,1:T(8,128)}, u32[]{:S(2)}) copy-start(s32[128,8]{0,1:T(8,128)} %param.11) | copy-start | bytes 12292
  22.8 16.6 %copy-start.6 = (f32[8,128]{1,0:T(8,128)S(1)}, f32[8,128]{1,0:T(8,128)}, u32[]{:S(2)}) copy-start(f32[8,128]{1,0:T(8,128)} %get-tuple-element.30.refs_3_.refs_0_) | copy-start | bytes 12292
  22.8 3.5 %collective-permute-start.4 = (bf16[1,16,1920]{2,1,0:T(8,128)(2,1)S(1)}, bf16[1,16,1920]{2,1,0:T(8,128)(2,1)S(1)}, u32[]{:S(2)}, u32[]{:S(2)}) collective-permute-start(bf16[1,16,1920]{2,1,0:T(8,128)(2,1)S(1)} %get-tuple-element.37), channel_id=1, source_target_pairs={{0,1},{1,0},{2,3},{3,2},{4,5},{5,4},{6,7},{7,6},{8,9},{9,8},{10,11... | collective-permute-start | bytes 184328 | tf_op jit(solution)/shard_map/ppermute | solution.py:299
  26.3 4.1 %collective-permute-start.9 = (bf16[4,64,896]{2,1,0:T(8,128)(2,1)S(1)}, bf16[4,64,896]{2,1,0:T(8,128)(2,1)S(1)}, u32[]{:S(2)}, u32[]{:S(2)}) collective-permute-start(bf16[4,64,896]{2,1,0:T(8,128)(2,1)S(1)} %shard_map.140.refs_5_), channel_id=1, source_target_pairs={{0,1},{1,0},{2,3},{3,2},{4,5},{5,4},{6,7},{7,6},{8,9},{9,8},{10,11... | collective-permute-start | bytes 1376264 | tf_op jit(solution)/shard_map/ppermute | solution.py:299
  26.4 4.0 %collective-permute-start.5 = (bf16[3,16,1920]{2,1,0:T(8,128)(2,1)S(1)}, bf16[3,16,1920]{2,1,0:T(8,128)(2,1)S(1)}, u32[]{:S(2)}, u32[]{:S(2)}) collective-permute-start(bf16[3,16,1920]{2,1,0:T(8,128)(2,1)S(1)} %get-tuple-element.38), channel_id=1, source_target_pairs={{0,1},{1,0},{2,3},{3,2},{4,5},{5,4},{6,7},{7,6},{8,9},{9,8},{10,11... | collective-permute-start | bytes 552968 | tf_op jit(solution)/shard_map/ppermute | solution.py:299
  26.9 7.7 %collective-permute-start.15 = (bf16[64,896]{1,0:T(8,128)(2,1)S(1)}, bf16[64,896]{1,0:T(8,128)(2,1)S(1)}, u32[]{:S(2)}, u32[]{:S(2)}) collective-permute-start(bf16[64,896]{1,0:T(8,128)(2,1)S(1)} %get-tuple-element.49.refs_1_), channel_id=1, source_target_pairs={{0,24},{8,16},{16,8},{24,0},{1,25},{9,17},{17,9},{25,1},{2,26},{10... | collective-permute-start | bytes 344072 | tf_op jit(solution)/shard_map/ppermute | solution.py:316
  28.5 7.4 %collective-permute-start.14 = (bf16[64,896]{1,0:T(8,128)(2,1)S(1)}, bf16[64,896]{1,0:T(8,128)(2,1)S(1)}, u32[]{:S(2)}, u32[]{:S(2)}) collective-permute-start(bf16[64,896]{1,0:T(8,128)(2,1)S(1)} %get-tuple-element.49.refs_1_), channel_id=1, source_target_pairs={{0,16},{8,24},{16,0},{24,8},{1,17},{9,25},{17,1},{25,9},{2,18},{10... | collective-permute-start | bytes 344072 | tf_op jit(solution)/shard_map/ppermute | solution.py:316
  29.9 6.1 %collective-permute-start.13 = (bf16[64,896]{1,0:T(8,128)(2,1)S(1)}, bf16[64,896]{1,0:T(8,128)(2,1)S(1)}, u32[]{:S(2)}, u32[]{:S(2)}) collective-permute-start(bf16[64,896]{1,0:T(8,128)(2,1)S(1)} %get-tuple-element.49.refs_1_), channel_id=1, source_target_pairs={{0,8},{8,0},{16,24},{24,16},{1,9},{9,1},{17,25},{25,17},{2,10},{10... | collective-permute-start | bytes 344072 | tf_op jit(solution)/shard_map/ppermute | solution.py:316
  30.5 7.3 %collective-permute-start.10 = (bf16[16,1920]{1,0:T(8,128)(2,1)S(1)}, bf16[16,1920]{1,0:T(8,128)(2,1)S(1)}, u32[]{:S(2)}, u32[]{:S(2)}) collective-permute-start(bf16[16,1920]{1,0:T(8,128)(2,1)S(1)} %get-tuple-element.44), channel_id=1, source_target_pairs={{0,6},{1,7},{2,4},{3,5},{4,2},{5,3},{6,0},{7,1},{8,14},{9,15},{10,... | collective-permute-start | bytes 184328 | tf_op jit(solution)/shard_map/ppermute | solution.py:299
  33.0 5.8 %collective-permute-start.11 = (bf16[16,1920]{1,0:T(8,128)(2,1)S(1)}, bf16[16,1920]{1,0:T(8,128)(2,1)S(1)}, u32[]{:S(2)}, u32[]{:S(2)}) collective-permute-start(bf16[16,1920]{1,0:T(8,128)(2,1)S(1)} %get-tuple-element.45), channel_id=1, source_target_pairs={{0,4},{1,5},{2,6},{3,7},{4,0},{5,1},{6,2},{7,3},{8,12},{9,13},{10,... | collective-permute-start | bytes 184328 | tf_op jit(solution)/shard_map/ppermute | solution.py:299
  34.6 4.8 %collective-permute-start.12 = (bf16[16,1920]{1,0:T(8,128)(2,1)S(1)}, bf16[16,1920]{1,0:T(8,128)(2,1)S(1)}, u32[]{:S(2)}, u32[]{:S(2)}) collective-permute-start(bf16[16,1920]{1,0:T(8,128)(2,1)S(1)} %get-tuple-element.46), channel_id=1, source_target_pairs={{0,2},{1,3},{2,0},{3,1},{4,6},{5,7},{6,4},{7,5},{8,10},{9,11},{10,... | collective-permute-start | bytes 184328 | tf_op jit(solution)/shard_map/ppermute | solution.py:299

commit v5 on v4

--- a/solution.py
+++ b/solution.py
@@ -97,28 +97,12 @@
         )
 
 
-def quarter_kernel(shift, count, *refs):
-    copies = lax.axis_size("dp")
-    pay_refs, out_refs, all_refs = refs[:count], refs[count : count + copies], refs[count + copies :]
-    quarter = out_refs[0].shape[1]
-    me = lax.axis_index("dp")
-    for step, out_ref in enumerate(out_refs):
-        start = pl.multiple_of(shift(me, step) * quarter, LANES)
-        at = 0
-        for ref in pay_refs:
-            for block in range(ref.shape[0]):
-                out_ref[at : at + BLOCK, :] = ref[block, :, pl.ds(start, quarter)]
-                at += BLOCK
-    for all_ref in all_refs:
-        at = 0
-        for ref in pay_refs:
-            all_ref[at : at + ref.shape[0]] = ref[...]
-            at += ref.shape[0]
-
-
-def stack_kernel(*refs):
-    for at, ref in enumerate(refs[:-1]):
-        refs[-1][at] = ref[...]
+def stack_kernel(kept, *refs):
+    at = 0
+    for ref in refs[:-1]:
+        value = ref[...] if kept is None else ref[:kept][None]
+        refs[-1][at : at + value.shape[0]] = value
+        at += value.shape[0]
 
 
 def turn_kernel(gate_ref, up_ref, down_ref, in_ref, down_turned_ref, in_turned_ref):
@@ -129,11 +113,15 @@
     down_turned_ref[...] = down_ref[...].T
 
 
-def expert_kernel(blocks, groups, *refs):
-    pay_refs, refs = refs[: -(len(groups) + 5)], refs[-(len(groups) + 5) :]
-    (in_ref, down_ref, turned_ref), back_refs, (grads_ref, rows_ref) = refs[:3], refs[3:-2], refs[-2:]
+def expert_kernel(blocks, groups, copies, shift, *refs):
+    count = 3 + len(groups) + copies + 2
+    pay_refs, refs = refs[:-count], refs[-count:]
+    (in_ref, down_ref, turned_ref), refs = refs[:3], refs[3:]
+    back_refs, share_refs = refs[: len(groups)], refs[len(groups) : -3]
+    own_rows_ref, grads_ref, rows_ref = refs[-3:]
     width, units = down_ref.shape
     half = width // 2
+    quarter = width // copies
     pays = [ref[...].reshape(-1, ref.shape[-1]) for ref in pay_refs]
     at = 0
     for pay in pays:
@@ -176,6 +164,13 @@
         for lanes in range(2):
             digits = jnp.where(line == 2 * place + lanes, value[lanes : lanes + 1], digits)
     grads_ref[:, 3 * units :] = digits.astype(BF16)
+    me = lax.axis_index("dp")
+    own_rows_ref[...] = rows_ref[:, pl.ds(pl.multiple_of(me * quarter, LANES), quarter)]
+    for step, ref in enumerate(share_refs, 1):
+        start = pl.multiple_of(shift(me, step) * quarter, LANES)
+        sent = ref.shape[0] - blocks * CAP
+        ref[:sent, :quarter] = rows_ref[:sent, pl.ds(start, quarter)]
+        ref[sent:, : grads_ref.shape[1]] = grads_ref[...]
     part_dx = dot(grad_in, turned_ref[...], 1, 0)
     part_dx = part_dx.reshape(blocks, CAP, width)
     dx = jnp.concatenate([part_dx[:, :, :half], part_dx[:, :, half:]], axis=1).astype(BF16)
@@ -231,13 +226,13 @@
 def weight_kernel(units, blocks, copies, bias_ref, *refs):
     given, (gate_ref, up_ref, down_ref, new_ref) = refs[:-4], refs[-4:]
     quarter = gate_ref.shape[1]
-    grads = [ref[...] for ref in given[:copies]]
-    rows = []
+    rows, grads = [given[0][...]], [given[1][...]]
+    for step, ref in enumerate(given[2 : 1 + copies]):
+        sent = ref.shape[0] - blocks * CAP
+        rows.append(ref[:sent, :quarter])
+        grads.append(ref[sent:, :])
+        rows += [other[step, :, :quarter] for other in given[1 + copies :]]
     load = jnp.zeros((2, LANES), F32)
-    for step in range(copies):
-        for ref in given[copies:]:
-            ref = ref if len(ref.shape) == 2 else ref.at[step]
-            rows.append(ref[...])
     rows = jnp.concatenate(rows, axis=0)
     hidden, scaled = [], []
     for value in grads:
@@ -300,7 +295,7 @@
 
     if flights == 1:
         near = [payload] + [swap(payload, step) for step in range(2, SPLIT, 2)]
-        groups = [4, 1, 3]
+        groups = [SPLIT // 2, SPLIT // 2]
     else:
         spread = jnp.broadcast_to(payload[:, None], (flights, SPLIT) + payload.shape[1:])
         spread = spread.reshape((sources,) + payload.shape[1:])
@@ -317,55 +312,55 @@
 
     rows = sources * BLOCK
     kept = groups[0] * BLOCK
-    got = [struct((groups[0],) + payload.shape[1:], BF16)] if flights == 1 else []
-    sent = call(
-        functools.partial(quarter_kernel, shift, len(near)),
-        [struct((kept, quarter), BF16)] * copies + got,
-        near,
-        1000,
-        after=[weights[2]],
-        order=[0, 3, 1, 2] if flights == 1 else None,
-    )
-    got = [sent[-1], swap(sent[-1], 1)] if flights == 1 else near
-    rows_in = [sent[0]] + [across(sent[step], step) for step in range(1, copies)]
-
-    *back, grads = call(
-        functools.partial(expert_kernel, sources, groups),
+    got = near
+    if flights == 1:
+        (near,) = call(
+            functools.partial(stack_kernel, None),
+            [struct((groups[0],) + payload.shape[1:], BF16)],
+            near,
+            1000,
+            after=[weights[2]],
+            order=[0, 3, 1, 2],
+        )
+        got = [near, swap(near, 1)]
+
+    wide = max(quarter, 3 * units + LANES)
+    outs = call(
+        functools.partial(expert_kernel, sources, groups, copies, shift),
         [struct((group, BLOCK, half + LANES), BF16) for group in groups]
-        + [struct((sources * CAP, 3 * units + LANES), BF16)],
+        + [struct((kept + sources * CAP, wide), BF16)] * (copies - 1)
+        + [struct((rows, quarter), BF16), struct((sources * CAP, 3 * units + LANES), BF16)],
         [*got, *weights],
         4 * 10**7,
         [pltpu.VMEM((rows, width), BF16)],
         limit=18,
     )
-    grads = [grads] + [across(grads, step) for step in range(1, copies)]
+    back, shares, own = outs[: len(groups)], outs[len(groups) : -2], outs[-2:]
+    shares = [across(value, step) for step, value in enumerate(shares, 1)]
 
     if flights == 1:
         other = [swap(value, 1) for value in back[1:]]
-        rows_in = call(
-            stack_kernel,
-            [struct((copies,) + rows_in[0].shape, BF16)],
-            rows_in,
-            1000,
-            after=[other[0]],
-            order=[0, *range(copies - 1, 0, -1)],
-        )
-        rows_in = [rows_in[0], swap(rows_in[0], 1)]
         block = (BLOCK, half + LANES)
         sums = call(
             pair_kernel,
             [struct(block, F32)] + [struct(block, BF16)] * 3,
             [back[0], *other],
             1000,
-            after=[rows_in[1]],
         )
         parts = [sums[0]] + [swap(sums[at], 2 * at) for at in range(1, 4)]
         parts = [part.reshape((1, 1) + block) for part in parts]
+        (rows_in,) = call(
+            functools.partial(stack_kernel, kept),
+            [struct((copies - 1, kept, wide), BF16)],
+            shares,
+            1000,
+            after=parts[1:],
+            order=[*range(copies - 2, -1, -1)],
+        )
+        shares = [*shares, swap(rows_in, 1)]
     else:
         parts = lax.all_to_all(back[0], "expert", split_axis=0, concat_axis=0, tiled=True)
         parts = [parts.reshape(flights, SPLIT, BLOCK, half + LANES)]
-        rows_in = [jnp.stack(rows_in)]
-
     grad_gate, grad_up, grad_down, new_bias = call(
         functools.partial(weight_kernel, units, sources, copies),
         [
@@ -374,7 +369,7 @@
             struct((1, units, quarter), BF16),
             struct((1, EXPERTS_ALL), F32),
         ],
-        [router_bias[None], *grads, *rows_in],
+        [router_bias[None], *own, *shares],
         1000,
     )
     token_grad, gate_grad = call(

time: 41 us -> 39.5 us (0.963)
  starting transfers between devices: 18.9 us -> 15.9 us
  waiting for transfers between devices: 7.77 us -> 8.89 us
    ppermute x6 -> x3, starting transfers between devices: 7.04 us -> 3.5 us  [across(): lax.ppermute(values, 'dp', [(i, shift(i, step)) for i in range(copies)])]
    ppermute x6 -> x3, waiting for transfers between devices: 3.39 us -> 4.09 us  [across(): lax.ppermute(values, 'dp', [(i, shift(i, step)) for i in range(copies)])]
    ppermute x10 -> x9, starting transfers between devices: 11.9 us -> 12.4 us  [swap(): lax.ppermute(values, 'expert', [(i, i ^ step) for i in range(sources)])]
    ppermute x10 -> x9, waiting for transfers between devices: 4.38 us -> 4.8 us  [swap(): lax.ppermute(values, 'expert', [(i, i ^ step) for i in range(sources)])]
  transfers between devices with their start and end apart: 16 -> 12, of which waited for: 7 -> 6; matrix products, arithmetic and copies ran while one was open for 0% -> 0% of each run, Pallas kernels for 14% -> 8%
where the time goes in v5:
time: 39.5 us; the launch traced here: 38.9 us
  starting transfers between devices  15.9 us (40%)
  Pallas kernels  9.64 us (24%)
  waiting for transfers between devices  8.89 us (23%)
  local copies, waits for them, and re-layouts  3.71 us (9%)
  between operations  0.75 us (2%)
    ppermute x9, starting transfers between devices, swap(): lax.ppermute(values, 'expert', [(i, i ^ step) for i in range(sources)])  12.4 us
    pallas_call x8, Pallas kernels, call(): pl.pallas_call(kernel, out_shape=outs, in_specs=[pl.BlockSpec(memory_spac...  9.64 us
    ppermute x9, waiting for transfers between devices, swap(): lax.ppermute(values, 'expert', [(i, i ^ step) for i in range(sources)])  4.8 us
    ppermute x3, waiting for transfers between devices, across(): lax.ppermute(values, 'dp', [(i, shift(i, step)) for i in range(copies)])  4.09 us
    unnamed x16, local copies, waits for them, and re-layouts  3.71 us
    ppermute x3, starting transfers between devices, across(): lax.ppermute(values, 'dp', [(i, shift(i, step)) for i in range(copies)])  3.5 us
  transfers between devices with their start and end apart: 12, of which 6 were waited for; matrix products, arithmetic and copies ran while one was open for 0% of the time, Pallas kernels for 8%

profile of v5, /device:TPU:0, one launch (start us, length us, event | category | flops | bytes accessed | tf_op | source)
XLA Modules:
  0.0 38.9 jit_solution(2868150868951064696)
XLA Ops:
  0.6 2.7 %shard_map.136 = (bf16[1,16,3712]{2,1,0:T(8,128)(2,1)}, f32[8,128]{1,0:T(8,128)}) custom-call(bf16[128,3584]{1,0:T(8,128)(2,1)} %refs_0_.1, bf16[128,3584]{1,0:T(8,128)(2,1)} %refs_1_.1, s32[8,128]{1,0:T(8,128)} %bitcast.22, s32[8,128]{1,0:T(8,128)} %bitcast.25, s32[1,256]{1,0:T(1,128)} %refs_4_.1), custom_call_target="tpu_custom_call" | custom-call | bytes 1835008 | tf_op jit(solution)/shard_map/pallas_call | solution.py:38
  3.3 4.1 %collective-permute-start.2 = (bf16[1,16,3712]{2,1,0:T(8,128)(2,1)}, bf16[1,16,3712]{2,1,0:T(8,128)(2,1)S(1)}, u32[]{:S(2)}, u32[]{:S(2)}) collective-permute-start(bf16[1,16,3712]{2,1,0:T(8,128)(2,1)} %get-tuple-element.29.refs_0_), channel_id=1, source_target_pairs={{0,4},{1,5},{2,6},{3,7},{4,0},{5,1},{6,2},{7,3},{8,12},{9,13},{10,... | collective-permute-start | bytes 356360 | tf_op jit(solution)/shard_map/ppermute | solution.py:294
  7.4 1.6 %collective-permute-start.1 = (bf16[1,16,3712]{2,1,0:T(8,128)(2,1)}, bf16[1,16,3712]{2,1,0:T(8,128)(2,1)S(1)}, u32[]{:S(2)}, u32[]{:S(2)}) collective-permute-start(bf16[1,16,3712]{2,1,0:T(8,128)(2,1)} %get-tuple-element.29.refs_0_), channel_id=1, source_target_pairs={{0,2},{1,3},{2,0},{3,1},{4,6},{5,7},{6,4},{7,5},{8,10},{9,11},{10,... | collective-permute-start | bytes 356360 | tf_op jit(solution)/shard_map/ppermute | solution.py:294
  9.0 0.0 collective-permute-start
  9.0 1.5 %copy-done.1 = bf16[1,3584,256]{2,1,0:T(8,128)(2,1)S(1)} copy-done((bf16[1,3584,256]{2,1,0:T(8,128)(2,1)S(1)}, bf16[1,3584,256]{2,1,0:T(8,128)(2,1)}, u32[]{:S(2)}) %copy-start.1) | copy-done | bytes 1835032
  10.5 1.5 %copy-done.2 = bf16[1,256,3584]{2,1,0:T(8,128)(2,1)S(1)} copy-done((bf16[1,256,3584]{2,1,0:T(8,128)(2,1)S(1)}, bf16[1,256,3584]{2,1,0:T(8,128)(2,1)}, u32[]{:S(2)}) %copy-start.2) | copy-done | bytes 1835032
  12.0 0.7 %copy-done.5 = f32[8,128]{1,0:T(8,128)S(1)} copy-done((f32[8,128]{1,0:T(8,128)S(1)}, f32[8,128]{1,0:T(8,128)}, u32[]{:S(2)}) %copy-start.5) | copy-done | bytes 4120
  12.7 1.7 %shard_map.137 = (bf16[3584,512]{1,0:T(8,128)(2,1)S(1)}, bf16[3584,256]{1,0:T(8,128)(2,1)S(1)}, bf16[512,3584]{1,0:T(8,128)(2,1)S(1)}) custom-call(bf16[3584,256]{1,0:T(8,128)(2,1)S(1)} %bitcast.12, bf16[3584,256]{1,0:T(8,128)(2,1)S(1)} %bitcast.13, bf16[256,3584]{1,0:T(8,128)(2,1)S(1)} %bitcast.14, f32[8,128]{1,0:T(8,128)S(1)} %copy-done.5), custom_call_target="tpu_custom_call" | custom-call | bytes 40000000 | tf_op jit(solution)/shard_map/pallas_call | solution.py:38
  14.4 0.6 %collective-permute-done.2.refs_3_ = bf16[1,16,3712]{2,1,0:T(8,128)(2,1)S(1)} collective-permute-done((bf16[1,16,3712]{2,1,0:T(8,128)(2,1)}, bf16[1,16,3712]{2,1,0:T(8,128)(2,1)S(1)}, u32[]{:S(2)}, u32[]{:S(2)}) %collective-permute-start.2) | collective-permute-done | bytes 118816 | tf_op jit(solution)/shard_map/ppermute | solution.py:294
  15.0 0.0 collective-permute-done.1.refs_2_
  15.0 2.1 %collective-permute-done.refs_1_ = bf16[1,16,3712]{2,1,0:T(8,128)(2,1)S(1)} collective-permute-done((bf16[1,16,3712]{2,1,0:T(8,128)(2,1)}, bf16[1,16,3712]{2,1,0:T(8,128)(2,1)S(1)}, u32[]{:S(2)}, u32[]{:S(2)}) %collective-permute-start) | collective-permute-done | bytes 118816 | tf_op jit(solution)/shard_map/ppermute | solution.py:294
  17.1 0.1 collective-permute-start.3
  17.2 1.8 %collective-permute-done.3.refs_1_ = bf16[4,16,3712]{2,1,0:T(8,128)(2,1)S(1)} collective-permute-done((bf16[4,16,3712]{2,1,0:T(8,128)(2,1)S(1)}, bf16[4,16,3712]{2,1,0:T(8,128)(2,1)S(1)}, u32[]{:S(2)}, u32[]{:S(2)}) %collective-permute-start.3) | collective-permute-done | bytes 475168 | tf_op jit(solution)/shard_map/ppermute | solution.py:294
  19.1 2.0 %shard_map.139 = (bf16[4,16,1920]{2,1,0:T(8,128)(2,1)S(1)}, bf16[4,16,1920]{2,1,0:T(8,128)(2,1)S(1)}, bf16[128,896]{1,0:T(8,128)(2,1)S(1)}, bf16[128,896]{1,0:T(...) custom-call(bf16[4,16,3712]{2,1,0:T(8,128)(2,1)S(1)} %shard_map.138.refs_0_, ...), custom_call_target="tpu_custom_call" | custom-call | bytes 40000000 | tf_op jit(solution)/shard_map/pallas_call | solution.py:38
  21.1 0.0 copy-start.7
  21.1 0.2 collective-permute-start.4
  21.3 1.5 %collective-permute-start.8 = (bf16[128,896]{1,0:T(8,128)(2,1)S(1)}, bf16[128,896]{1,0:T(8,128)(2,1)S(1)}, u32[]{:S(2)}, u32[]{:S(2)}) collective-permute-start(bf16[128,896]{1,0:T(8,128)(2,1)S(1)} %get-tuple-element.43), channel_id=1, source_target_pairs={{0,8},{8,0},{16,24},{24,16},{1,9},{9,1},{17,25},{25,17},{2,10},{10... | collective-permute-start | bytes 688136 | tf_op jit(solution)/shard_map/ppermute | solution.py:311
  22.8 1.6 %collective-permute-start.9 = (bf16[128,896]{1,0:T(8,128)(2,1)S(1)}, bf16[128,896]{1,0:T(8,128)(2,1)S(1)}, u32[]{:S(2)}, u32[]{:S(2)}) collective-permute-start(bf16[128,896]{1,0:T(8,128)(2,1)S(1)} %get-tuple-element.44), channel_id=1, source_target_pairs={{0,16},{8,24},{16,0},{24,8},{1,17},{9,25},{17,1},{25,9},{2,18},{10... | collective-permute-start | bytes 688136 | tf_op jit(solution)/shard_map/ppermute | solution.py:311
  24.4 0.4 %collective-permute-start.10 = (bf16[128,896]{1,0:T(8,128)(2,1)S(1)}, bf16[128,896]{1,0:T(8,128)(2,1)S(1)}, u32[]{:S(2)}, u32[]{:S(2)}) collective-permute-start(bf16[128,896]{1,0:T(8,128)(2,1)S(1)} %get-tuple-element.45), channel_id=1, source_target_pairs={{0,24},{8,16},{16,8},{24,0},{1,25},{9,17},{17,9},{25,1},{2,26},{10... | collective-permute-start | bytes 688136 | tf_op jit(solution)/shard_map/ppermute | solution.py:311
  24.8 0.0 collective-permute-done.4.refs_1_
  24.8 0.1 shard_map.140
  24.8 2.6 %collective-permute-start.5 = (bf16[16,1920]{1,0:T(8,128)(2,1)S(1)}, bf16[16,1920]{1,0:T(8,128)(2,1)S(1)}, u32[]{:S(2)}, u32[]{:S(2)}) collective-permute-start(bf16[16,1920]{1,0:T(8,128)(2,1)S(1)} %get-tuple-element.36), channel_id=1, source_target_pairs={{0,6},{1,7},{2,4},{3,5},{4,2},{5,3},{6,0},{7,1},{8,14},{9,15},{10,... | collective-permute-start | bytes 184328 | tf_op jit(solution)/shard_map/ppermute | solution.py:294
  27.4 1.6 %collective-permute-start.6 = (bf16[16,1920]{1,0:T(8,128)(2,1)S(1)}, bf16[16,1920]{1,0:T(8,128)(2,1)S(1)}, u32[]{:S(2)}, u32[]{:S(2)}) collective-permute-start(bf16[16,1920]{1,0:T(8,128)(2,1)S(1)} %get-tuple-element.37), channel_id=1, source_target_pairs={{0,4},{1,5},{2,6},{3,7},{4,0},{5,1},{6,2},{7,3},{8,12},{9,13},{10,... | collective-permute-start | bytes 184328 | tf_op jit(solution)/shard_map/ppermute | solution.py:294
  29.0 0.7 %collective-permute-done.8.refs_2_.refs_3_ = bf16[128,896]{1,0:T(8,128)(2,1)S(1)} collective-permute-done((bf16[128,896]{1,0:T(8,128)(2,1)S(1)}, bf16[128,896]{1,0:T(8,128)(2,1)S(1)}, u32[]{:S(2)}, u32[]{:S(2)}) %collective-permute-start.8) | collective-permute-done | bytes 229408 | tf_op jit(solution)/shard_map/ppermute | solution.py:311
  29.7 2.2 %collective-permute-start.7 = (bf16[16,1920]{1,0:T(8,128)(2,1)S(1)}, bf16[16,1920]{1,0:T(8,128)(2,1)S(1)}, u32[]{:S(2)}, u32[]{:S(2)}) collective-permute-start(bf16[16,1920]{1,0:T(8,128)(2,1)S(1)} %get-tuple-element.38), channel_id=1, source_target_pairs={{0,2},{1,3},{2,0},{3,1},{4,6},{5,7},{6,4},{7,5},{8,10},{9,11},{10,... | collective-permute-start | bytes 184328 | tf_op jit(solution)/shard_map/ppermute | solution.py:294
  31.9 3.4 %collective-permute-done.9.refs_1_.refs_4_ = bf16[128,896]{1,0:T(8,128)(2,1)S(1)} collective-permute-done((bf16[128,896]{1,0:T(8,128)(2,1)S(1)}, bf16[128,896]{1,0:T(8,128)(2,1)S(1)}, u32[]{:S(2)}, u32[]{:S(2)}) %collective-permute-start.9) | collective-permute-done | bytes 229408 | tf_op jit(solution)/shard_map/ppermute | solution.py:311
  35.3 0.0 collective-permute-done.10.refs_0_.refs_5_
  35.3 0.0 collective-permute-done.5
  35.4 0.1 collective-permute-start.11
  35.5 1.4 %shard_map.141 = (bf16[128,3584]{1,0:T(8,128)(2,1)}, f32[8,128]{1,0:T(8,128)}) custom-call(f32[8,128]{1,0:T(8,128)S(1)} %copy-done.6, s32[8,128]{1,0:T(8,128)S(1)} %bitcast.23, f32[1,1,16,1920]{3,2,1,0:T(8,128)S(1)} %bitcast.21, bf16[1,1,16,1920]{3,2,1,0:T(8,128)(2,1)S(1)} %bitcast.16, bf16[1,1,16,1920]{3,2,1,0:T(8,128)(2,1)S(1)} %bitcast.18, ...), custom_call_target="tpu_custom_call" | custom-call | bytes 1000 | tf_op jit(solution)/shard_map/pallas_call | solution.py:38
  36.8 0.3 collective-permute-done.11.refs_6_
  37.1 1.8 %shard_map.143 = (bf16[1,896,256]{2,1,0:T(8,128)(2,1)}, bf16[1,896,256]{2,1,0:T(8,128)(2,1)}, bf16[1,256,896]{2,1,0:T(8,128)(2,1)}, f32[1,256]{1,0:T(1,128)}) custom-call(f32[1,256]{1,0:T(1,128)S(1)} %bitcast.24, bf16[128,896]{1,0:T(8,128)(2,1)S(1)} %get-tuple-element.41.refs_1_, bf16[64,896]{1,0:T(8,128)(2,1)S(1)} %get-tuple-element.42.refs_2_, ...), custom_call_target="tpu_custom_call" | custom-call | bytes 1000 | tf_op jit(solution)/shard_map/pallas_call | solution.py:38
  (16 shorter events, 0.1 us)
Async XLA Ops:
  0.6 8.4 %copy-start = (bf16[1,3584,256]{2,1,0:T(8,128)(2,1)S(1)}, bf16[1,3584,256]{2,1,0:T(8,128)(2,1)}, u32[]{:S(2)}) copy-start(bf16[1,3584,256]{2,1,0:T(8,128)(2,1)} %param.13) | copy-start | bytes 5505028
  3.3 11.7 %collective-permute-start.2 = (bf16[1,16,3712]{2,1,0:T(8,128)(2,1)}, bf16[1,16,3712]{2,1,0:T(8,128)(2,1)S(1)}, u32[]{:S(2)}, u32[]{:S(2)}) collective-permute-start(bf16[1,16,3712]{2,1,0:T(8,128)(2,1)} %get-tuple-element.29.refs_0_), channel_id=1, source_target_pairs={{0,4},{1,5},{2,6},{3,7},{4,0},{5,1},{6,2},{7,3},{8,12},{9,13},{10,... | collective-permute-start | bytes 356360 | tf_op jit(solution)/shard_map/ppermute | solution.py:294
  7.4 7.6 %collective-permute-start.1 = (bf16[1,16,3712]{2,1,0:T(8,128)(2,1)}, bf16[1,16,3712]{2,1,0:T(8,128)(2,1)S(1)}, u32[]{:S(2)}, u32[]{:S(2)}) collective-permute-start(bf16[1,16,3712]{2,1,0:T(8,128)(2,1)} %get-tuple-element.29.refs_0_), channel_id=1, source_target_pairs={{0,2},{1,3},{2,0},{3,1},{4,6},{5,7},{6,4},{7,5},{8,10},{9,11},{10,... | collective-permute-start | bytes 356360 | tf_op jit(solution)/shard_map/ppermute | solution.py:294
  9.0 8.1 %collective-permute-start = (bf16[1,16,3712]{2,1,0:T(8,128)(2,1)}, bf16[1,16,3712]{2,1,0:T(8,128)(2,1)S(1)}, u32[]{:S(2)}, u32[]{:S(2)}) collective-permute-start(bf16[1,16,3712]{2,1,0:T(8,128)(2,1)} %get-tuple-element.29.refs_0_), channel_id=1, source_target_pairs={{0,6},{1,7},{2,4},{3,5},{4,2},{5,3},{6,0},{7,1},{8,14},{9,15},{10,... | collective-permute-start | bytes 356360 | tf_op jit(solution)/shard_map/ppermute | solution.py:294
  9.0 1.5 %copy-start.1 = (bf16[1,3584,256]{2,1,0:T(8,128)(2,1)S(1)}, bf16[1,3584,256]{2,1,0:T(8,128)(2,1)}, u32[]{:S(2)}) copy-start(bf16[1,3584,256]{2,1,0:T(8,128)(2,1)} %param.14) | copy-start | bytes 5505028
  10.5 1.5 %copy-start.2 = (bf16[1,256,3584]{2,1,0:T(8,128)(2,1)S(1)}, bf16[1,256,3584]{2,1,0:T(8,128)(2,1)}, u32[]{:S(2)}) copy-start(bf16[1,256,3584]{2,1,0:T(8,128)(2,1)} %param.15) | copy-start | bytes 5505028
  12.0 0.7 %copy-start.5 = (f32[8,128]{1,0:T(8,128)S(1)}, f32[8,128]{1,0:T(8,128)}, u32[]{:S(2)}) copy-start(f32[8,128]{1,0:T(8,128)} %get-tuple-element.28.refs_3_.refs_0_) | copy-start | bytes 12292
  12.7 4.4 %copy-start.3 = (bf16[1,16,3712]{2,1,0:T(8,128)(2,1)S(1)}, bf16[1,16,3712]{2,1,0:T(8,128)(2,1)}, u32[]{:S(2)}) copy-start(bf16[1,16,3712]{2,1,0:T(8,128)(2,1)} %get-tuple-element.29.refs_0_) | copy-start | bytes 356356
  17.1 1.9 %collective-permute-start.3 = (bf16[4,16,3712]{2,1,0:T(8,128)(2,1)S(1)}, bf16[4,16,3712]{2,1,0:T(8,128)(2,1)S(1)}, u32[]{:S(2)}, u32[]{:S(2)}) collective-permute-start(bf16[4,16,3712]{2,1,0:T(8,128)(2,1)S(1)} %shard_map.138.refs_0_), channel_id=1, source_target_pairs={{0,1},{1,0},{2,3},{3,2},{4,5},{5,4},{6,7},{7,6},{8,9},{9,8},{10,11... | collective-permute-start | bytes 1425416 | tf_op jit(solution)/shard_map/ppermute | solution.py:294
  19.0 16.4 %copy-start.4 = (s32[128,8]{0,1:T(8,128)S(1)}, s32[128,8]{0,1:T(8,128)}, u32[]{:S(2)}) copy-start(s32[128,8]{0,1:T(8,128)} %param.11) | copy-start | bytes 12292
  19.1 16.4 %copy-start.6 = (f32[8,128]{1,0:T(8,128)S(1)}, f32[8,128]{1,0:T(8,128)}, u32[]{:S(2)}) copy-start(f32[8,128]{1,0:T(8,128)} %get-tuple-element.28.refs_3_.refs_0_) | copy-start | bytes 12292
  21.1 16.0 %copy-start.7 = (f32[256]{0:T(256)S(1)}, f32[256]{0:T(256)}, u32[]{:S(2)}) copy-start(f32[256]{0:T(256)} %param.16) | copy-start | bytes 3076
  21.1 3.7 %collective-permute-start.4 = (bf16[4,16,1920]{2,1,0:T(8,128)(2,1)S(1)}, bf16[4,16,1920]{2,1,0:T(8,128)(2,1)S(1)}, u32[]{:S(2)}, u32[]{:S(2)}) collective-permute-start(bf16[4,16,1920]{2,1,0:T(8,128)(2,1)S(1)} %get-tuple-element.34), channel_id=1, source_target_pairs={{0,1},{1,0},{2,3},{3,2},{4,5},{5,4},{6,7},{7,6},{8,9},{9,8},{10,11... | collective-permute-start | bytes 737288 | tf_op jit(solution)/shard_map/ppermute | solution.py:294
  21.3 8.4 %collective-permute-start.8 = (bf16[128,896]{1,0:T(8,128)(2,1)S(1)}, bf16[128,896]{1,0:T(8,128)(2,1)S(1)}, u32[]{:S(2)}, u32[]{:S(2)}) collective-permute-start(bf16[128,896]{1,0:T(8,128)(2,1)S(1)} %get-tuple-element.43), channel_id=1, source_target_pairs={{0,8},{8,0},{16,24},{24,16},{1,9},{9,1},{17,25},{25,17},{2,10},{10... | collective-permute-start | bytes 688136 | tf_op jit(solution)/shard_map/ppermute | solution.py:311
  22.8 12.5 %collective-permute-start.9 = (bf16[128,896]{1,0:T(8,128)(2,1)S(1)}, bf16[128,896]{1,0:T(8,128)(2,1)S(1)}, u32[]{:S(2)}, u32[]{:S(2)}) collective-permute-start(bf16[128,896]{1,0:T(8,128)(2,1)S(1)} %get-tuple-element.44), channel_id=1, source_target_pairs={{0,16},{8,24},{16,0},{24,8},{1,17},{9,25},{17,1},{25,9},{2,18},{10... | collective-permute-start | bytes 688136 | tf_op jit(solution)/shard_map/ppermute | solution.py:311
  24.4 10.9 %collective-permute-start.10 = (bf16[128,896]{1,0:T(8,128)(2,1)S(1)}, bf16[128,896]{1,0:T(8,128)(2,1)S(1)}, u32[]{:S(2)}, u32[]{:S(2)}) collective-permute-start(bf16[128,896]{1,0:T(8,128)(2,1)S(1)} %get-tuple-element.45), channel_id=1, source_target_pairs={{0,24},{8,16},{16,8},{24,0},{1,25},{9,17},{17,9},{25,1},{2,26},{10... | collective-permute-start | bytes 688136 | tf_op jit(solution)/shard_map/ppermute | solution.py:311
  24.8 10.5 %collective-permute-start.5 = (bf16[16,1920]{1,0:T(8,128)(2,1)S(1)}, bf16[16,1920]{1,0:T(8,128)(2,1)S(1)}, u32[]{:S(2)}, u32[]{:S(2)}) collective-permute-start(bf16[16,1920]{1,0:T(8,128)(2,1)S(1)} %get-tuple-element.36), channel_id=1, source_target_pairs={{0,6},{1,7},{2,4},{3,5},{4,2},{5,3},{6,0},{7,1},{8,14},{9,15},{10,... | collective-permute-start | bytes 184328 | tf_op jit(solution)/shard_map/ppermute | solution.py:294
  27.4 7.9 %collective-permute-start.6 = (bf16[16,1920]{1,0:T(8,128)(2,1)S(1)}, bf16[16,1920]{1,0:T(8,128)(2,1)S(1)}, u32[]{:S(2)}, u32[]{:S(2)}) collective-permute-start(bf16[16,1920]{1,0:T(8,128)(2,1)S(1)} %get-tuple-element.37), channel_id=1, source_target_pairs={{0,4},{1,5},{2,6},{3,7},{4,0},{5,1},{6,2},{7,3},{8,12},{9,13},{10,... | collective-permute-start | bytes 184328 | tf_op jit(solution)/shard_map/ppermute | solution.py:294
  29.7 5.6 %collective-permute-start.7 = (bf16[16,1920]{1,0:T(8,128)(2,1)S(1)}, bf16[16,1920]{1,0:T(8,128)(2,1)S(1)}, u32[]{:S(2)}, u32[]{:S(2)}) collective-permute-start(bf16[16,1920]{1,0:T(8,128)(2,1)S(1)} %get-tuple-element.38), channel_id=1, source_target_pairs={{0,2},{1,3},{2,0},{3,1},{4,6},{5,7},{6,4},{7,5},{8,10},{9,11},{10,... | collective-permute-start | bytes 184328 | tf_op jit(solution)/shard_map/ppermute | solution.py:294
  35.4 1.7 %collective-permute-start.11 = (bf16[3,64,896]{2,1,0:T(8,128)(2,1)S(1)}, bf16[3,64,896]{2,1,0:T(8,128)(2,1)S(1)}, u32[]{:S(2)}, u32[]{:S(2)}) collective-permute-start(bf16[3,64,896]{2,1,0:T(8,128)(2,1)S(1)} %shard_map.142), channel_id=1, source_target_pairs={{0,1},{1,0},{2,3},{3,2},{4,5},{5,4},{6,7},{7,6},{8,9},{9,8},{10,11... | collective-permute-start | bytes 1032200 | tf_op jit(solution)/shard_map/ppermute | solution.py:294

commit v6 on v5

--- a/solution.py
+++ b/solution.py
@@ -294,7 +294,8 @@
         return lax.ppermute(values, "expert", [(i, i ^ step) for i in range(sources)])
 
     if flights == 1:
-        near = [payload] + [swap(payload, step) for step in range(2, SPLIT, 2)]
+        hops = [0, 4, 2, 6]
+        near = [payload] + [swap(payload, step) for step in hops[1:]]
         groups = [SPLIT // 2, SPLIT // 2]
     else:
         spread = jnp.broadcast_to(payload[:, None], (flights, SPLIT) + payload.shape[1:])
@@ -314,15 +315,17 @@
     kept = groups[0] * BLOCK
     got = near
     if flights == 1:
-        (near,) = call(
-            functools.partial(stack_kernel, None),
-            [struct((groups[0],) + payload.shape[1:], BF16)],
-            near,
-            1000,
-            after=[weights[2]],
-            order=[0, 3, 1, 2],
-        )
-        got = [near, swap(near, 1)]
+        got = []
+        for part, order, after in ((near[:2], None, ()), (near[2:], [1, 0], weights[2:])):
+            got += call(
+                functools.partial(stack_kernel, None),
+                [struct((len(part),) + payload.shape[1:], BF16)],
+                part,
+                1000,
+                after=after,
+                order=order,
+            )
+        got = got + [swap(value, 1) for value in got]
 
     wide = max(quarter, 3 * units + LANES)
     outs = call(
@@ -347,14 +350,14 @@
             [back[0], *other],
             1000,
         )
-        parts = [sums[0]] + [swap(sums[at], 2 * at) for at in range(1, 4)]
+        parts = [sums[0]] + [swap(sums[at], hops[at]) for at in range(1, 4)]
         parts = [part.reshape((1, 1) + block) for part in parts]
         (rows_in,) = call(
             functools.partial(stack_kernel, kept),
             [struct((copies - 1, kept, wide), BF16)],
             shares,
             1000,
-            after=parts[1:],
+            after=parts[:0:-1],
             order=[*range(copies - 2, -1, -1)],
         )
         shares = [*shares, swap(rows_in, 1)]
@@ -371,13 +374,14 @@
         ],
         [router_bias[None], *own, *shares],
         1000,
+        order=[0, 1, 2, 5, 3, 4, 6] if flights == 1 and copies == 4 else None,
     )
     token_grad, gate_grad = call(
         functools.partial(token_kernel, flights),
         [struct((row_count, width), BF16), struct((top_count, row_count), F32)],
         [pick, route.T] + parts,
         1000,
-        order=[0, 1, 2, 5, 4, 3] if flights == 1 else None,
+        order=[0, 1, 2, 5, 3, 4] if flights == 1 else None,
     )
     return (token_grad, gate_grad.T, grad_gate, grad_up, grad_down, new_bias[0])
 

time: 39.5 us -> 38.9 us (0.985)
    ppermute x9 -> x10, waiting for transfers between devices: 4.8 us -> 4.34 us  [swap(): lax.ppermute(values, 'expert', [(i, i ^ step) for i in range(sources)])]
    pallas_call x8 -> x9, Pallas kernels: 9.64 us -> 9.65 us  [call(): pl.pallas_call(kernel, out_shape=outs, in_specs=[pl.BlockSpec(memory_spac...]
    ppermute x9 -> x10, starting transfers between devices: 12.4 us -> 12.4 us  [swap(): lax.ppermute(values, 'expert', [(i, i ^ step) for i in range(sources)])]
  transfers between devices with their start and end apart: 12 -> 13, of which waited for: 6 -> 6; matrix products, arithmetic and copies ran while one was open for 0% -> 0% of each run, Pallas kernels for 8% -> 8%
where the time goes in v6:
time: 38.9 us; the launch traced here: 38.7 us
  starting transfers between devices  16 us (41%)
  Pallas kernels  9.65 us (25%)
  waiting for transfers between devices  8.58 us (22%)
  local copies, waits for them, and re-layouts  3.71 us (10%)
  between operations  0.78 us (2%)
    ppermute x10, starting transfers between devices, swap(): lax.ppermute(values, 'expert', [(i, i ^ step) for i in range(sources)])  12.4 us
    pallas_call x9, Pallas kernels, call(): pl.pallas_call(kernel, out_shape=outs, in_specs=[pl.BlockSpec(memory_spac...  9.65 us
    ppermute x10, waiting for transfers between devices, swap(): lax.ppermute(values, 'expert', [(i, i ^ step) for i in range(sources)])  4.34 us
    ppermute x3, waiting for transfers between devices, across(): lax.ppermute(values, 'dp', [(i, shift(i, step)) for i in range(copies)])  4.24 us
    unnamed x16, local copies, waits for them, and re-layouts  3.71 us
    ppermute x3, starting transfers between devices, across(): lax.ppermute(values, 'dp', [(i, shift(i, step)) for i in range(copies)])  3.55 us
  transfers between devices with their start and end apart: 13, of which 6 were waited for; matrix products, arithmetic and copies ran while one was open for 0% of the time, Pallas kernels for 8%

profile of v6, /device:TPU:0, one launch (start us, length us, event | category | flops | bytes accessed | tf_op | source)
XLA Modules:
  0.0 38.7 jit_solution(3285412243329624686)
XLA Ops:
  0.6 2.7 %shard_map.136 = (bf16[1,16,3712]{2,1,0:T(8,128)(2,1)}, f32[8,128]{1,0:T(8,128)}) custom-call(bf16[128,3584]{1,0:T(8,128)(2,1)} %refs_0_.1, bf16[128,3584]{1,0:T(8,128)(2,1)} %refs_1_.1, s32[8,128]{1,0:T(8,128)} %bitcast.22, s32[8,128]{1,0:T(8,128)} %bitcast.25, s32[1,256]{1,0:T(1,128)} %refs_4_.1), custom_call_target="tpu_custom_call" | custom-call | bytes 1835008 | tf_op jit(solution)/shard_map/pallas_call | solution.py:38
  3.3 4.1 %collective-permute-start = (bf16[1,16,3712]{2,1,0:T(8,128)(2,1)}, bf16[1,16,3712]{2,1,0:T(8,128)(2,1)S(1)}, u32[]{:S(2)}, u32[]{:S(2)}) collective-permute-start(bf16[1,16,3712]{2,1,0:T(8,128)(2,1)} %get-tuple-element.29.refs_0_), channel_id=1, source_target_pairs={{0,4},{1,5},{2,6},{3,7},{4,0},{5,1},{6,2},{7,3},{8,12},{9,13},{10,... | collective-permute-start | bytes 356360 | tf_op jit(solution)/shard_map/ppermute | solution.py:294
  7.4 1.6 %collective-permute-start.2 = (bf16[1,16,3712]{2,1,0:T(8,128)(2,1)}, bf16[1,16,3712]{2,1,0:T(8,128)(2,1)S(1)}, u32[]{:S(2)}, u32[]{:S(2)}) collective-permute-start(bf16[1,16,3712]{2,1,0:T(8,128)(2,1)} %get-tuple-element.29.refs_0_), channel_id=1, source_target_pairs={{0,2},{1,3},{2,0},{3,1},{4,6},{5,7},{6,4},{7,5},{8,10},{9,11},{10,... | collective-permute-start | bytes 356360 | tf_op jit(solution)/shard_map/ppermute | solution.py:294
  9.0 0.0 collective-permute-start.1
  9.0 1.5 %copy-done.1 = bf16[1,3584,256]{2,1,0:T(8,128)(2,1)S(1)} copy-done((bf16[1,3584,256]{2,1,0:T(8,128)(2,1)S(1)}, bf16[1,3584,256]{2,1,0:T(8,128)(2,1)}, u32[]{:S(2)}) %copy-start.1) | copy-done | bytes 1835032
  10.5 1.5 %copy-done.2 = bf16[1,256,3584]{2,1,0:T(8,128)(2,1)S(1)} copy-done((bf16[1,256,3584]{2,1,0:T(8,128)(2,1)S(1)}, bf16[1,256,3584]{2,1,0:T(8,128)(2,1)}, u32[]{:S(2)}) %copy-start.2) | copy-done | bytes 1835032
  12.0 0.7 %copy-done.5 = f32[8,128]{1,0:T(8,128)S(1)} copy-done((f32[8,128]{1,0:T(8,128)S(1)}, f32[8,128]{1,0:T(8,128)}, u32[]{:S(2)}) %copy-start.5) | copy-done | bytes 4120
  12.7 1.7 %shard_map.138 = (bf16[3584,512]{1,0:T(8,128)(2,1)S(1)}, bf16[3584,256]{1,0:T(8,128)(2,1)S(1)}, bf16[512,3584]{1,0:T(8,128)(2,1)S(1)}) custom-call(bf16[3584,256]{1,0:T(8,128)(2,1)S(1)} %bitcast.12, bf16[3584,256]{1,0:T(8,128)(2,1)S(1)} %bitcast.13, bf16[256,3584]{1,0:T(8,128)(2,1)S(1)} %bitcast.14, f32[8,128]{1,0:T(8,128)S(1)} %copy-done.5), custom_call_target="tpu_custom_call" | custom-call | bytes 40000000 | tf_op jit(solution)/shard_map/pallas_call | solution.py:38
  14.4 0.6 %collective-permute-done.refs_1_ = bf16[1,16,3712]{2,1,0:T(8,128)(2,1)S(1)} collective-permute-done((bf16[1,16,3712]{2,1,0:T(8,128)(2,1)}, bf16[1,16,3712]{2,1,0:T(8,128)(2,1)S(1)}, u32[]{:S(2)}, u32[]{:S(2)}) %collective-permute-start) | collective-permute-done | bytes 118816 | tf_op jit(solution)/shard_map/ppermute | solution.py:294
  15.1 0.1 collective-permute-start.3
  15.1 0.0 collective-permute-done.2.refs_1_
  15.2 1.9 %collective-permute-done.1.refs_0_ = bf16[1,16,3712]{2,1,0:T(8,128)(2,1)S(1)} collective-permute-done((bf16[1,16,3712]{2,1,0:T(8,128)(2,1)}, bf16[1,16,3712]{2,1,0:T(8,128)(2,1)S(1)}, u32[]{:S(2)}, u32[]{:S(2)}) %collective-permute-start.1) | collective-permute-done | bytes 118816 | tf_op jit(solution)/shard_map/ppermute | solution.py:294
  17.1 0.1 collective-permute-start.4
  17.2 1.5 %collective-permute-done.4.refs_3_ = bf16[2,16,3712]{2,1,0:T(8,128)(2,1)S(1)} collective-permute-done((bf16[2,16,3712]{2,1,0:T(8,128)(2,1)S(1)}, bf16[2,16,3712]{2,1,0:T(8,128)(2,1)S(1)}, u32[]{:S(2)}, u32[]{:S(2)}) %collective-permute-start.4) | collective-permute-done | bytes 237600 | tf_op jit(solution)/shard_map/ppermute | solution.py:294
  18.7 2.0 %shard_map.140 = (bf16[4,16,1920]{2,1,0:T(8,128)(2,1)S(1)}, bf16[4,16,1920]{2,1,0:T(8,128)(2,1)S(1)}, bf16[128,896]{1,0:T(8,128)(2,1)S(1)}, bf16[128,896]{1,0:T(...) custom-call(bf16[2,16,3712]{2,1,0:T(8,128)(2,1)S(1)} %shard_map.137.refs_0_, ...), custom_call_target="tpu_custom_call" | custom-call | bytes 40000000 | tf_op jit(solution)/shard_map/pallas_call | solution.py:38
  20.7 0.0 copy-start.7
  20.7 0.2 collective-permute-start.5
  20.9 3.0 %collective-permute-start.9 = (bf16[128,896]{1,0:T(8,128)(2,1)S(1)}, bf16[128,896]{1,0:T(8,128)(2,1)S(1)}, u32[]{:S(2)}, u32[]{:S(2)}) collective-permute-start(bf16[128,896]{1,0:T(8,128)(2,1)S(1)} %get-tuple-element.43), channel_id=1, source_target_pairs={{0,24},{8,16},{16,8},{24,0},{1,25},{9,17},{17,9},{25,1},{2,26},{10... | collective-permute-start | bytes 688136 | tf_op jit(solution)/shard_map/ppermute | solution.py:312
  23.9 0.5 %collective-permute-start.10 = (bf16[128,896]{1,0:T(8,128)(2,1)S(1)}, bf16[128,896]{1,0:T(8,128)(2,1)S(1)}, u32[]{:S(2)}, u32[]{:S(2)}) collective-permute-start(bf16[128,896]{1,0:T(8,128)(2,1)S(1)} %get-tuple-element.44), channel_id=1, source_target_pairs={{0,8},{8,0},{16,24},{24,16},{1,9},{9,1},{17,25},{25,17},{2,10},{10... | collective-permute-start | bytes 688136 | tf_op jit(solution)/shard_map/ppermute | solution.py:312
  24.4 0.1 collective-permute-start.11
  24.5 0.1 shard_map.141
  24.5 2.9 %collective-permute-start.6 = (bf16[16,1920]{1,0:T(8,128)(2,1)S(1)}, bf16[16,1920]{1,0:T(8,128)(2,1)S(1)}, u32[]{:S(2)}, u32[]{:S(2)}) collective-permute-start(bf16[16,1920]{1,0:T(8,128)(2,1)S(1)} %get-tuple-element.36), channel_id=1, source_target_pairs={{0,6},{1,7},{2,4},{3,5},{4,2},{5,3},{6,0},{7,1},{8,14},{9,15},{10,... | collective-permute-start | bytes 184328 | tf_op jit(solution)/shard_map/ppermute | solution.py:294
  27.5 1.2 %collective-permute-start.7 = (bf16[16,1920]{1,0:T(8,128)(2,1)S(1)}, bf16[16,1920]{1,0:T(8,128)(2,1)S(1)}, u32[]{:S(2)}, u32[]{:S(2)}) collective-permute-start(bf16[16,1920]{1,0:T(8,128)(2,1)S(1)} %get-tuple-element.37), channel_id=1, source_target_pairs={{0,4},{1,5},{2,6},{3,7},{4,0},{5,1},{6,2},{7,3},{8,12},{9,13},{10,... | collective-permute-start | bytes 184328 | tf_op jit(solution)/shard_map/ppermute | solution.py:294
  28.7 1.7 %collective-permute-done.9.refs_0_.refs_3_ = bf16[128,896]{1,0:T(8,128)(2,1)S(1)} collective-permute-done((bf16[128,896]{1,0:T(8,128)(2,1)S(1)}, bf16[128,896]{1,0:T(8,128)(2,1)S(1)}, u32[]{:S(2)}, u32[]{:S(2)}) %collective-permute-start.9) | collective-permute-done | bytes 229408 | tf_op jit(solution)/shard_map/ppermute | solution.py:312
  30.3 2.2 %collective-permute-start.8 = (bf16[16,1920]{1,0:T(8,128)(2,1)S(1)}, bf16[16,1920]{1,0:T(8,128)(2,1)S(1)}, u32[]{:S(2)}, u32[]{:S(2)}) collective-permute-start(bf16[16,1920]{1,0:T(8,128)(2,1)S(1)} %get-tuple-element.38), channel_id=1, source_target_pairs={{0,2},{1,3},{2,0},{3,1},{4,6},{5,7},{6,4},{7,5},{8,10},{9,11},{10,... | collective-permute-start | bytes 184328 | tf_op jit(solution)/shard_map/ppermute | solution.py:294
  32.5 2.6 %collective-permute-done.10.refs_2_.refs_4_ = bf16[128,896]{1,0:T(8,128)(2,1)S(1)} collective-permute-done((bf16[128,896]{1,0:T(8,128)(2,1)S(1)}, bf16[128,896]{1,0:T(8,128)(2,1)S(1)}, u32[]{:S(2)}, u32[]{:S(2)}) %collective-permute-start.10) | collective-permute-done | bytes 229408 | tf_op jit(solution)/shard_map/ppermute | solution.py:312
  35.1 0.0 collective-permute-done.11.refs_1_.refs_5_
  35.1 0.0 collective-permute-done.6
  35.1 0.1 collective-permute-start.12
  35.2 1.4 %shard_map.142 = (bf16[128,3584]{1,0:T(8,128)(2,1)}, f32[8,128]{1,0:T(8,128)}) custom-call(f32[8,128]{1,0:T(8,128)S(1)} %copy-done.6, s32[8,128]{1,0:T(8,128)S(1)} %bitcast.23, f32[1,1,16,1920]{3,2,1,0:T(8,128)S(1)} %bitcast.21, bf16[1,1,16,1920]{3,2,1,0:T(8,128)(2,1)S(1)} %bitcast.16, bf16[1,1,16,1920]{3,2,1,0:T(8,128)(2,1)S(1)} %bitcast.18, ...), custom_call_target="tpu_custom_call" | custom-call | bytes 1000 | tf_op jit(solution)/shard_map/pallas_call | solution.py:38
  36.6 0.3 collective-permute-done.12.refs_6_
  36.9 1.8 %shard_map.144 = (bf16[1,896,256]{2,1,0:T(8,128)(2,1)}, bf16[1,896,256]{2,1,0:T(8,128)(2,1)}, bf16[1,256,896]{2,1,0:T(8,128)(2,1)}, f32[1,256]{1,0:T(1,128)}) custom-call(f32[1,256]{1,0:T(1,128)S(1)} %bitcast.24, bf16[128,896]{1,0:T(8,128)(2,1)S(1)} %get-tuple-element.41.refs_1_, bf16[64,896]{1,0:T(8,128)(2,1)S(1)} %get-tuple-element.42.refs_2_, ...), custom_call_target="tpu_custom_call" | custom-call | bytes 1000 | tf_op jit(solution)/shard_map/pallas_call | solution.py:38
  (19 shorter events, 0.1 us)
Async XLA Ops:
  0.6 8.4 %copy-start = (bf16[1,3584,256]{2,1,0:T(8,128)(2,1)S(1)}, bf16[1,3584,256]{2,1,0:T(8,128)(2,1)}, u32[]{:S(2)}) copy-start(bf16[1,3584,256]{2,1,0:T(8,128)(2,1)} %param.13) | copy-start | bytes 5505028
  3.3 11.7 %collective-permute-start = (bf16[1,16,3712]{2,1,0:T(8,128)(2,1)}, bf16[1,16,3712]{2,1,0:T(8,128)(2,1)S(1)}, u32[]{:S(2)}, u32[]{:S(2)}) collective-permute-start(bf16[1,16,3712]{2,1,0:T(8,128)(2,1)} %get-tuple-element.29.refs_0_), channel_id=1, source_target_pairs={{0,4},{1,5},{2,6},{3,7},{4,0},{5,1},{6,2},{7,3},{8,12},{9,13},{10,... | collective-permute-start | bytes 356360 | tf_op jit(solution)/shard_map/ppermute | solution.py:294
  7.4 7.7 %collective-permute-start.2 = (bf16[1,16,3712]{2,1,0:T(8,128)(2,1)}, bf16[1,16,3712]{2,1,0:T(8,128)(2,1)S(1)}, u32[]{:S(2)}, u32[]{:S(2)}) collective-permute-start(bf16[1,16,3712]{2,1,0:T(8,128)(2,1)} %get-tuple-element.29.refs_0_), channel_id=1, source_target_pairs={{0,2},{1,3},{2,0},{3,1},{4,6},{5,7},{6,4},{7,5},{8,10},{9,11},{10,... | collective-permute-start | bytes 356360 | tf_op jit(solution)/shard_map/ppermute | solution.py:294
  9.0 8.1 %collective-permute-start.1 = (bf16[1,16,3712]{2,1,0:T(8,128)(2,1)}, bf16[1,16,3712]{2,1,0:T(8,128)(2,1)S(1)}, u32[]{:S(2)}, u32[]{:S(2)}) collective-permute-start(bf16[1,16,3712]{2,1,0:T(8,128)(2,1)} %get-tuple-element.29.refs_0_), channel_id=1, source_target_pairs={{0,6},{1,7},{2,4},{3,5},{4,2},{5,3},{6,0},{7,1},{8,14},{9,15},{10,... | collective-permute-start | bytes 356360 | tf_op jit(solution)/shard_map/ppermute | solution.py:294
  9.0 1.5 %copy-start.1 = (bf16[1,3584,256]{2,1,0:T(8,128)(2,1)S(1)}, bf16[1,3584,256]{2,1,0:T(8,128)(2,1)}, u32[]{:S(2)}) copy-start(bf16[1,3584,256]{2,1,0:T(8,128)(2,1)} %param.14) | copy-start | bytes 5505028
  10.5 1.5 %copy-start.2 = (bf16[1,256,3584]{2,1,0:T(8,128)(2,1)S(1)}, bf16[1,256,3584]{2,1,0:T(8,128)(2,1)}, u32[]{:S(2)}) copy-start(bf16[1,256,3584]{2,1,0:T(8,128)(2,1)} %param.15) | copy-start | bytes 5505028
  12.0 0.7 %copy-start.5 = (f32[8,128]{1,0:T(8,128)S(1)}, f32[8,128]{1,0:T(8,128)}, u32[]{:S(2)}) copy-start(f32[8,128]{1,0:T(8,128)} %get-tuple-element.28.refs_3_.refs_0_) | copy-start | bytes 12292
  12.7 2.4 %copy-start.3 = (bf16[1,16,3712]{2,1,0:T(8,128)(2,1)S(1)}, bf16[1,16,3712]{2,1,0:T(8,128)(2,1)}, u32[]{:S(2)}) copy-start(bf16[1,16,3712]{2,1,0:T(8,128)(2,1)} %get-tuple-element.29.refs_0_) | copy-start | bytes 356356
  15.1 2.1 %collective-permute-start.3 = (bf16[2,16,3712]{2,1,0:T(8,128)(2,1)S(1)}, bf16[2,16,3712]{2,1,0:T(8,128)(2,1)S(1)}, u32[]{:S(2)}, u32[]{:S(2)}) collective-permute-start(bf16[2,16,3712]{2,1,0:T(8,128)(2,1)S(1)} %shard_map.137.refs_0_), channel_id=1, source_target_pairs={{0,1},{1,0},{2,3},{3,2},{4,5},{5,4},{6,7},{7,6},{8,9},{9,8},{10,11... | collective-permute-start | bytes 712712 | tf_op jit(solution)/shard_map/ppermute | solution.py:294
  17.1 1.6 %collective-permute-start.4 = (bf16[2,16,3712]{2,1,0:T(8,128)(2,1)S(1)}, bf16[2,16,3712]{2,1,0:T(8,128)(2,1)S(1)}, u32[]{:S(2)}, u32[]{:S(2)}) collective-permute-start(bf16[2,16,3712]{2,1,0:T(8,128)(2,1)S(1)} %shard_map.139.refs_1_), channel_id=1, source_target_pairs={{0,1},{1,0},{2,3},{3,2},{4,5},{5,4},{6,7},{7,6},{8,9},{9,8},{10,11... | collective-permute-start | bytes 712712 | tf_op jit(solution)/shard_map/ppermute | solution.py:294
  18.7 16.5 %copy-start.4 = (s32[128,8]{0,1:T(8,128)S(1)}, s32[128,8]{0,1:T(8,128)}, u32[]{:S(2)}) copy-start(s32[128,8]{0,1:T(8,128)} %param.11) | copy-start | bytes 12292
  18.7 16.5 %copy-start.6 = (f32[8,128]{1,0:T(8,128)S(1)}, f32[8,128]{1,0:T(8,128)}, u32[]{:S(2)}) copy-start(f32[8,128]{1,0:T(8,128)} %get-tuple-element.28.refs_3_.refs_0_) | copy-start | bytes 12292
  20.7 16.2 %copy-start.7 = (f32[256]{0:T(256)S(1)}, f32[256]{0:T(256)}, u32[]{:S(2)}) copy-start(f32[256]{0:T(256)} %param.16) | copy-start | bytes 3076
  20.7 3.8 %collective-permute-start.5 = (bf16[4,16,1920]{2,1,0:T(8,128)(2,1)S(1)}, bf16[4,16,1920]{2,1,0:T(8,128)(2,1)S(1)}, u32[]{:S(2)}, u32[]{:S(2)}) collective-permute-start(bf16[4,16,1920]{2,1,0:T(8,128)(2,1)S(1)} %get-tuple-element.34), channel_id=1, source_target_pairs={{0,1},{1,0},{2,3},{3,2},{4,5},{5,4},{6,7},{7,6},{8,9},{9,8},{10,11... | collective-permute-start | bytes 737288 | tf_op jit(solution)/shard_map/ppermute | solution.py:294
  20.9 9.4 %collective-permute-start.9 = (bf16[128,896]{1,0:T(8,128)(2,1)S(1)}, bf16[128,896]{1,0:T(8,128)(2,1)S(1)}, u32[]{:S(2)}, u32[]{:S(2)}) collective-permute-start(bf16[128,896]{1,0:T(8,128)(2,1)S(1)} %get-tuple-element.43), channel_id=1, source_target_pairs={{0,24},{8,16},{16,8},{24,0},{1,25},{9,17},{17,9},{25,1},{2,26},{10... | collective-permute-start | bytes 688136 | tf_op jit(solution)/shard_map/ppermute | solution.py:312
  23.9 11.2 %collective-permute-start.10 = (bf16[128,896]{1,0:T(8,128)(2,1)S(1)}, bf16[128,896]{1,0:T(8,128)(2,1)S(1)}, u32[]{:S(2)}, u32[]{:S(2)}) collective-permute-start(bf16[128,896]{1,0:T(8,128)(2,1)S(1)} %get-tuple-element.44), channel_id=1, source_target_pairs={{0,8},{8,0},{16,24},{24,16},{1,9},{9,1},{17,25},{25,17},{2,10},{10... | collective-permute-start | bytes 688136 | tf_op jit(solution)/shard_map/ppermute | solution.py:312
  24.4 10.7 %collective-permute-start.11 = (bf16[128,896]{1,0:T(8,128)(2,1)S(1)}, bf16[128,896]{1,0:T(8,128)(2,1)S(1)}, u32[]{:S(2)}, u32[]{:S(2)}) collective-permute-start(bf16[128,896]{1,0:T(8,128)(2,1)S(1)} %get-tuple-element.45), channel_id=1, source_target_pairs={{0,16},{8,24},{16,0},{24,8},{1,17},{9,25},{17,1},{25,9},{2,18},{10... | collective-permute-start | bytes 688136 | tf_op jit(solution)/shard_map/ppermute | solution.py:312
  24.5 10.6 %collective-permute-start.6 = (bf16[16,1920]{1,0:T(8,128)(2,1)S(1)}, bf16[16,1920]{1,0:T(8,128)(2,1)S(1)}, u32[]{:S(2)}, u32[]{:S(2)}) collective-permute-start(bf16[16,1920]{1,0:T(8,128)(2,1)S(1)} %get-tuple-element.36), channel_id=1, source_target_pairs={{0,6},{1,7},{2,4},{3,5},{4,2},{5,3},{6,0},{7,1},{8,14},{9,15},{10,... | collective-permute-start | bytes 184328 | tf_op jit(solution)/shard_map/ppermute | solution.py:294
  27.5 7.6 %collective-permute-start.7 = (bf16[16,1920]{1,0:T(8,128)(2,1)S(1)}, bf16[16,1920]{1,0:T(8,128)(2,1)S(1)}, u32[]{:S(2)}, u32[]{:S(2)}) collective-permute-start(bf16[16,1920]{1,0:T(8,128)(2,1)S(1)} %get-tuple-element.37), channel_id=1, source_target_pairs={{0,4},{1,5},{2,6},{3,7},{4,0},{5,1},{6,2},{7,3},{8,12},{9,13},{10,... | collective-permute-start | bytes 184328 | tf_op jit(solution)/shard_map/ppermute | solution.py:294
  30.3 4.8 %collective-permute-start.8 = (bf16[16,1920]{1,0:T(8,128)(2,1)S(1)}, bf16[16,1920]{1,0:T(8,128)(2,1)S(1)}, u32[]{:S(2)}, u32[]{:S(2)}) collective-permute-start(bf16[16,1920]{1,0:T(8,128)(2,1)S(1)} %get-tuple-element.38), channel_id=1, source_target_pairs={{0,2},{1,3},{2,0},{3,1},{4,6},{5,7},{6,4},{7,5},{8,10},{9,11},{10,... | collective-permute-start | bytes 184328 | tf_op jit(solution)/shard_map/ppermute | solution.py:294
  35.1 1.7 %collective-permute-start.12 = (bf16[3,64,896]{2,1,0:T(8,128)(2,1)S(1)}, bf16[3,64,896]{2,1,0:T(8,128)(2,1)S(1)}, u32[]{:S(2)}, u32[]{:S(2)}) collective-permute-start(bf16[3,64,896]{2,1,0:T(8,128)(2,1)S(1)} %shard_map.143), channel_id=1, source_target_pairs={{0,1},{1,0},{2,3},{3,2},{4,5},{5,4},{6,7},{7,6},{8,9},{9,8},{10,11... | collective-permute-start | bytes 1032200 | tf_op jit(solution)/shard_map/ppermute | solution.py:294

commit v7 on v6

--- a/solution.py
+++ b/solution.py
@@ -236,19 +236,17 @@
     rows = jnp.concatenate(rows, axis=0)
     hidden, scaled = [], []
     for value in grads:
-        value = value.astype(F32)
-        digit = value[:CAP, 3 * units :]
+        digit = value[:BLOCK].astype(F32)[:CAP, 3 * units :]
         load = load + digit[0:2] + digit[2:4] * LANES + digit[4:6] * LANES**2
-        value = value.reshape(blocks, CAP, value.shape[1])
-        left, right = value[:, :, : 2 * units], value[:, :, 2 * units : 3 * units]
-        left = jnp.concatenate([left, jnp.zeros_like(left)], axis=1)
-        right = jnp.concatenate([jnp.zeros_like(right), right], axis=1)
-        hidden.append(left.reshape(blocks * BLOCK, 2 * units).astype(BF16))
-        scaled.append(right.reshape(blocks * BLOCK, units).astype(BF16))
-    both = dot(rows, jnp.concatenate(hidden, axis=0), 0, 0)
+        hidden.append(value[:, : 2 * units])
+        scaled.append(value[:, 2 * units : 3 * units])
+    rows = rows.astype(F32).reshape(-1, BLOCK, quarter)
+    rows_in = rows[:, :CAP].reshape(-1, quarter).astype(BF16)
+    rows_grad = rows[:, CAP:].reshape(-1, quarter).astype(BF16)
+    both = dot(rows_in, jnp.concatenate(hidden, axis=0), 0, 0)
     gate_ref[0] = both[:, :units].astype(BF16)
     up_ref[0] = both[:, units:].astype(BF16)
-    down_ref[0] = dot(jnp.concatenate(scaled, axis=0), rows, 0, 0).astype(BF16)
+    down_ref[0] = dot(jnp.concatenate(scaled, axis=0), rows_grad, 0, 0).astype(BF16)
     load = jnp.concatenate([load[0:1], load[1:2]], axis=1)
     diff = jnp.sum(load, axis=1, keepdims=True) - EXPERTS_ALL * load
     sign = jnp.where(diff > 0.0, 1.0, jnp.where(diff < 0.0, -1.0, 0.0))

time: 38.9 us -> 38.6 us (level)
  no operation moved by 1% of the time
where the time goes in v7:
time: 38.6 us; the launch traced here: 38.4 us
  starting transfers between devices  16 us (41%)
  Pallas kernels  9.36 us (24%)
  waiting for transfers between devices  8.58 us (22%)
  local copies, waits for them, and re-layouts  3.71 us (10%)
  between operations  0.78 us (2%)
    ppermute x10, starting transfers between devices, swap(): lax.ppermute(values, 'expert', [(i, i ^ step) for i in range(sources)])  12.4 us
    pallas_call x9, Pallas kernels, call(): pl.pallas_call(kernel, out_shape=outs, in_specs=[pl.BlockSpec(memory_spac...  9.36 us
    ppermute x10, waiting for transfers between devices, swap(): lax.ppermute(values, 'expert', [(i, i ^ step) for i in range(sources)])  4.34 us
    ppermute x3, waiting for transfers between devices, across(): lax.ppermute(values, 'dp', [(i, shift(i, step)) for i in range(copies)])  4.24 us
    unnamed x16, local copies, waits for them, and re-layouts  3.71 us
    ppermute x3, starting transfers between devices, across(): lax.ppermute(values, 'dp', [(i, shift(i, step)) for i in range(copies)])  3.55 us
  transfers between devices with their start and end apart: 13, of which 6 were waited for; matrix products, arithmetic and copies ran while one was open for 0% of the time, Pallas kernels for 8%

profile of v7, /device:TPU:0, one launch (start us, length us, event | category | flops | bytes accessed | tf_op | source)
XLA Modules:
  0.0 38.4 jit_solution(8259868920138101055)
XLA Ops:
  0.6 2.7 %shard_map.136 = (bf16[1,16,3712]{2,1,0:T(8,128)(2,1)}, f32[8,128]{1,0:T(8,128)}) custom-call(bf16[128,3584]{1,0:T(8,128)(2,1)} %refs_0_.1, bf16[128,3584]{1,0:T(8,128)(2,1)} %refs_1_.1, s32[8,128]{1,0:T(8,128)} %bitcast.22, s32[8,128]{1,0:T(8,128)} %bitcast.25, s32[1,256]{1,0:T(1,128)} %refs_4_.1), custom_call_target="tpu_custom_call" | custom-call | bytes 1835008 | tf_op jit(solution)/shard_map/pallas_call | solution.py:38
  3.3 4.1 %collective-permute-start = (bf16[1,16,3712]{2,1,0:T(8,128)(2,1)}, bf16[1,16,3712]{2,1,0:T(8,128)(2,1)S(1)}, u32[]{:S(2)}, u32[]{:S(2)}) collective-permute-start(bf16[1,16,3712]{2,1,0:T(8,128)(2,1)} %get-tuple-element.29.refs_0_), channel_id=1, source_target_pairs={{0,4},{1,5},{2,6},{3,7},{4,0},{5,1},{6,2},{7,3},{8,12},{9,13},{10,... | collective-permute-start | bytes 356360 | tf_op jit(solution)/shard_map/ppermute | solution.py:292
  7.4 1.6 %collective-permute-start.2 = (bf16[1,16,3712]{2,1,0:T(8,128)(2,1)}, bf16[1,16,3712]{2,1,0:T(8,128)(2,1)S(1)}, u32[]{:S(2)}, u32[]{:S(2)}) collective-permute-start(bf16[1,16,3712]{2,1,0:T(8,128)(2,1)} %get-tuple-element.29.refs_0_), channel_id=1, source_target_pairs={{0,2},{1,3},{2,0},{3,1},{4,6},{5,7},{6,4},{7,5},{8,10},{9,11},{10,... | collective-permute-start | bytes 356360 | tf_op jit(solution)/shard_map/ppermute | solution.py:292
  9.0 0.0 collective-permute-start.1
  9.0 1.5 %copy-done.1 = bf16[1,3584,256]{2,1,0:T(8,128)(2,1)S(1)} copy-done((bf16[1,3584,256]{2,1,0:T(8,128)(2,1)S(1)}, bf16[1,3584,256]{2,1,0:T(8,128)(2,1)}, u32[]{:S(2)}) %copy-start.1) | copy-done | bytes 1835032
  10.5 1.5 %copy-done.2 = bf16[1,256,3584]{2,1,0:T(8,128)(2,1)S(1)} copy-done((bf16[1,256,3584]{2,1,0:T(8,128)(2,1)S(1)}, bf16[1,256,3584]{2,1,0:T(8,128)(2,1)}, u32[]{:S(2)}) %copy-start.2) | copy-done | bytes 1835032
  12.0 0.7 %copy-done.5 = f32[8,128]{1,0:T(8,128)S(1)} copy-done((f32[8,128]{1,0:T(8,128)S(1)}, f32[8,128]{1,0:T(8,128)}, u32[]{:S(2)}) %copy-start.5) | copy-done | bytes 4120
  12.7 1.7 %shard_map.138 = (bf16[3584,512]{1,0:T(8,128)(2,1)S(1)}, bf16[3584,256]{1,0:T(8,128)(2,1)S(1)}, bf16[512,3584]{1,0:T(8,128)(2,1)S(1)}) custom-call(bf16[3584,256]{1,0:T(8,128)(2,1)S(1)} %bitcast.12, bf16[3584,256]{1,0:T(8,128)(2,1)S(1)} %bitcast.13, bf16[256,3584]{1,0:T(8,128)(2,1)S(1)} %bitcast.14, f32[8,128]{1,0:T(8,128)S(1)} %copy-done.5), custom_call_target="tpu_custom_call" | custom-call | bytes 40000000 | tf_op jit(solution)/shard_map/pallas_call | solution.py:38
  14.4 0.6 %collective-permute-done.refs_1_ = bf16[1,16,3712]{2,1,0:T(8,128)(2,1)S(1)} collective-permute-done((bf16[1,16,3712]{2,1,0:T(8,128)(2,1)}, bf16[1,16,3712]{2,1,0:T(8,128)(2,1)S(1)}, u32[]{:S(2)}, u32[]{:S(2)}) %collective-permute-start) | collective-permute-done | bytes 118816 | tf_op jit(solution)/shard_map/ppermute | solution.py:292
  15.1 0.1 collective-permute-start.3
  15.1 0.0 collective-permute-done.2.refs_1_
  15.2 1.9 %collective-permute-done.1.refs_0_ = bf16[1,16,3712]{2,1,0:T(8,128)(2,1)S(1)} collective-permute-done((bf16[1,16,3712]{2,1,0:T(8,128)(2,1)}, bf16[1,16,3712]{2,1,0:T(8,128)(2,1)S(1)}, u32[]{:S(2)}, u32[]{:S(2)}) %collective-permute-start.1) | collective-permute-done | bytes 118816 | tf_op jit(solution)/shard_map/ppermute | solution.py:292
  17.1 0.1 collective-permute-start.4
  17.2 1.5 %collective-permute-done.4.refs_3_ = bf16[2,16,3712]{2,1,0:T(8,128)(2,1)S(1)} collective-permute-done((bf16[2,16,3712]{2,1,0:T(8,128)(2,1)S(1)}, bf16[2,16,3712]{2,1,0:T(8,128)(2,1)S(1)}, u32[]{:S(2)}, u32[]{:S(2)}) %collective-permute-start.4) | collective-permute-done | bytes 237600 | tf_op jit(solution)/shard_map/ppermute | solution.py:292
  18.7 2.0 %shard_map.140 = (bf16[4,16,1920]{2,1,0:T(8,128)(2,1)S(1)}, bf16[4,16,1920]{2,1,0:T(8,128)(2,1)S(1)}, bf16[128,896]{1,0:T(8,128)(2,1)S(1)}, bf16[128,896]{1,0:T(...) custom-call(bf16[2,16,3712]{2,1,0:T(8,128)(2,1)S(1)} %shard_map.137.refs_0_, ...), custom_call_target="tpu_custom_call" | custom-call | bytes 40000000 | tf_op jit(solution)/shard_map/pallas_call | solution.py:38
  20.7 0.0 copy-start.7
  20.7 0.2 collective-permute-start.5
  20.9 3.0 %collective-permute-start.9 = (bf16[128,896]{1,0:T(8,128)(2,1)S(1)}, bf16[128,896]{1,0:T(8,128)(2,1)S(1)}, u32[]{:S(2)}, u32[]{:S(2)}) collective-permute-start(bf16[128,896]{1,0:T(8,128)(2,1)S(1)} %get-tuple-element.43), channel_id=1, source_target_pairs={{0,24},{8,16},{16,8},{24,0},{1,25},{9,17},{17,9},{25,1},{2,26},{10... | collective-permute-start | bytes 688136 | tf_op jit(solution)/shard_map/ppermute | solution.py:310
  23.9 0.5 %collective-permute-start.10 = (bf16[128,896]{1,0:T(8,128)(2,1)S(1)}, bf16[128,896]{1,0:T(8,128)(2,1)S(1)}, u32[]{:S(2)}, u32[]{:S(2)}) collective-permute-start(bf16[128,896]{1,0:T(8,128)(2,1)S(1)} %get-tuple-element.44), channel_id=1, source_target_pairs={{0,8},{8,0},{16,24},{24,16},{1,9},{9,1},{17,25},{25,17},{2,10},{10... | collective-permute-start | bytes 688136 | tf_op jit(solution)/shard_map/ppermute | solution.py:310
  24.4 0.1 collective-permute-start.11
  24.5 0.1 shard_map.141
  24.5 2.9 %collective-permute-start.6 = (bf16[16,1920]{1,0:T(8,128)(2,1)S(1)}, bf16[16,1920]{1,0:T(8,128)(2,1)S(1)}, u32[]{:S(2)}, u32[]{:S(2)}) collective-permute-start(bf16[16,1920]{1,0:T(8,128)(2,1)S(1)} %get-tuple-element.36), channel_id=1, source_target_pairs={{0,6},{1,7},{2,4},{3,5},{4,2},{5,3},{6,0},{7,1},{8,14},{9,15},{10,... | collective-permute-start | bytes 184328 | tf_op jit(solution)/shard_map/ppermute | solution.py:292
  27.5 1.2 %collective-permute-start.7 = (bf16[16,1920]{1,0:T(8,128)(2,1)S(1)}, bf16[16,1920]{1,0:T(8,128)(2,1)S(1)}, u32[]{:S(2)}, u32[]{:S(2)}) collective-permute-start(bf16[16,1920]{1,0:T(8,128)(2,1)S(1)} %get-tuple-element.37), channel_id=1, source_target_pairs={{0,4},{1,5},{2,6},{3,7},{4,0},{5,1},{6,2},{7,3},{8,12},{9,13},{10,... | collective-permute-start | bytes 184328 | tf_op jit(solution)/shard_map/ppermute | solution.py:292
  28.7 1.7 %collective-permute-done.9.refs_0_.refs_3_ = bf16[128,896]{1,0:T(8,128)(2,1)S(1)} collective-permute-done((bf16[128,896]{1,0:T(8,128)(2,1)S(1)}, bf16[128,896]{1,0:T(8,128)(2,1)S(1)}, u32[]{:S(2)}, u32[]{:S(2)}) %collective-permute-start.9) | collective-permute-done | bytes 229408 | tf_op jit(solution)/shard_map/ppermute | solution.py:310
  30.3 2.2 %collective-permute-start.8 = (bf16[16,1920]{1,0:T(8,128)(2,1)S(1)}, bf16[16,1920]{1,0:T(8,128)(2,1)S(1)}, u32[]{:S(2)}, u32[]{:S(2)}) collective-permute-start(bf16[16,1920]{1,0:T(8,128)(2,1)S(1)} %get-tuple-element.38), channel_id=1, source_target_pairs={{0,2},{1,3},{2,0},{3,1},{4,6},{5,7},{6,4},{7,5},{8,10},{9,11},{10,... | collective-permute-start | bytes 184328 | tf_op jit(solution)/shard_map/ppermute | solution.py:292
  32.5 2.6 %collective-permute-done.10.refs_2_.refs_4_ = bf16[128,896]{1,0:T(8,128)(2,1)S(1)} collective-permute-done((bf16[128,896]{1,0:T(8,128)(2,1)S(1)}, bf16[128,896]{1,0:T(8,128)(2,1)S(1)}, u32[]{:S(2)}, u32[]{:S(2)}) %collective-permute-start.10) | collective-permute-done | bytes 229408 | tf_op jit(solution)/shard_map/ppermute | solution.py:310
  35.1 0.0 collective-permute-done.11.refs_1_.refs_5_
  35.1 0.0 collective-permute-done.6
  35.1 0.1 collective-permute-start.12
  35.2 1.4 %shard_map.142 = (bf16[128,3584]{1,0:T(8,128)(2,1)}, f32[8,128]{1,0:T(8,128)}) custom-call(f32[8,128]{1,0:T(8,128)S(1)} %copy-done.6, s32[8,128]{1,0:T(8,128)S(1)} %bitcast.23, f32[1,1,16,1920]{3,2,1,0:T(8,128)S(1)} %bitcast.21, bf16[1,1,16,1920]{3,2,1,0:T(8,128)(2,1)S(1)} %bitcast.16, bf16[1,1,16,1920]{3,2,1,0:T(8,128)(2,1)S(1)} %bitcast.18, ...), custom_call_target="tpu_custom_call" | custom-call | bytes 1000 | tf_op jit(solution)/shard_map/pallas_call | solution.py:38
  36.6 0.3 collective-permute-done.12.refs_6_
  36.9 1.5 %shard_map.144 = (bf16[1,896,256]{2,1,0:T(8,128)(2,1)}, bf16[1,896,256]{2,1,0:T(8,128)(2,1)}, bf16[1,256,896]{2,1,0:T(8,128)(2,1)}, f32[1,256]{1,0:T(1,128)}) custom-call(f32[1,256]{1,0:T(1,128)S(1)} %bitcast.24, bf16[128,896]{1,0:T(8,128)(2,1)S(1)} %get-tuple-element.41.refs_1_, bf16[64,896]{1,0:T(8,128)(2,1)S(1)} %get-tuple-element.42.refs_2_, ...), custom_call_target="tpu_custom_call" | custom-call | bytes 1000 | tf_op jit(solution)/shard_map/pallas_call | solution.py:38
  (19 shorter events, 0.1 us)
Async XLA Ops:
  0.6 8.4 %copy-start = (bf16[1,3584,256]{2,1,0:T(8,128)(2,1)S(1)}, bf16[1,3584,256]{2,1,0:T(8,128)(2,1)}, u32[]{:S(2)}) copy-start(bf16[1,3584,256]{2,1,0:T(8,128)(2,1)} %param.13) | copy-start | bytes 5505028
  3.3 11.7 %collective-permute-start = (bf16[1,16,3712]{2,1,0:T(8,128)(2,1)}, bf16[1,16,3712]{2,1,0:T(8,128)(2,1)S(1)}, u32[]{:S(2)}, u32[]{:S(2)}) collective-permute-start(bf16[1,16,3712]{2,1,0:T(8,128)(2,1)} %get-tuple-element.29.refs_0_), channel_id=1, source_target_pairs={{0,4},{1,5},{2,6},{3,7},{4,0},{5,1},{6,2},{7,3},{8,12},{9,13},{10,... | collective-permute-start | bytes 356360 | tf_op jit(solution)/shard_map/ppermute | solution.py:292
  7.4 7.7 %collective-permute-start.2 = (bf16[1,16,3712]{2,1,0:T(8,128)(2,1)}, bf16[1,16,3712]{2,1,0:T(8,128)(2,1)S(1)}, u32[]{:S(2)}, u32[]{:S(2)}) collective-permute-start(bf16[1,16,3712]{2,1,0:T(8,128)(2,1)} %get-tuple-element.29.refs_0_), channel_id=1, source_target_pairs={{0,2},{1,3},{2,0},{3,1},{4,6},{5,7},{6,4},{7,5},{8,10},{9,11},{10,... | collective-permute-start | bytes 356360 | tf_op jit(solution)/shard_map/ppermute | solution.py:292
  9.0 8.1 %collective-permute-start.1 = (bf16[1,16,3712]{2,1,0:T(8,128)(2,1)}, bf16[1,16,3712]{2,1,0:T(8,128)(2,1)S(1)}, u32[]{:S(2)}, u32[]{:S(2)}) collective-permute-start(bf16[1,16,3712]{2,1,0:T(8,128)(2,1)} %get-tuple-element.29.refs_0_), channel_id=1, source_target_pairs={{0,6},{1,7},{2,4},{3,5},{4,2},{5,3},{6,0},{7,1},{8,14},{9,15},{10,... | collective-permute-start | bytes 356360 | tf_op jit(solution)/shard_map/ppermute | solution.py:292
  9.0 1.5 %copy-start.1 = (bf16[1,3584,256]{2,1,0:T(8,128)(2,1)S(1)}, bf16[1,3584,256]{2,1,0:T(8,128)(2,1)}, u32[]{:S(2)}) copy-start(bf16[1,3584,256]{2,1,0:T(8,128)(2,1)} %param.14) | copy-start | bytes 5505028
  10.5 1.5 %copy-start.2 = (bf16[1,256,3584]{2,1,0:T(8,128)(2,1)S(1)}, bf16[1,256,3584]{2,1,0:T(8,128)(2,1)}, u32[]{:S(2)}) copy-start(bf16[1,256,3584]{2,1,0:T(8,128)(2,1)} %param.15) | copy-start | bytes 5505028
  12.0 0.7 %copy-start.5 = (f32[8,128]{1,0:T(8,128)S(1)}, f32[8,128]{1,0:T(8,128)}, u32[]{:S(2)}) copy-start(f32[8,128]{1,0:T(8,128)} %get-tuple-element.28.refs_3_.refs_0_) | copy-start | bytes 12292
  12.7 2.4 %copy-start.3 = (bf16[1,16,3712]{2,1,0:T(8,128)(2,1)S(1)}, bf16[1,16,3712]{2,1,0:T(8,128)(2,1)}, u32[]{:S(2)}) copy-start(bf16[1,16,3712]{2,1,0:T(8,128)(2,1)} %get-tuple-element.29.refs_0_) | copy-start | bytes 356356
  15.1 2.1 %collective-permute-start.3 = (bf16[2,16,3712]{2,1,0:T(8,128)(2,1)S(1)}, bf16[2,16,3712]{2,1,0:T(8,128)(2,1)S(1)}, u32[]{:S(2)}, u32[]{:S(2)}) collective-permute-start(bf16[2,16,3712]{2,1,0:T(8,128)(2,1)S(1)} %shard_map.137.refs_0_), channel_id=1, source_target_pairs={{0,1},{1,0},{2,3},{3,2},{4,5},{5,4},{6,7},{7,6},{8,9},{9,8},{10,11... | collective-permute-start | bytes 712712 | tf_op jit(solution)/shard_map/ppermute | solution.py:292
  17.1 1.6 %collective-permute-start.4 = (bf16[2,16,3712]{2,1,0:T(8,128)(2,1)S(1)}, bf16[2,16,3712]{2,1,0:T(8,128)(2,1)S(1)}, u32[]{:S(2)}, u32[]{:S(2)}) collective-permute-start(bf16[2,16,3712]{2,1,0:T(8,128)(2,1)S(1)} %shard_map.139.refs_1_), channel_id=1, source_target_pairs={{0,1},{1,0},{2,3},{3,2},{4,5},{5,4},{6,7},{7,6},{8,9},{9,8},{10,11... | collective-permute-start | bytes 712712 | tf_op jit(solution)/shard_map/ppermute | solution.py:292
  18.7 16.5 %copy-start.4 = (s32[128,8]{0,1:T(8,128)S(1)}, s32[128,8]{0,1:T(8,128)}, u32[]{:S(2)}) copy-start(s32[128,8]{0,1:T(8,128)} %param.11) | copy-start | bytes 12292
  18.7 16.5 %copy-start.6 = (f32[8,128]{1,0:T(8,128)S(1)}, f32[8,128]{1,0:T(8,128)}, u32[]{:S(2)}) copy-start(f32[8,128]{1,0:T(8,128)} %get-tuple-element.28.refs_3_.refs_0_) | copy-start | bytes 12292
  20.7 16.2 %copy-start.7 = (f32[256]{0:T(256)S(1)}, f32[256]{0:T(256)}, u32[]{:S(2)}) copy-start(f32[256]{0:T(256)} %param.16) | copy-start | bytes 3076
  20.7 3.8 %collective-permute-start.5 = (bf16[4,16,1920]{2,1,0:T(8,128)(2,1)S(1)}, bf16[4,16,1920]{2,1,0:T(8,128)(2,1)S(1)}, u32[]{:S(2)}, u32[]{:S(2)}) collective-permute-start(bf16[4,16,1920]{2,1,0:T(8,128)(2,1)S(1)} %get-tuple-element.34), channel_id=1, source_target_pairs={{0,1},{1,0},{2,3},{3,2},{4,5},{5,4},{6,7},{7,6},{8,9},{9,8},{10,11... | collective-permute-start | bytes 737288 | tf_op jit(solution)/shard_map/ppermute | solution.py:292
  20.9 9.4 %collective-permute-start.9 = (bf16[128,896]{1,0:T(8,128)(2,1)S(1)}, bf16[128,896]{1,0:T(8,128)(2,1)S(1)}, u32[]{:S(2)}, u32[]{:S(2)}) collective-permute-start(bf16[128,896]{1,0:T(8,128)(2,1)S(1)} %get-tuple-element.43), channel_id=1, source_target_pairs={{0,24},{8,16},{16,8},{24,0},{1,25},{9,17},{17,9},{25,1},{2,26},{10... | collective-permute-start | bytes 688136 | tf_op jit(solution)/shard_map/ppermute | solution.py:310
  23.9 11.2 %collective-permute-start.10 = (bf16[128,896]{1,0:T(8,128)(2,1)S(1)}, bf16[128,896]{1,0:T(8,128)(2,1)S(1)}, u32[]{:S(2)}, u32[]{:S(2)}) collective-permute-start(bf16[128,896]{1,0:T(8,128)(2,1)S(1)} %get-tuple-element.44), channel_id=1, source_target_pairs={{0,8},{8,0},{16,24},{24,16},{1,9},{9,1},{17,25},{25,17},{2,10},{10... | collective-permute-start | bytes 688136 | tf_op jit(solution)/shard_map/ppermute | solution.py:310
  24.4 10.7 %collective-permute-start.11 = (bf16[128,896]{1,0:T(8,128)(2,1)S(1)}, bf16[128,896]{1,0:T(8,128)(2,1)S(1)}, u32[]{:S(2)}, u32[]{:S(2)}) collective-permute-start(bf16[128,896]{1,0:T(8,128)(2,1)S(1)} %get-tuple-element.45), channel_id=1, source_target_pairs={{0,16},{8,24},{16,0},{24,8},{1,17},{9,25},{17,1},{25,9},{2,18},{10... | collective-permute-start | bytes 688136 | tf_op jit(solution)/shard_map/ppermute | solution.py:310
  24.5 10.6 %collective-permute-start.6 = (bf16[16,1920]{1,0:T(8,128)(2,1)S(1)}, bf16[16,1920]{1,0:T(8,128)(2,1)S(1)}, u32[]{:S(2)}, u32[]{:S(2)}) collective-permute-start(bf16[16,1920]{1,0:T(8,128)(2,1)S(1)} %get-tuple-element.36), channel_id=1, source_target_pairs={{0,6},{1,7},{2,4},{3,5},{4,2},{5,3},{6,0},{7,1},{8,14},{9,15},{10,... | collective-permute-start | bytes 184328 | tf_op jit(solution)/shard_map/ppermute | solution.py:292
  27.5 7.6 %collective-permute-start.7 = (bf16[16,1920]{1,0:T(8,128)(2,1)S(1)}, bf16[16,1920]{1,0:T(8,128)(2,1)S(1)}, u32[]{:S(2)}, u32[]{:S(2)}) collective-permute-start(bf16[16,1920]{1,0:T(8,128)(2,1)S(1)} %get-tuple-element.37), channel_id=1, source_target_pairs={{0,4},{1,5},{2,6},{3,7},{4,0},{5,1},{6,2},{7,3},{8,12},{9,13},{10,... | collective-permute-start | bytes 184328 | tf_op jit(solution)/shard_map/ppermute | solution.py:292
  30.3 4.8 %collective-permute-start.8 = (bf16[16,1920]{1,0:T(8,128)(2,1)S(1)}, bf16[16,1920]{1,0:T(8,128)(2,1)S(1)}, u32[]{:S(2)}, u32[]{:S(2)}) collective-permute-start(bf16[16,1920]{1,0:T(8,128)(2,1)S(1)} %get-tuple-element.38), channel_id=1, source_target_pairs={{0,2},{1,3},{2,0},{3,1},{4,6},{5,7},{6,4},{7,5},{8,10},{9,11},{10,... | collective-permute-start | bytes 184328 | tf_op jit(solution)/shard_map/ppermute | solution.py:292
  35.1 1.7 %collective-permute-start.12 = (bf16[3,64,896]{2,1,0:T(8,128)(2,1)S(1)}, bf16[3,64,896]{2,1,0:T(8,128)(2,1)S(1)}, u32[]{:S(2)}, u32[]{:S(2)}) collective-permute-start(bf16[3,64,896]{2,1,0:T(8,128)(2,1)S(1)} %shard_map.143), channel_id=1, source_target_pairs={{0,1},{1,0},{2,3},{3,2},{4,5},{5,4},{6,7},{7,6},{8,9},{9,8},{10,11... | collective-permute-start | bytes 1032200 | tf_op jit(solution)/shard_map/ppermute | solution.py:292
